TPU v7x, 128 devices: a whole 4x4x4 slice. The times are simulated.
128 devices in a mesh: tm: 16 (over y_hi, x, core), height: 8 (over y_lo, z).
Axes of the slice: x: 4, y: 4 (y_hi: 2, y_lo: 2; y = y_hi * 2 + y_lo), z: 4, core: 2. Of those that a mesh axis runs over, the one named last changes fastest.
Arguments:
- hidden: bfloat16 [32, 16, 128, 1536], P('tm', 'height'), may hold values from -6 to 6
- control: bfloat16 [32, 16, 8192], P('tm', 'height'), may hold values from -6 to 6
- conv_weight: bfloat16 [1728, 256], replicated, may hold values from -0.15625 to 0.15625
- ctrl_proj: bfloat16 [256, 1536], replicated, may hold values from -0.375 to 0.375
- mod_gain: float32 [1536], replicated, may hold values from 0.1 to 1.9
- mod_shift: float32 [1536], replicated, may hold values from -3 to 3
- w_qkv: bfloat16 [1536, 4608], replicated, may hold values from -0.15625 to 0.15625
- kv_stale: bfloat16 [32, 16, 128, 3072], P('tm', 'height'), may hold values from -64 to 64
- key_tiles: int32 [16, 8, 4, 8], P('tm', 'height'), may hold values from 0 to 511, as said below
- key_count: int32 [16, 8, 4], P('tm', 'height'), may hold values from 1 to 8, as said below
Outputs:
- attended: bfloat16 [32, 16, 128, 1536], P('tm', 'height')
- fresh_kv: bfloat16 [32, 16, 128, 3072], P('tm', 'height')
Inputs may be any that keep to these rules, and one draw needn't show every extreme that they name: `key_tiles`: with tile t = (a 8 + b) * 4 + c, the entries of list (a, b, c) are distinct tiles other than t itself, each with the same a and b differing by at most 1, or the same b and a differing by 1, 2 or 4. Only the first key_count entries are read. `key_count`: some list uses all 8 entries and some list only one.
All inputs are finite; a program needn't handle non-finite values.
Results may differ from a plain program's by a relative error of at most 0.012.
Values may be sent and summed in bfloat16 or wider, within the bound.
No kernel may reach another device: no remote copies, remote signals or barrier semaphores. Data moves between devices by JAX's collectives and lax.ppermute only.
A program may use at most 448 MiB of HBM per device.

v0:
```python
import functools

import jax
import jax.numpy as jnp
from jax import lax
from jax.experimental import pallas as pl
from jax.experimental.pallas import tpu as pltpu
from jax.sharding import PartitionSpec as P

HEADS = 12
HD = 128
LOG2E = 1.4426950408889634
AHEAD = 2
RING = 8
GROUPS = ((0, 3), (1, 2, 4, 5, 6, 7), (8,), (9, 10, 11, 12), (13,))
COSTS = (30, 50, 20, 8, 8)


def around(device, step):
    return device // RING * RING + (device + step) % RING


def swap(parity):
    return [(i, i ^ 1) for i in range(2 * RING) if i % 2 == parity]


def fetch_blocks(kv):
    everyone = range(2 * RING)
    half = kv.shape[-1] // 2
    up = [(i, around(i, 2)) for i in everyone]
    down = [(i, around(i, -2)) for i in everyone]
    over = [(0, 8), (1, 9), (2, 10), (3, 11), (12, 4), (13, 5), (14, 6), (15, 7)]
    below = lax.ppermute(kv, "tm", up)
    above = lax.ppermute(kv, "tm", down)
    rows_before = from_behind(kv, "height", 1)
    rows_after = from_behind(kv, "height", -1)
    mate = lax.ppermute(kv, "tm", swap(0) + swap(1))
    odd_below = lax.ppermute(below, "tm", swap(1))
    even_above = lax.ppermute(above, "tm", swap(0))
    far_keys = lax.ppermute(below[..., :half], "tm", up)
    far_values = lax.ppermute(above[..., half:], "tm", down)
    across_below = lax.ppermute(below, "tm", [(0, 8), (1, 9)])
    across_above = lax.ppermute(above, "tm", [(14, 6), (15, 7)])
    mate_below = lax.ppermute(across_below, "tm", [(9, 8)])
    mate_above = lax.ppermute(across_above, "tm", [(6, 7)])
    across_keys = lax.ppermute(far_keys, "tm", over)
    across_values = lax.ppermute(far_values, "tm", over)
    singles = (kv, rows_before, rows_after, mate, below, above, odd_below, even_above)
    crossed = (across_below, across_above, mate_below, mate_above)
    halves = [(block,) for block in singles] + [(far_keys, far_values)]
    return halves + [(block,) for block in crossed] + [(across_keys, across_values)]


def locate(dframe, drow, frame_idx):
    odd = frame_idx % 2
    spot = frame_idx % RING // 2
    low, high, left = spot == 0, spot == RING // 2 - 1, spot < 2
    table = {
        -1: jnp.where(odd == 1, 3, jnp.where(low, 11, 6)),
        1: jnp.where(odd == 0, 3, jnp.where(high, 12, 7)),
        -2: jnp.where(low, 9, 4),
        2: jnp.where(high, 10, 5),
        -4: jnp.where(left, 13, 8),
        4: jnp.where(left, 8, 13),
    }
    source = jnp.where(drow == -1, 1, jnp.where(drow == 1, 2, 0))
    for step, place in table.items():
        source = jnp.where(dframe == step, place, source)
    return source


def with_halo(cells, sides, width):
    for axis, dim in sides:
        count = lax.axis_size(axis)
        ends = count - 1
        head = lax.slice_in_dim(cells, 0, width, axis=dim)
        tail = lax.slice_in_dim(cells, cells.shape[dim] - width, cells.shape[dim], axis=dim)
        cells = jnp.concatenate(
            [
                lax.ppermute(tail, axis, [(i, (i + 1) % count) for i in range(ends)]),
                cells,
                lax.ppermute(head, axis, [((i + 1) % count, i) for i in range(ends)]),
            ],
            axis=dim,
        )
    return cells


def from_behind(block, axis, distance):
    devices = range(lax.axis_size(axis))
    route = [(i - distance, i) for i in devices if i - distance in devices]
    return lax.ppermute(block, axis, route)


def attend_kernel(ids, first, last, *refs):
    code_ref, q_ref = refs[0], refs[1]
    count = sum(n for _, n in ids)
    rest = refs[2 + count :]
    stale = []
    at = 2
    for which, n in ids:
        stale.append((which, refs[at], refs[at + n - 1], n == 1))
        at += n
    if not first:
        acc_in, top_in, sum_in = rest[:3]
        rest = rest[3:]
    if last:
        out_ref, acc, top, total = rest
    else:
        acc, top, total = rest
    planes, cols = q_ref.shape[0], q_ref.shape[1]
    tokens = planes * cols
    width = HEADS * HD
    tile = pl.program_id(0)
    scale = HD**-0.5 * LOG2E

    def add_tile(key_of, value_of, fresh):
        def scores(head):
            query = q_ref[:, :, head * HD : (head + 1) * HD].reshape(tokens, HD)
            return lax.dot_general(
                key_of(head), query, (((1,), (1,)), ((), ())), preferred_element_type=jnp.float32
            )

        ready = [scores(head) for head in range(AHEAD)]
        for head in range(HEADS):
            if head + AHEAD < HEADS:
                ready.append(scores(head + AHEAD))
            s = ready[head]
            new = jnp.max(s, axis=0, keepdims=True)
            if not fresh:
                old = top[0, head : head + 1]
                new = jnp.maximum(old, new)
                alpha = jnp.exp2((old - new) * scale)
            p = jnp.exp2((s - new) * scale)
            gain = jnp.sum(p, axis=0, keepdims=True)
            got = lax.dot_general(
                value_of(head),
                p.astype(jnp.bfloat16),
                (((0,), (0,)), ((), ())),
                preferred_element_type=jnp.float32,
            )
            if not fresh:
                gain = total[0, head : head + 1] * alpha + gain
                got = acc[0, head] * alpha + got
            top[0, head : head + 1] = new
            total[0, head : head + 1] = gain
            acc[0, head] = got

    if first:

        def fresh_part(low):
            return q_ref[:, :, low : low + HD].reshape(tokens, HD)

        add_tile(
            lambda head: fresh_part(width + head * HD),
            lambda head: fresh_part(2 * width + head * HD),
            True,
        )
    else:
        acc[...] = acc_in[...]
        top[...] = top_in[...]
        total[...] = sum_in[...]

    def slot(place, carry):
        code = code_ref[tile * 8 + place]
        for which, key_ref, value_ref, joined in stale:

            @pl.when(code >> 2 == which)
            def _():
                here = pl.ds(pl.multiple_of((code & 3) * cols, cols), cols)
                shift = width if joined else 0

                def key_of(head):
                    low = head * HD
                    return key_ref[:, here, low : low + HD].reshape(tokens, HD)

                def value_of(head):
                    low = shift + head * HD
                    return value_ref[:, here, low : low + HD].reshape(tokens, HD)

                add_tile(key_of, value_of, False)

        return carry

    lax.fori_loop(0, 8, slot, 0)
    if last:
        for head in range(HEADS):
            res = acc[0, head] / total[0, head : head + 1]
            res = jnp.transpose(res).astype(jnp.bfloat16)
            out_ref[:, :, head * HD : (head + 1) * HD] = res.reshape(planes, cols, HD)


def attend(code, qkv, sources, state, last, cost):
    ids = tuple((which, len(blocks)) for which, blocks in sources)
    blocks = [block for _, parts in sources for block in parts]
    planes, width, full = qkv.shape
    tiles = code.shape[0] // 8
    cols = width // tiles
    tokens = planes * cols
    first = state is None
    keep = pl.BlockSpec((1, HEADS, HD, tokens), lambda t: (t, 0, 0, 0))
    keep_row = pl.BlockSpec((1, HEADS, tokens), lambda t: (t, 0, 0))

    def whole(block):
        once = pl.Buffered(1)
        return pl.BlockSpec(block.shape, lambda t: (0, 0, 0), pipeline_mode=once)

    part = (planes, cols, HEADS * HD)
    qpart = (planes, cols, full) if first else part
    in_specs = [pl.BlockSpec(memory_space=pltpu.SMEM), pl.BlockSpec(qpart, lambda t: (0, t, 0))]
    in_specs += [whole(block) for block in blocks]
    operands = [code, qkv] + blocks
    if not first:
        in_specs += [keep, keep_row, keep_row]
        operands += list(state)
    kept = jax.ShapeDtypeStruct((tiles, HEADS, HD, tokens), jnp.float32)
    kept_row = jax.ShapeDtypeStruct((tiles, HEADS, tokens), jnp.float32)
    if last:
        out_shape = jax.ShapeDtypeStruct((planes, width, HEADS * HD), jnp.bfloat16)
        out_specs = pl.BlockSpec(part, lambda t: (0, t, 0))
        scratch = [pltpu.VMEM((1, HEADS, HD, tokens), jnp.float32)]
        scratch += [pltpu.VMEM((1, HEADS, tokens), jnp.float32)] * 2
    else:
        out_shape = [kept, kept_row, kept_row]
        out_specs = [keep, keep_row, keep_row]
        scratch = []
    return pl.pallas_call(
        functools.partial(attend_kernel, ids, first, last),
        grid=(tiles,),
        in_specs=in_specs,
        out_specs=out_specs,
        out_shape=out_shape,
        scratch_shapes=scratch,
        compiler_params=pltpu.CompilerParams(vmem_limit_bytes=56 << 20),
        cost_estimate=pl.CostEstimate(
            flops=cost * 1_000_000_000, bytes_accessed=cost * 3_000_000, transcendentals=0
        ),
    )(*operands)


def body(
    hidden,
    control,
    conv_weight,
    ctrl_proj,
    mod_gain,
    mod_shift,
    w_qkv,
    kv_stale,
    key_tiles,
    key_count,
):
    frames, rows, width, dmodel = hidden.shape
    tiles_dev = key_count.shape[2]
    cin = conv_weight.shape[0] // 27
    attn_width = HEADS * HD
    planes = frames * rows
    rim = with_halo(control, (("tm", 0), ("height", 1)), 1)
    rim, kv_stale = lax.optimization_barrier((rim, kv_stale))
    grid = rim.reshape(frames + 2, rows + 2, width, cin)
    grid = jnp.pad(grid, ((0, 0), (0, 0), (1, 1), (0, 0)))
    taps = [
        grid[i : i + frames, j : j + rows, k : k + width]
        for i in range(3)
        for j in range(3)
        for k in range(3)
    ]
    stacked = jnp.concatenate(taps, axis=-1).reshape(frames * rows * width, 27 * cin)
    conv = jnp.dot(stacked, conv_weight, preferred_element_type=jnp.float32)
    act = jax.nn.silu(conv).astype(jnp.bfloat16)
    mixed = hidden.reshape(frames * rows * width, dmodel).astype(jnp.float32) + jnp.dot(
        act, ctrl_proj, preferred_element_type=jnp.float32
    )
    center = mixed - jnp.mean(mixed, axis=-1, keepdims=True)
    spread = jnp.mean(center * center, axis=-1, keepdims=True)
    normed = (center * lax.rsqrt(spread + 1e-06) * mod_gain + mod_shift).astype(jnp.bfloat16)
    qkv = jnp.dot(normed, w_qkv, preferred_element_type=jnp.float32).astype(jnp.bfloat16)
    qkv_grid = qkv.reshape(frames, rows, width, 3 * attn_width)
    fresh_kv = qkv_grid[..., attn_width:]
    frame_idx = lax.axis_index("tm")
    row_idx = lax.axis_index("height")
    row_total = lax.axis_size("height")
    idents = key_tiles[0, 0]
    counts = key_count[0, 0]
    dframe = idents // (row_total * tiles_dev) - frame_idx
    drow = idents // tiles_dev % row_total - row_idx
    source = locate(dframe, drow, frame_idx)
    used = lax.broadcasted_iota(jnp.int32, idents.shape, 1) < counts[:, None]
    code = jnp.where(used, source * 4 + idents % tiles_dev, -1).reshape(-1)
    qkv = qkv.reshape(planes, width, 3 * attn_width)
    blocks = [
        tuple(part.reshape(planes, width, part.shape[-1]) for part in parts)
        for parts in fetch_blocks(kv_stale)
    ]
    state = None
    for group, cost in zip(GROUPS, COSTS):
        state = attend(code, qkv, [(w, blocks[w]) for w in group], state, group is GROUPS[-1], cost)
    return (state.reshape(frames, rows, width, attn_width), fresh_kv)


def solution(mesh):
    placed = (
        P("tm", "height", None, None),
        P("tm", "height", None),
        P(),
        P(),
        P(),
        P(),
        P(),
        P("tm", "height", None, None),
        P("tm", "height", None, None),
        P("tm", "height", None),
    )
    return jax.shard_map(
        body,
        mesh=mesh,
        in_specs=placed,
        out_specs=(P("tm", "height", None, None), P("tm", "height", None, None)),
        check_vma=False,
    )
```

profile of v0, /device:TPU:6, one launch (start us, length us, event | category | flops | bytes accessed | tf_op | source)
XLA Modules:
  0.0 254.6 jit_solution(11563692663930198346)
XLA Ops:
  3.5 3.6 %collective-permute-start.1 = (bf16[1,2,8192]{2,1,0:T(2,128)(2,1)S(1)}, bf16[1,2,8192]{2,1,0:T(2,128)(2,1)S(1)}, u32[]{:S(2)}, u32[]{:S(2)}) collective-permute-start(bf16[1,2,8192]{2,1,0:T(2,128)(2,1)S(1)} %get-tuple-element.59), channel_id=1, source_target_pairs={{8,0},{16,8},{24,16},{32,24},{40,32},{48,40},{56,48},{64,56},{72,6... | collective-permute-start | bytes 98312 | tf_op jit(solution)/shard_map/ppermute | solution.py:82
  9.5 3.8 %collective-permute-start.2 = (bf16[4,1,8192]{2,1,0:T(2,128)(2,1)S(1)}, bf16[4,1,8192]{2,1,0:T(2,128)(2,1)S(1)}, u32[]{:S(2)}, u32[]{:S(2)}) collective-permute-start(bf16[4,1,8192]{2,1,0:T(2,128)(2,1)S(1)} %get-tuple-element.57), channel_id=1, source_target_pairs={{0,1},{1,2},{2,3},{3,4},{4,5},{5,6},{6,7},{8,9},{9,10},{10,11},{11... | collective-permute-start | bytes 196616 | tf_op jit(solution)/shard_map/ppermute | solution.py:80
  15.9 4.4 %collective-permute-done.3 = bf16[4,1,8192]{2,1,0:T(2,128)(2,1)S(1)} collective-permute-done((bf16[4,1,8192]{2,1,0:T(2,128)(2,1)S(1)}, bf16[4,1,8192]{2,1,0:T(2,128)(2,1)S(1)}, u32[]{:S(2)}, u32[]{:S(2)}) %collective-permute-start.3) | collective-permute-done | bytes 65568 | tf_op jit(solution)/shard_map/ppermute | solution.py:82
  20.8 5.5 %collective-permute-start.18 = (bf16[2,2,128,3072]{3,2,1,0:T(8,128)(2,1)}, bf16[2,2,128,3072]{3,2,1,0:T(8,128)(2,1)}, u32[]{:S(2)}, u32[]{:S(2)}) collective-permute-start(bf16[2,2,128,3072]{3,2,1,0:T(8,128)(2,1)} %param.17), channel_id=1, source_target_pairs={{0,8},{16,24},{32,40},{48,56},{64,72},{80,88},{96,104},{112,120},{... | collective-permute-start | bytes 9437192 | tf_op jit(solution)/shard_map/ppermute | solution.py:37
  27.9 5.4 %collective-permute-start.14 = (bf16[2,2,128,3072]{3,2,1,0:T(8,128)(2,1)}, bf16[2,2,128,3072]{3,2,1,0:T(8,128)(2,1)}, u32[]{:S(2)}, u32[]{:S(2)}) collective-permute-start(bf16[2,2,128,3072]{3,2,1,0:T(8,128)(2,1)} %param.17), channel_id=1, source_target_pairs={{0,1},{1,2},{2,3},{3,4},{4,5},{5,6},{6,7},{8,9},{9,10},{10,11},{11... | collective-permute-start | bytes 9437192 | tf_op jit(solution)/shard_map/ppermute | solution.py:92
  40.2 4.5 %concatenate.11 = bf16[2,2,128,1728]{3,2,1,0:T(8,128)(2,1)S(1)} concatenate(bf16[2,2,128,64]{3,2,1,0:T(8,128)(2,1)} %get-tuple-element.56, bf16[2,2,128,64]{3,2,1,0:T(8,128)(2,1)} %get-tuple-element.55, bf16[2,2,128,64]{3,2,1,0:T(8,128)(2,1)} %get-tuple-element.31, bf16[2,2,128,64]{3,2,1,0:T(8,128)(2,1)} %get-tuple-element.32, bf16[2,2,128,64]{3,2,1,0:T(8,128)(2,1)} %get-tuple-element.54, ...), dimensions={3} | concatenate | bytes 3538944 | tf_op jit(solution)/shard_map/concatenate | solution.py:268
  44.8 5.2 %fusion.14 = (f32[512]{0:T(512)S(1)}, f32[512,1536]{1,0:T(8,128)}) fusion(bf16[256,1536]{1,0:T(8,128)(2,1)} %param.13, bf16[512,1536]{1,0:T(8,128)(2,1)} %bitcast.36, bf16[512,1728]{1,0:T(8,128)(2,1)S(1)} %bitcast.33, bf16[1728,256]{1,0:T(8,128)(2,1)S(1)} %copy-done), kind=kOutput, calls=%fused_computation.63 | convolution fusion | flops 858652160 | bytes 8161280 | tf_op jit(solution)/shard_map/dot_general | solution.py:271
  52.5 35.0 %collective-permute-done.4 = bf16[2,2,128,3072]{3,2,1,0:T(8,128)(2,1)} collective-permute-done((bf16[2,2,128,3072]{3,2,1,0:T(8,128)(2,1)}, bf16[2,2,128,3072]{3,2,1,0:T(8,128)(2,1)}, u32[]{:S(2)}, u32[]{:S(2)}) %collective-permute-start.4) | collective-permute-done | bytes 3145760 | tf_op jit(solution)/shard_map/ppermute | solution.py:33
  89.0 3.7 %collective-permute-start.5 = (bf16[2,2,128,1536]{3,2,1,0:T(8,128)(2,1)S(1)}, bf16[2,2,128,1536]{3,2,1,0:T(8,128)(2,1)S(1)}, u32[]{:S(2)}, u32[]{:S(2)}) collective-permute-start(bf16[2,2,128,1536]{3,2,1,0:T(8,128)(2,1)S(1)} %slice.156), channel_id=1, source_target_pairs={{0,16},{8,24},{16,32},{24,40},{32,48},{40,56},{48,0},{56,8},{64,80... | collective-permute-start | bytes 4718600 | tf_op jit(solution)/shard_map/ppermute | solution.py:40
  94.1 3.8 %collective-permute-done.7 = bf16[2,2,128,3072]{3,2,1,0:T(8,128)(2,1)} collective-permute-done((bf16[2,2,128,3072]{3,2,1,0:T(8,128)(2,1)}, bf16[2,2,128,3072]{3,2,1,0:T(8,128)(2,1)}, u32[]{:S(2)}, u32[]{:S(2)}) %collective-permute-start.7) | collective-permute-done | bytes 3145760 | tf_op jit(solution)/shard_map/ppermute | solution.py:34
  99.1 2.9 %collective-permute-start.17 = (bf16[2,2,128,3072]{3,2,1,0:T(8,128)(2,1)}, bf16[2,2,128,3072]{3,2,1,0:T(8,128)(2,1)}, u32[]{:S(2)}, u32[]{:S(2)}) collective-permute-start(bf16[2,2,128,3072]{3,2,1,0:T(8,128)(2,1)} %collective-permute-done.7), channel_id=1, source_target_pairs={{0,8},{16,24},{32,40},{48,56},{64,72},{80,88},{96,104},{112,120},{... | collective-permute-start | bytes 9437192 | tf_op jit(solution)/shard_map/ppermute | solution.py:39
  102.0 2.9 %collective-permute-done.15 = bf16[2,2,128,3072]{3,2,1,0:T(8,128)(2,1)} collective-permute-done((bf16[2,2,128,3072]{3,2,1,0:T(8,128)(2,1)}, bf16[2,2,128,3072]{3,2,1,0:T(8,128)(2,1)}, u32[]{:S(2)}, u32[]{:S(2)}) %collective-permute-start.15) | collective-permute-done | bytes 3145760 | tf_op jit(solution)/shard_map/ppermute | solution.py:92
  106.2 11.1 %convolution_convert_fusion = bf16[512,4608]{1,0:T(8,128)(2,1)S(1)} fusion(bf16[1536,4608]{1,0:T(8,128)(2,1)} %param.16, f32[512,1536]{1,0:T(8,128)S(1)} %copy-done.2, f32[1536]{0:T(1024)S(1)} %copy-done.7, f32[1536]{0:T(1024)S(1)} %copy-done.8, f32[512]{0:T(512)S(1)} %add_rsqrt_fusion, f32[512]{0:T(512)S(1)} %broadcast_multiply_fusion), kind=kOutput, calls=%fused_computation | convolution fusion | flops 7254048768 | bytes 22036480 | tf_op jit(solution)/shard_map/dot_general | solution.py:277
  122.0 6.8 %collective-permute-done.5 = bf16[2,2,128,1536]{3,2,1,0:T(8,128)(2,1)S(1)} collective-permute-done((bf16[2,2,128,1536]{3,2,1,0:T(8,128)(2,1)S(1)}, bf16[2,2,128,1536]{3,2,1,0:T(8,128)(2,1)S(1)}, u32[]{:S(2)}, u32[]{:S(2)}) %collective-permute-start.5) | collective-permute-done | bytes 1572896 | tf_op jit(solution)/shard_map/ppermute | solution.py:40
  129.7 15.5 %shard_map.113 = (f32[4,12,128,128]{3,2,1,0:T(8,128)}, f32[4,12,128]{2,1,0:T(8,128)}, f32[4,12,128]{2,1,0:T(8,128)}) custom-call(s32[32]{0:T(128)} %fusion.6.refs_0_, bf16[4,128,4608]{2,1,0:T(8,128)(2,1)} %bitcast.28, bf16[4,128,3072]{2,1,0:T(8,128)(2,1)} %bitcast.34, bf16[4,128,3072]{2,1,0:T(8,128)(2,1)} %bitcast.19.refs_3_), custom_call_target="tpu_custom_call" | custom-call | flops 30000001024 | bytes 90000000 | tf_op jit(solution)/shard_map/pallas_call | solution.py:227
  145.3 22.0 %collective-permute-done.8 = bf16[2,2,128,1536]{3,2,1,0:T(8,128)(2,1)} collective-permute-done((bf16[2,2,128,1536]{3,2,1,0:T(8,128)(2,1)S(1)}, bf16[2,2,128,1536]{3,2,1,0:T(8,128)(2,1)}, u32[]{:S(2)}, u32[]{:S(2)}) %collective-permute-start.8) | collective-permute-done | bytes 1572896 | tf_op jit(solution)/shard_map/ppermute | solution.py:41
  169.9 2.6 %collective-permute-start.12 = (bf16[2,2,128,3072]{3,2,1,0:T(8,128)(2,1)S(1)}, bf16[2,2,128,3072]{3,2,1,0:T(8,128)(2,1)}, u32[]{:S(2)}, u32[]{:S(2)}) collective-permute-start(bf16[2,2,128,3072]{3,2,1,0:T(8,128)(2,1)S(1)} %collective-permute-done.10), channel_id=1, source_target_pairs={{72,64},{73,65},{74,66},{75,67},{76,68},{77,69},{78,70},{79,71}} | collective-permute-start | bytes 9437192 | tf_op jit(solution)/shard_map/ppermute | solution.py:44
  172.5 7.1 %collective-permute-done.11 = bf16[2,2,128,3072]{3,2,1,0:T(8,128)(2,1)} collective-permute-done((bf16[2,2,128,3072]{3,2,1,0:T(8,128)(2,1)}, bf16[2,2,128,3072]{3,2,1,0:T(8,128)(2,1)}, u32[]{:S(2)}, u32[]{:S(2)}) %collective-permute-start.11) | collective-permute-done | bytes 3145760 | tf_op jit(solution)/shard_map/ppermute | solution.py:43
  179.7 3.0 %collective-permute-start.13 = (bf16[2,2,128,3072]{3,2,1,0:T(8,128)(2,1)}, bf16[2,2,128,3072]{3,2,1,0:T(8,128)(2,1)}, u32[]{:S(2)}, u32[]{:S(2)}) collective-permute-start(bf16[2,2,128,3072]{3,2,1,0:T(8,128)(2,1)} %collective-permute-done.11), channel_id=1, source_target_pairs={{48,56},{49,57},{50,58},{51,59},{52,60},{53,61},{54,62},{55,63}} | collective-permute-start | bytes 9437192 | tf_op jit(solution)/shard_map/ppermute | solution.py:45
  182.7 17.1 %shard_map.114 = (f32[4,12,128,128]{3,2,1,0:T(8,128)}, f32[4,12,128]{2,1,0:T(8,128)}, f32[4,12,128]{2,1,0:T(8,128)}) custom-call(s32[32]{0:T(128)} %fusion.6.refs_0_, bf16[4,128,4608]{2,1,0:T(8,128)(2,1)} %bitcast.29, bf16[4,128,3072]{2,1,0:T(8,128)(2,1)} %bitcast.12.refs_2_, bf16[4,128,3072]{2,1,0:T(8,128)(2,1)} %bitcast.13.refs_3_, ...), custom_call_target="tpu_custom_call" | custom-call | flops 49999998976 | bytes 150000000 | tf_op jit(solution)/shard_map/pallas_call | solution.py:227
  199.8 12.9 %shard_map.115 = (f32[4,12,128,128]{3,2,1,0:T(8,128)}, f32[4,12,128]{2,1,0:T(8,128)}, f32[4,12,128]{2,1,0:T(8,128)}) custom-call(s32[32]{0:T(128)} %fusion.6.refs_0_, bf16[4,128,4608]{2,1,0:T(8,128)(2,1)} %bitcast.30, bf16[4,128,1536]{2,1,0:T(8,128)(2,1)} %bitcast.37, bf16[4,128,1536]{2,1,0:T(8,128)(2,1)} %bitcast.11.refs_3_, ...), custom_call_target="tpu_custom_call" | custom-call | flops 20000000000 | bytes 60000000 | tf_op jit(solution)/shard_map/pallas_call | solution.py:227
  212.7 12.0 %shard_map.116 = (f32[4,12,128,128]{3,2,1,0:T(8,128)}, f32[4,12,128]{2,1,0:T(8,128)}, f32[4,12,128]{2,1,0:T(8,128)}) custom-call(s32[32]{0:T(128)} %fusion.6.refs_0_, bf16[4,128,4608]{2,1,0:T(8,128)(2,1)} %bitcast.31, bf16[4,128,3072]{2,1,0:T(8,128)(2,1)} %bitcast.35, bf16[4,128,3072]{2,1,0:T(8,128)(2,1)} %bitcast.7.refs_3_, ...), custom_call_target="tpu_custom_call" | custom-call | flops 8000000000 | bytes 24000000 | tf_op jit(solution)/shard_map/pallas_call | solution.py:227
  224.8 19.8 %collective-permute-done.9 = bf16[2,2,128,1536]{3,2,1,0:T(8,128)(2,1)} collective-permute-done((bf16[2,2,128,1536]{3,2,1,0:T(8,128)(2,1)}, bf16[2,2,128,1536]{3,2,1,0:T(8,128)(2,1)}, u32[]{:S(2)}, u32[]{:S(2)}) %collective-permute-start.9) | collective-permute-done | bytes 1572896 | tf_op jit(solution)/shard_map/ppermute | solution.py:47
  244.6 10.1 %shard_map.117 = bf16[4,128,1536]{2,1,0:T(8,128)(2,1)} custom-call(s32[32]{0:T(128)} %fusion.6.refs_0_, bf16[4,128,4608]{2,1,0:T(8,128)(2,1)} %bitcast.32, bf16[4,128,1536]{2,1,0:T(8,128)(2,1)} %bitcast.38, bf16[4,128,1536]{2,1,0:T(8,128)(2,1)} %bitcast.5.refs_3_, f32[4,12,128,128]{3,2,1,0:T(8,128)} %get-tuple-element.27.refs_4_, ...), custom_call_target="tpu_custom_call" | custom-call | flops 8000000000 | bytes 24000000 | tf_op jit(solution)/shard_map/pallas_call | solution.py:227
  (60 shorter events, 32.7 us)
Async XLA Ops:
  0.6 44.1 %copy-start = (bf16[1728,256]{1,0:T(8,128)(2,1)S(1)}, bf16[1728,256]{1,0:T(8,128)(2,1)}, u32[]{:S(2)}) copy-start(bf16[1728,256]{1,0:T(8,128)(2,1)} %param.12) | copy-start | bytes 2654212
  1.6 5.6 %collective-permute-start = (bf16[1,2,8192]{2,1,0:T(2,128)(2,1)S(1)}, bf16[1,2,8192]{2,1,0:T(2,128)(2,1)S(1)}, u32[]{:S(2)}, u32[]{:S(2)}) collective-permute-start(bf16[1,2,8192]{2,1,0:T(2,128)(2,1)S(1)} %get-tuple-element.60), channel_id=1, source_target_pairs={{0,8},{8,16},{16,24},{24,32},{32,40},{40,48},{48,56},{56,64},{64,7... | collective-permute-start | bytes 98312 | tf_op jit(solution)/shard_map/ppermute | solution.py:80
  3.5 5.8 %collective-permute-start.1 = (bf16[1,2,8192]{2,1,0:T(2,128)(2,1)S(1)}, bf16[1,2,8192]{2,1,0:T(2,128)(2,1)S(1)}, u32[]{:S(2)}, u32[]{:S(2)}) collective-permute-start(bf16[1,2,8192]{2,1,0:T(2,128)(2,1)S(1)} %get-tuple-element.59), channel_id=1, source_target_pairs={{8,0},{16,8},{24,16},{32,24},{40,32},{48,40},{56,48},{64,56},{72,6... | collective-permute-start | bytes 98312 | tf_op jit(solution)/shard_map/ppermute | solution.py:82
  9.5 6.3 %collective-permute-start.2 = (bf16[4,1,8192]{2,1,0:T(2,128)(2,1)S(1)}, bf16[4,1,8192]{2,1,0:T(2,128)(2,1)S(1)}, u32[]{:S(2)}, u32[]{:S(2)}) collective-permute-start(bf16[4,1,8192]{2,1,0:T(2,128)(2,1)S(1)} %get-tuple-element.57), channel_id=1, source_target_pairs={{0,1},{1,2},{2,3},{3,4},{4,5},{5,6},{6,7},{8,9},{9,10},{10,11},{11... | collective-permute-start | bytes 196616 | tf_op jit(solution)/shard_map/ppermute | solution.py:80
  13.4 6.9 %collective-permute-start.3 = (bf16[4,1,8192]{2,1,0:T(2,128)(2,1)S(1)}, bf16[4,1,8192]{2,1,0:T(2,128)(2,1)S(1)}, u32[]{:S(2)}, u32[]{:S(2)}) collective-permute-start(bf16[4,1,8192]{2,1,0:T(2,128)(2,1)S(1)} %get-tuple-element.58), channel_id=1, source_target_pairs={{1,0},{2,1},{3,2},{4,3},{5,4},{6,5},{7,6},{9,8},{10,9},{11,10},{12... | collective-permute-start | bytes 196616 | tf_op jit(solution)/shard_map/ppermute | solution.py:82
  20.7 66.9 %collective-permute-start.4 = (bf16[2,2,128,3072]{3,2,1,0:T(8,128)(2,1)}, bf16[2,2,128,3072]{3,2,1,0:T(8,128)(2,1)}, u32[]{:S(2)}, u32[]{:S(2)}) collective-permute-start(bf16[2,2,128,3072]{3,2,1,0:T(8,128)(2,1)} %param.17), channel_id=1, source_target_pairs={{0,16},{8,24},{16,32},{24,40},{32,48},{40,56},{48,0},{56,8},{64,80... | collective-permute-start | bytes 9437192 | tf_op jit(solution)/shard_map/ppermute | solution.py:33
  20.8 72.0 %collective-permute-start.18 = (bf16[2,2,128,3072]{3,2,1,0:T(8,128)(2,1)}, bf16[2,2,128,3072]{3,2,1,0:T(8,128)(2,1)}, u32[]{:S(2)}, u32[]{:S(2)}) collective-permute-start(bf16[2,2,128,3072]{3,2,1,0:T(8,128)(2,1)} %param.17), channel_id=1, source_target_pairs={{0,8},{16,24},{32,40},{48,56},{64,72},{80,88},{96,104},{112,120},{... | collective-permute-start | bytes 9437192 | tf_op jit(solution)/shard_map/ppermute | solution.py:37
  26.2 71.6 %collective-permute-start.7 = (bf16[2,2,128,3072]{3,2,1,0:T(8,128)(2,1)}, bf16[2,2,128,3072]{3,2,1,0:T(8,128)(2,1)}, u32[]{:S(2)}, u32[]{:S(2)}) collective-permute-start(bf16[2,2,128,3072]{3,2,1,0:T(8,128)(2,1)} %param.17), channel_id=1, source_target_pairs={{0,48},{8,56},{16,0},{24,8},{32,16},{40,24},{48,32},{56,40},{64,11... | collective-permute-start | bytes 9437192 | tf_op jit(solution)/shard_map/ppermute | solution.py:34
  27.9 71.2 %collective-permute-start.14 = (bf16[2,2,128,3072]{3,2,1,0:T(8,128)(2,1)}, bf16[2,2,128,3072]{3,2,1,0:T(8,128)(2,1)}, u32[]{:S(2)}, u32[]{:S(2)}) collective-permute-start(bf16[2,2,128,3072]{3,2,1,0:T(8,128)(2,1)} %param.17), channel_id=1, source_target_pairs={{0,1},{1,2},{2,3},{3,4},{4,5},{5,6},{6,7},{8,9},{9,10},{10,11},{11... | collective-permute-start | bytes 9437192 | tf_op jit(solution)/shard_map/ppermute | solution.py:92
  33.3 71.6 %collective-permute-start.15 = (bf16[2,2,128,3072]{3,2,1,0:T(8,128)(2,1)}, bf16[2,2,128,3072]{3,2,1,0:T(8,128)(2,1)}, u32[]{:S(2)}, u32[]{:S(2)}) collective-permute-start(bf16[2,2,128,3072]{3,2,1,0:T(8,128)(2,1)} %param.17), channel_id=1, source_target_pairs={{1,0},{2,1},{3,2},{4,3},{5,4},{6,5},{7,6},{9,8},{10,9},{11,10},{12... | collective-permute-start | bytes 9437192 | tf_op jit(solution)/shard_map/ppermute | solution.py:92
  50.0 56.2 %copy-start.2 = (f32[512,1536]{1,0:T(8,128)S(1)}, f32[512,1536]{1,0:T(8,128)}, u32[]{:S(2)}) copy-start(f32[512,1536]{1,0:T(8,128)} %get-tuple-element.62) | copy-start | bytes 9437188
  50.0 56.2 %copy-start.7 = (f32[1536]{0:T(1024)S(1)}, f32[1536]{0:T(1024)}, u32[]{:S(2)}) copy-start(f32[1536]{0:T(1024)} %param.15) | copy-start | bytes 18436
  50.0 56.2 %copy-start.8 = (f32[1536]{0:T(1024)S(1)}, f32[1536]{0:T(1024)}, u32[]{:S(2)}) copy-start(f32[1536]{0:T(1024)} %param.14) | copy-start | bytes 18436
  89.0 39.8 %collective-permute-start.5 = (bf16[2,2,128,1536]{3,2,1,0:T(8,128)(2,1)S(1)}, bf16[2,2,128,1536]{3,2,1,0:T(8,128)(2,1)S(1)}, u32[]{:S(2)}, u32[]{:S(2)}) collective-permute-start(bf16[2,2,128,1536]{3,2,1,0:T(8,128)(2,1)S(1)} %slice.156), channel_id=1, source_target_pairs={{0,16},{8,24},{16,32},{24,40},{32,48},{40,56},{48,0},{56,8},{64,80... | collective-permute-start | bytes 4718600 | tf_op jit(solution)/shard_map/ppermute | solution.py:40
  92.8 75.8 %collective-permute-start.16 = (bf16[2,2,128,3072]{3,2,1,0:T(8,128)(2,1)}, bf16[2,2,128,3072]{3,2,1,0:T(8,128)(2,1)}, u32[]{:S(2)}, u32[]{:S(2)}) collective-permute-start(bf16[2,2,128,3072]{3,2,1,0:T(8,128)(2,1)} %collective-permute-done.4), channel_id=1, source_target_pairs={{8,0},{24,16},{40,32},{56,48},{72,64},{88,80},{104,96},{120,112},{... | collective-permute-start | bytes 9437192 | tf_op jit(solution)/shard_map/ppermute | solution.py:38
  97.8 72.0 %collective-permute-start.10 = (bf16[2,2,128,3072]{3,2,1,0:T(8,128)(2,1)}, bf16[2,2,128,3072]{3,2,1,0:T(8,128)(2,1)S(1)}, u32[]{:S(2)}, u32[]{:S(2)}) collective-permute-start(bf16[2,2,128,3072]{3,2,1,0:T(8,128)(2,1)} %collective-permute-done.4), channel_id=1, source_target_pairs={{0,64},{8,72},{1,65},{9,73},{2,66},{10,74},{3,67},{11,75},{4,68},{... | collective-permute-start | bytes 9437192 | tf_op jit(solution)/shard_map/ppermute | solution.py:42
  99.1 83.6 %collective-permute-start.17 = (bf16[2,2,128,3072]{3,2,1,0:T(8,128)(2,1)}, bf16[2,2,128,3072]{3,2,1,0:T(8,128)(2,1)}, u32[]{:S(2)}, u32[]{:S(2)}) collective-permute-start(bf16[2,2,128,3072]{3,2,1,0:T(8,128)(2,1)} %collective-permute-done.7), channel_id=1, source_target_pairs={{0,8},{16,24},{32,40},{48,56},{64,72},{80,88},{96,104},{112,120},{... | collective-permute-start | bytes 9437192 | tf_op jit(solution)/shard_map/ppermute | solution.py:39
  104.9 74.7 %collective-permute-start.11 = (bf16[2,2,128,3072]{3,2,1,0:T(8,128)(2,1)}, bf16[2,2,128,3072]{3,2,1,0:T(8,128)(2,1)}, u32[]{:S(2)}, u32[]{:S(2)}) collective-permute-start(bf16[2,2,128,3072]{3,2,1,0:T(8,128)(2,1)} %collective-permute-done.7), channel_id=1, source_target_pairs={{112,48},{120,56},{113,49},{121,57},{114,50},{122,58},{115,51},{12... | collective-permute-start | bytes 9437192 | tf_op jit(solution)/shard_map/ppermute | solution.py:43
  128.8 38.4 %copy-start.5 = (bf16[2,2,128,1536]{3,2,1,0:T(8,128)(2,1)}, bf16[2,2,128,1536]{3,2,1,0:T(8,128)(2,1)S(1)}, u32[]{:S(2)}) copy-start(bf16[2,2,128,1536]{3,2,1,0:T(8,128)(2,1)S(1)} %collective-permute-done.5) | copy-start | bytes 4718596
  128.8 38.4 %collective-permute-start.8 = (bf16[2,2,128,1536]{3,2,1,0:T(8,128)(2,1)S(1)}, bf16[2,2,128,1536]{3,2,1,0:T(8,128)(2,1)}, u32[]{:S(2)}, u32[]{:S(2)}) collective-permute-start(bf16[2,2,128,1536]{3,2,1,0:T(8,128)(2,1)S(1)} %slice.157), channel_id=1, source_target_pairs={{0,48},{8,56},{16,0},{24,8},{32,16},{40,24},{48,32},{56,40},{64,11... | collective-permute-start | bytes 4718600 | tf_op jit(solution)/shard_map/ppermute | solution.py:41
  167.2 57.5 %collective-permute-start.6 = (bf16[2,2,128,1536]{3,2,1,0:T(8,128)(2,1)S(1)}, bf16[2,2,128,1536]{3,2,1,0:T(8,128)(2,1)S(1)}, u32[]{:S(2)}, u32[]{:S(2)}) collective-permute-start(bf16[2,2,128,1536]{3,2,1,0:T(8,128)(2,1)S(1)} %collective-permute-done.5), channel_id=1, source_target_pairs={{0,64},{8,72},{16,80},{24,88},{96,32},{104,40},{112,48},{120,56},{... | collective-permute-start | bytes 4718600 | tf_op jit(solution)/shard_map/ppermute | solution.py:46
  168.5 76.0 %collective-permute-start.9 = (bf16[2,2,128,1536]{3,2,1,0:T(8,128)(2,1)}, bf16[2,2,128,1536]{3,2,1,0:T(8,128)(2,1)}, u32[]{:S(2)}, u32[]{:S(2)}) collective-permute-start(bf16[2,2,128,1536]{3,2,1,0:T(8,128)(2,1)} %collective-permute-done.8), channel_id=1, source_target_pairs={{0,64},{8,72},{16,80},{24,88},{96,32},{104,40},{112,48},{120,56},{... | collective-permute-start | bytes 4718600 | tf_op jit(solution)/shard_map/ppermute | solution.py:47
  169.9 42.8 %collective-permute-start.12 = (bf16[2,2,128,3072]{3,2,1,0:T(8,128)(2,1)S(1)}, bf16[2,2,128,3072]{3,2,1,0:T(8,128)(2,1)}, u32[]{:S(2)}, u32[]{:S(2)}) collective-permute-start(bf16[2,2,128,3072]{3,2,1,0:T(8,128)(2,1)S(1)} %collective-permute-done.10), channel_id=1, source_target_pairs={{72,64},{73,65},{74,66},{75,67},{76,68},{77,69},{78,70},{79,71}} | collective-permute-start | bytes 9437192 | tf_op jit(solution)/shard_map/ppermute | solution.py:44
  179.7 33.1 %collective-permute-start.13 = (bf16[2,2,128,3072]{3,2,1,0:T(8,128)(2,1)}, bf16[2,2,128,3072]{3,2,1,0:T(8,128)(2,1)}, u32[]{:S(2)}, u32[]{:S(2)}) collective-permute-start(bf16[2,2,128,3072]{3,2,1,0:T(8,128)(2,1)} %collective-permute-done.11), channel_id=1, source_target_pairs={{48,56},{49,57},{50,58},{51,59},{52,60},{53,61},{54,62},{55,63}} | collective-permute-start | bytes 9437192 | tf_op jit(solution)/shard_map/ppermute | solution.py:45
  (4 other events, 63.0 us)
where the time goes:
time: 256 us; the launch traced here: 255 us
  waiting for transfers between devices  105 us (41%)
  Pallas kernels  67.6 us (26%)
  starting transfers between devices  43.7 us (17%)
  local copies, waits for them, and re-layouts  17.1 us (7%)
  matrix products  16.3 us (6%)
  other arithmetic  4.25 us (2%)
    pallas_call x5, Pallas kernels, attend(): pl.pallas_call(functools.partial(attend_kernel, ids, first, last), grid=(...  67.6 us
    ppermute x1, waiting for transfers between devices, fetch_blocks(): below = lax.ppermute(kv, 'tm', up)  35 us
    ppermute x1, waiting for transfers between devices, fetch_blocks(): far_values = lax.ppermute(above[..., half:], 'tm', down)  22 us
    ppermute x1, waiting for transfers between devices, fetch_blocks(): across_values = lax.ppermute(far_values, 'tm', over)  19.8 us
    dot_general x1, matrix products, body(): jnp.dot(normed, w_qkv, preferred_element_type=jnp.float32)  11.1 us
    ppermute x1, waiting for transfers between devices, fetch_blocks(): across_above = lax.ppermute(above, 'tm', [(14, 6), (15, 7)])  7.14 us
    ppermute x1, waiting for transfers between devices, fetch_blocks(): far_keys = lax.ppermute(below[..., :half], 'tm', up)  6.84 us
    ppermute x2, starting transfers between devices, from_behind(): return lax.ppermute(block, axis, route)  6.66 us
  transfers between devices with their start and end apart: 19, of which 11 were waited for; matrix products, arithmetic and copies ran while one was open for 14% of the time, Pallas kernels for 23%

commit v1 on v0

--- a/solution.py
+++ b/solution.py
@@ -12,8 +12,6 @@
 LOG2E = 1.4426950408889634
 AHEAD = 2
 RING = 8
-GROUPS = ((0, 3), (1, 2, 4, 5, 6, 7), (8,), (9, 10, 11, 12), (13,))
-COSTS = (30, 50, 20, 8, 8)
 
 
 def around(device, step):
@@ -24,44 +22,53 @@
     return [(i, i ^ 1) for i in range(2 * RING) if i % 2 == parity]
 
 
-def fetch_blocks(kv):
+def nearest(kv):
     everyone = range(2 * RING)
-    half = kv.shape[-1] // 2
-    up = [(i, around(i, 2)) for i in everyone]
-    down = [(i, around(i, -2)) for i in everyone]
-    over = [(0, 8), (1, 9), (2, 10), (3, 11), (12, 4), (13, 5), (14, 6), (15, 7)]
-    below = lax.ppermute(kv, "tm", up)
-    above = lax.ppermute(kv, "tm", down)
+    below = lax.ppermute(kv, "tm", [(i, around(i, 2)) for i in everyone])
+    above = lax.ppermute(kv, "tm", [(i, around(i, -2)) for i in everyone])
     rows_before = from_behind(kv, "height", 1)
     rows_after = from_behind(kv, "height", -1)
     mate = lax.ppermute(kv, "tm", swap(0) + swap(1))
-    odd_below = lax.ppermute(below, "tm", swap(1))
-    even_above = lax.ppermute(above, "tm", swap(0))
-    far_keys = lax.ppermute(below[..., :half], "tm", up)
-    far_values = lax.ppermute(above[..., half:], "tm", down)
-    across_below = lax.ppermute(below, "tm", [(0, 8), (1, 9)])
-    across_above = lax.ppermute(above, "tm", [(14, 6), (15, 7)])
-    mate_below = lax.ppermute(across_below, "tm", [(9, 8)])
-    mate_above = lax.ppermute(across_above, "tm", [(6, 7)])
-    across_keys = lax.ppermute(far_keys, "tm", over)
-    across_values = lax.ppermute(far_values, "tm", over)
-    singles = (kv, rows_before, rows_after, mate, below, above, odd_below, even_above)
-    crossed = (across_below, across_above, mate_below, mate_above)
-    halves = [(block,) for block in singles] + [(far_keys, far_values)]
-    return halves + [(block,) for block in crossed] + [(across_keys, across_values)]
+    return below, above, rows_before, rows_after, mate
+
+
+def second(below, above, frame_idx):
+    everyone = range(2 * RING)
+    half = below.shape[-1] // 2
+    from_below = (frame_idx < 2) | (frame_idx == 12) | (frame_idx == 13)
+    odd = frame_idx % 2 == 1
+    parts = (
+        below[..., :half],
+        above[..., half:],
+        jnp.where(from_below, below[..., :half], above[..., :half]),
+        jnp.where(from_below, below[..., half:], above[..., half:]),
+    )
+    below_keys, above_values, edge_keys, edge_values = lax.optimization_barrier(parts)
+    over = [(0, 8), (1, 9), (2, 10), (3, 11), (12, 4), (13, 5), (14, 6), (15, 7)]
+    far_keys = lax.ppermute(below_keys, "tm", [(i, around(i, 2)) for i in everyone])
+    far_values = lax.ppermute(above_values, "tm", [(i, around(i, -2)) for i in everyone])
+    cross_keys = lax.ppermute(edge_keys, "tm", over)
+    cross_values = lax.ppermute(edge_values, "tm", over)
+    beside = lax.ppermute(jnp.where(odd, below, above), "tm", swap(0) + swap(1))
+    return far_keys, far_values, cross_keys, cross_values, beside
+
+
+def third(cross):
+    trade = [(8, 10), (9, 11), (10, 8), (11, 9), (4, 6), (5, 7), (6, 4), (7, 5)]
+    return lax.ppermute(cross, "tm", trade), lax.ppermute(cross, "tm", [(9, 8), (6, 7)])
 
 
 def locate(dframe, drow, frame_idx):
     odd = frame_idx % 2
     spot = frame_idx % RING // 2
-    low, high, left = spot == 0, spot == RING // 2 - 1, spot < 2
+    low, high = spot == 0, spot == RING // 2 - 1
     table = {
-        -1: jnp.where(odd == 1, 3, jnp.where(low, 11, 6)),
-        1: jnp.where(odd == 0, 3, jnp.where(high, 12, 7)),
-        -2: jnp.where(low, 9, 4),
-        2: jnp.where(high, 10, 5),
-        -4: jnp.where(left, 13, 8),
-        4: jnp.where(left, 8, 13),
+        -1: jnp.where(odd == 1, 3, jnp.where(low, 9, 6)),
+        1: jnp.where(odd == 0, 3, jnp.where(high, 9, 6)),
+        -2: jnp.where(low, 8, 4),
+        2: jnp.where(high, 8, 5),
+        -4: jnp.where(spot < 2, 10, 7),
+        4: jnp.where(spot < 2, 7, 10),
     }
     source = jnp.where(drow == -1, 1, jnp.where(drow == 1, 2, 0))
     for step, place in table.items():
@@ -288,13 +295,29 @@
     used = lax.broadcasted_iota(jnp.int32, idents.shape, 1) < counts[:, None]
     code = jnp.where(used, source * 4 + idents % tiles_dev, -1).reshape(-1)
     qkv = qkv.reshape(planes, width, 3 * attn_width)
-    blocks = [
-        tuple(part.reshape(planes, width, part.shape[-1]) for part in parts)
-        for parts in fetch_blocks(kv_stale)
-    ]
-    state = None
-    for group, cost in zip(GROUPS, COSTS):
-        state = attend(code, qkv, [(w, blocks[w]) for w in group], state, group is GROUPS[-1], cost)
+
+    def add(state, cost, *sources, last=False):
+        flat = [
+            (which, tuple(part.reshape(planes, width, part.shape[-1]) for part in parts))
+            for which, *parts in sources
+        ]
+        return attend(code, qkv, flat, state, last, cost)
+
+    below, above, rows_before, rows_after, mate = nearest(kv_stale)
+    state = add(None, 20, (0, kv_stale), (3, mate))
+    below, above, state = lax.optimization_barrier((below, above, state))
+    far_keys, far_values, cross_keys, cross_values, beside = second(below, above, frame_idx)
+    near = [(1, rows_before), (2, rows_after), (4, below), (5, above)]
+    state = add(state, 30, *near, (6, beside))
+    cross_keys, state = lax.optimization_barrier((cross_keys, state))
+    trade_keys, mate_keys = third(cross_keys)
+    state = add(state, 15, (7, far_keys, far_values))
+    cross_values, trade_keys, mate_keys, state = lax.optimization_barrier(
+        (cross_values, trade_keys, mate_keys, state)
+    )
+    trade_values, mate_values = third(cross_values)
+    state = add(state, 12, (8, cross_keys, cross_values), (9, mate_keys, mate_values))
+    state = add(state, 8, (10, trade_keys, trade_values), last=True)
     return (state.reshape(frames, rows, width, attn_width), fresh_kv)
 
 

time: 256 us -> 242 us (0.945)
  the two profiles are of different devices: /device:TPU:6 before, /device:TPU:25 now
where the time goes in v1:
time: 242 us; the launch traced here: 239 us
  waiting for transfers between devices  72.8 us (30%)
  Pallas kernels  67 us (28%)
  starting transfers between devices  50.7 us (21%)
  matrix products  19.7 us (8%)
  local copies, waits for them, and re-layouts  14.6 us (6%)
  other arithmetic  13.4 us (6%)
    pallas_call x5, Pallas kernels, attend(): pl.pallas_call(functools.partial(attend_kernel, ids, first, last), grid=(...  67 us
    ppermute x2, waiting for transfers between devices, third(): lax.ppermute(cross, 'tm', trade)  24 us
    ppermute x1, waiting for transfers between devices, nearest(): below = lax.ppermute(kv, 'tm', [(i, around(i, 2)) for i in everyone])  21.1 us
    ppermute x1, waiting for transfers between devices, second(): cross_values = lax.ppermute(edge_values, 'tm', over)  18.6 us
    dot_general x1, matrix products, body(): jnp.dot(normed, w_qkv, preferred_element_type=jnp.float32)  14.4 us
    ppermute x2, starting transfers between devices, third(): lax.ppermute(cross, 'tm', [(9, 8), (6, 7)])  9.38 us
    ppermute x2, starting transfers between devices, from_behind(): return lax.ppermute(block, axis, route)  7.96 us
    ppermute x2, starting transfers between devices, with_halo(): lax.ppermute(tail, axis, [(i, (i + 1) % count) for i in range(ends)])  7.23 us
  transfers between devices with their start and end apart: 18, of which 7 were waited for; matrix products, arithmetic and copies ran while one was open for 17% of the time, Pallas kernels for 24%

profile of v1, /device:TPU:25, one launch (start us, length us, event | category | flops | bytes accessed | tf_op | source)
XLA Modules:
  0.0 239.0 jit_solution(14992280108760926632)
XLA Ops:
  1.6 3.7 %collective-permute-start = (bf16[1,2,8192]{2,1,0:T(2,128)(2,1)S(1)}, bf16[1,2,8192]{2,1,0:T(2,128)(2,1)S(1)}, u32[]{:S(2)}, u32[]{:S(2)}) collective-permute-start(bf16[1,2,8192]{2,1,0:T(2,128)(2,1)S(1)} %get-tuple-element.102), channel_id=1, source_target_pairs={{0,8},{8,16},{16,24},{24,32},{32,40},{40,48},{48,56},{56,64},{64,7... | collective-permute-start | bytes 98312 | tf_op jit(solution)/shard_map/ppermute | solution.py:87
  10.9 3.5 %collective-permute-start.2 = (bf16[4,1,8192]{2,1,0:T(2,128)(2,1)S(1)}, bf16[4,1,8192]{2,1,0:T(2,128)(2,1)S(1)}, u32[]{:S(2)}, u32[]{:S(2)}) collective-permute-start(bf16[4,1,8192]{2,1,0:T(2,128)(2,1)S(1)} %get-tuple-element.99), channel_id=1, source_target_pairs={{0,1},{1,2},{2,3},{3,4},{4,5},{5,6},{6,7},{8,9},{9,10},{10,11},{11... | collective-permute-start | bytes 196616 | tf_op jit(solution)/shard_map/ppermute | solution.py:87
  14.5 4.2 %collective-permute-start.3 = (bf16[4,1,8192]{2,1,0:T(2,128)(2,1)S(1)}, bf16[4,1,8192]{2,1,0:T(2,128)(2,1)S(1)}, u32[]{:S(2)}, u32[]{:S(2)}) collective-permute-start(bf16[4,1,8192]{2,1,0:T(2,128)(2,1)S(1)} %get-tuple-element.100), channel_id=1, source_target_pairs={{1,0},{2,1},{3,2},{4,3},{5,4},{6,5},{7,6},{9,8},{10,9},{11,10},{12... | collective-permute-start | bytes 196616 | tf_op jit(solution)/shard_map/ppermute | solution.py:89
  24.6 4.3 %collective-permute-start.6 = (bf16[2,2,128,3072]{3,2,1,0:T(8,128)(2,1)}, bf16[2,2,128,3072]{3,2,1,0:T(8,128)(2,1)}, u32[]{:S(2)}, u32[]{:S(2)}) collective-permute-start(bf16[2,2,128,3072]{3,2,1,0:T(8,128)(2,1)} %param.17), channel_id=1, source_target_pairs={{0,8},{16,24},{32,40},{48,56},{64,72},{80,88},{96,104},{112,120},{... | collective-permute-start | bytes 9437192 | tf_op jit(solution)/shard_map/ppermute | solution.py:31
  31.5 3.5 %collective-permute-start.9 = (bf16[2,2,128,3072]{3,2,1,0:T(8,128)(2,1)}, bf16[2,2,128,3072]{3,2,1,0:T(8,128)(2,1)}, u32[]{:S(2)}, u32[]{:S(2)}) collective-permute-start(bf16[2,2,128,3072]{3,2,1,0:T(8,128)(2,1)} %param.17), channel_id=1, source_target_pairs={{0,1},{1,2},{2,3},{3,4},{4,5},{5,6},{6,7},{8,9},{9,10},{10,11},{11... | collective-permute-start | bytes 9437192 | tf_op jit(solution)/shard_map/ppermute | solution.py:99
  35.0 4.4 %collective-permute-start.10 = (bf16[2,2,128,3072]{3,2,1,0:T(8,128)(2,1)}, bf16[2,2,128,3072]{3,2,1,0:T(8,128)(2,1)}, u32[]{:S(2)}, u32[]{:S(2)}) collective-permute-start(bf16[2,2,128,3072]{3,2,1,0:T(8,128)(2,1)} %param.17), channel_id=1, source_target_pairs={{1,0},{2,1},{3,2},{4,3},{5,4},{6,5},{7,6},{9,8},{10,9},{11,10},{12... | collective-permute-start | bytes 9437192 | tf_op jit(solution)/shard_map/ppermute | solution.py:99
  39.5 4.5 %concatenate.11 = bf16[2,2,128,1728]{3,2,1,0:T(8,128)(2,1)S(1)} concatenate(bf16[2,2,128,64]{3,2,1,0:T(8,128)(2,1)} %get-tuple-element.98, bf16[2,2,128,64]{3,2,1,0:T(8,128)(2,1)} %get-tuple-element.97, bf16[2,2,128,64]{3,2,1,0:T(8,128)(2,1)} %get-tuple-element.73, bf16[2,2,128,64]{3,2,1,0:T(8,128)(2,1)} %get-tuple-element.74, bf16[2,2,128,64]{3,2,1,0:T(8,128)(2,1)} %get-tuple-element.96, ...), dimensions={3} | concatenate | bytes 3538944 | tf_op jit(solution)/shard_map/concatenate | solution.py:275
  44.0 5.2 %fusion.14 = (f32[512]{0:T(512)S(1)}, f32[512,1536]{1,0:T(8,128)}) fusion(bf16[256,1536]{1,0:T(8,128)(2,1)} %param.13, bf16[512,1536]{1,0:T(8,128)(2,1)} %bitcast.35, bf16[512,1728]{1,0:T(8,128)(2,1)S(1)} %bitcast.34, bf16[1728,256]{1,0:T(8,128)(2,1)S(1)} %copy-done), kind=kOutput, calls=%fused_computation.66 | convolution fusion | flops 858652160 | bytes 8161280 | tf_op jit(solution)/shard_map/dot_general | solution.py:278
  52.1 14.4 %convolution_convert_fusion = bf16[512,4608]{1,0:T(8,128)(2,1)} fusion(bf16[1536,4608]{1,0:T(8,128)(2,1)} %param.16, f32[512,1536]{1,0:T(8,128)S(1)} %copy-done.2, f32[1536]{0:T(1024)S(1)} %copy-done.4, f32[1536]{0:T(1024)S(1)} %copy-done.5, f32[512]{0:T(512)S(1)} %add_rsqrt_fusion, f32[512]{0:T(512)S(1)} %broadcast_multiply_fusion), kind=kOutput, calls=%fused_computation | convolution fusion | flops 7254048768 | bytes 22036480 | tf_op jit(solution)/shard_map/dot_general | solution.py:284
  66.5 12.4 %shard_map.113 = (f32[4,12,128,128]{3,2,1,0:T(8,128)}, f32[4,12,128]{2,1,0:T(8,128)}, f32[4,12,128]{2,1,0:T(8,128)}) custom-call(s32[32]{0:T(128)} %fusion.6.refs_0_, bf16[4,128,4608]{2,1,0:T(8,128)(2,1)} %bitcast.26, bf16[4,128,3072]{2,1,0:T(8,128)(2,1)} %bitcast.4.refs_2_, bf16[4,128,3072]{2,1,0:T(8,128)(2,1)} %bitcast.5.refs_3_), custom_call_target="tpu_custom_call" | custom-call | flops 20000000000 | bytes 60000000 | tf_op jit(solution)/shard_map/pallas_call | solution.py:234
  79.0 21.1 %collective-permute-done.4 = bf16[2,2,128,3072]{3,2,1,0:T(8,128)(2,1)} collective-permute-done((bf16[2,2,128,3072]{3,2,1,0:T(8,128)(2,1)}, bf16[2,2,128,3072]{3,2,1,0:T(8,128)(2,1)}, u32[]{:S(2)}, u32[]{:S(2)}) %collective-permute-start.4) | collective-permute-done | bytes 3145760 | tf_op jit(solution)/shard_map/ppermute | solution.py:27
  100.1 3.9 %broadcast_select_fusion = bf16[2,2,128,3072]{3,2,1,0:T(8,128)(2,1)} fusion(bf16[2,2,128,3072]{3,2,1,0:T(8,128)(2,1)} %collective-permute-done.4, bf16[2,2,128,3072]{3,2,1,0:T(8,128)(2,1)} %collective-permute-done.5, pred[]{:T(512)S(6)} %eq.79), kind=kLoop, calls=%fused_computation.4 | loop fusion | flops 1572864 | bytes 9437185 | tf_op jit(solution)/shard_map/jit(_where)/select_n | solution.py:52
  104.8 5.3 %slice_select_fusion = (bf16[2,2,128,1536]{3,2,1,0:T(8,128)(2,1)S(1)}, bf16[2,2,128,1536]{3,2,1,0:T(8,128)(2,1)}, bf16[2,2,128,1536]{3,2,1,0:T(8,128)(2,1)}, bf16[2,2,128,1536]{3,2,1,0:T(8,128)(2,1)}) fusion(bf16[2,2,128,3072]{3,2,1,0:T(8,128)(2,1)} %collective-permute-done.4, pred[]{:T(512)S(6)} %or.7, bf16[2,2,128,3072]{3,2,1,0:T(8,128)(2,1)} %collective-permute-done.5), kind=kLoop, calls=%fused_computation.5 | loop fusion | flops 1572864 | bytes 12582913 | tf_op jit(solution)/shard_map/jit(_where)/select_n | solution.py:44
  111.7 5.6 %collective-permute-start.15 = (bf16[2,2,128,1536]{3,2,1,0:T(8,128)(2,1)}, bf16[2,2,128,1536]{3,2,1,0:T(8,128)(2,1)}, u32[]{:S(2)}, u32[]{:S(2)}) collective-permute-start(bf16[2,2,128,1536]{3,2,1,0:T(8,128)(2,1)} %get-tuple-element.52), channel_id=1, source_target_pairs={{0,48},{8,56},{16,0},{24,8},{32,16},{40,24},{48,32},{56,40},{64,11... | collective-permute-start | bytes 4718600 | tf_op jit(solution)/shard_map/ppermute | solution.py:49
  118.6 24.5 %shard_map.114 = (f32[4,12,128,128]{3,2,1,0:T(8,128)}, f32[4,12,128]{2,1,0:T(8,128)}, f32[4,12,128]{2,1,0:T(8,128)}) custom-call(s32[32]{0:T(128)} %fusion.6.refs_0_, bf16[4,128,4608]{2,1,0:T(8,128)(2,1)} %bitcast.27, bf16[4,128,3072]{2,1,0:T(8,128)(2,1)} %bitcast.6.refs_2_, bf16[4,128,3072]{2,1,0:T(8,128)(2,1)} %bitcast.7.refs_3_, ...), custom_call_target="tpu_custom_call" | custom-call | flops 30000001024 | bytes 90000000 | tf_op jit(solution)/shard_map/pallas_call | solution.py:234
  143.1 6.7 %collective-permute-done.8 = bf16[2,2,128,1536]{3,2,1,0:T(8,128)(2,1)} collective-permute-done((bf16[2,2,128,1536]{3,2,1,0:T(8,128)(2,1)}, bf16[2,2,128,1536]{3,2,1,0:T(8,128)(2,1)}, u32[]{:S(2)}, u32[]{:S(2)}) %collective-permute-start.8) | collective-permute-done | bytes 1572896 | tf_op jit(solution)/shard_map/ppermute | solution.py:50
  151.7 4.2 %collective-permute-start.13 = (bf16[2,2,128,1536]{3,2,1,0:T(8,128)(2,1)}, bf16[2,2,128,1536]{3,2,1,0:T(8,128)(2,1)}, u32[]{:S(2)}, u32[]{:S(2)}) collective-permute-start(bf16[2,2,128,1536]{3,2,1,0:T(8,128)(2,1)} %collective-permute-done.8), channel_id=1, source_target_pairs={{72,64},{48,56},{73,65},{49,57},{74,66},{50,58},{75,67},{51,59},{7... | collective-permute-start | bytes 4718600 | tf_op jit(solution)/shard_map/ppermute | solution.py:58
  156.0 8.9 %shard_map.115 = (f32[4,12,128,128]{3,2,1,0:T(8,128)}, f32[4,12,128]{2,1,0:T(8,128)}, f32[4,12,128]{2,1,0:T(8,128)}) custom-call(s32[32]{0:T(128)} %fusion.6.refs_0_, bf16[4,128,4608]{2,1,0:T(8,128)(2,1)} %bitcast.28, bf16[4,128,1536]{2,1,0:T(8,128)(2,1)} %bitcast.11.refs_2_, bf16[4,128,1536]{2,1,0:T(8,128)(2,1)} %bitcast.12.refs_3_, ...), custom_call_target="tpu_custom_call" | custom-call | flops 15000000512 | bytes 45000000 | tf_op jit(solution)/shard_map/pallas_call | solution.py:234
  164.9 18.6 %collective-permute-done.7 = bf16[2,2,128,1536]{3,2,1,0:T(8,128)(2,1)} collective-permute-done((bf16[2,2,128,1536]{3,2,1,0:T(8,128)(2,1)S(1)}, bf16[2,2,128,1536]{3,2,1,0:T(8,128)(2,1)}, u32[]{:S(2)}, u32[]{:S(2)}) %collective-permute-start.7) | collective-permute-done | bytes 1572896 | tf_op jit(solution)/shard_map/ppermute | solution.py:51
  183.5 3.2 %collective-permute-done.12 = bf16[2,2,128,1536]{3,2,1,0:T(8,128)(2,1)} collective-permute-done((bf16[2,2,128,1536]{3,2,1,0:T(8,128)(2,1)}, bf16[2,2,128,1536]{3,2,1,0:T(8,128)(2,1)}, u32[]{:S(2)}, u32[]{:S(2)}) %collective-permute-start.12) | collective-permute-done | bytes 1572896 | tf_op jit(solution)/shard_map/ppermute | solution.py:58
  186.7 5.2 %collective-permute-start.17 = (bf16[2,2,128,1536]{3,2,1,0:T(8,128)(2,1)}, bf16[2,2,128,1536]{3,2,1,0:T(8,128)(2,1)}, u32[]{:S(2)}, u32[]{:S(2)}) collective-permute-start(bf16[2,2,128,1536]{3,2,1,0:T(8,128)(2,1)} %collective-permute-done.7), channel_id=1, source_target_pairs={{72,64},{48,56},{73,65},{49,57},{74,66},{50,58},{75,67},{51,59},{7... | collective-permute-start | bytes 4718600 | tf_op jit(solution)/shard_map/ppermute | solution.py:58
  196.0 12.1 %shard_map.116 = (f32[4,12,128,128]{3,2,1,0:T(8,128)}, f32[4,12,128]{2,1,0:T(8,128)}, f32[4,12,128]{2,1,0:T(8,128)}) custom-call(s32[32]{0:T(128)} %fusion.6.refs_0_, bf16[4,128,4608]{2,1,0:T(8,128)(2,1)} %bitcast.29, bf16[4,128,1536]{2,1,0:T(8,128)(2,1)} %bitcast.15.refs_2_, bf16[4,128,1536]{2,1,0:T(8,128)(2,1)} %bitcast.16.refs_3_, ...), custom_call_target="tpu_custom_call" | custom-call | flops 12000000000 | bytes 36000000 | tf_op jit(solution)/shard_map/pallas_call | solution.py:234
  208.1 20.8 %collective-permute-done.16 = bf16[2,2,128,1536]{3,2,1,0:T(8,128)(2,1)S(1)} collective-permute-done((bf16[2,2,128,1536]{3,2,1,0:T(8,128)(2,1)}, bf16[2,2,128,1536]{3,2,1,0:T(8,128)(2,1)S(1)}, u32[]{:S(2)}, u32[]{:S(2)}) %collective-permute-start.16) | collective-permute-done | bytes 1572896 | tf_op jit(solution)/shard_map/ppermute | solution.py:58
  230.0 9.0 %shard_map.117 = bf16[4,128,1536]{2,1,0:T(8,128)(2,1)} custom-call(s32[32]{0:T(128)} %fusion.6.refs_0_, bf16[4,128,4608]{2,1,0:T(8,128)(2,1)} %bitcast.30, bf16[4,128,1536]{2,1,0:T(8,128)(2,1)} %bitcast.13.refs_2_, bf16[4,128,1536]{2,1,0:T(8,128)(2,1)} %bitcast.36, f32[4,12,128,128]{3,2,1,0:T(8,128)} %get-tuple-element.65.refs_4_, ...), custom_call_target="tpu_custom_call" | custom-call | flops 8000000000 | bytes 24000000 | tf_op jit(solution)/shard_map/pallas_call | solution.py:234
  (57 shorter events, 28.7 us)
Async XLA Ops:
  0.6 43.4 %copy-start = (bf16[1728,256]{1,0:T(8,128)(2,1)S(1)}, bf16[1728,256]{1,0:T(8,128)(2,1)}, u32[]{:S(2)}) copy-start(bf16[1728,256]{1,0:T(8,128)(2,1)} %param.12) | copy-start | bytes 2654212
  1.6 7.2 %collective-permute-start = (bf16[1,2,8192]{2,1,0:T(2,128)(2,1)S(1)}, bf16[1,2,8192]{2,1,0:T(2,128)(2,1)S(1)}, u32[]{:S(2)}, u32[]{:S(2)}) collective-permute-start(bf16[1,2,8192]{2,1,0:T(2,128)(2,1)S(1)} %get-tuple-element.102), channel_id=1, source_target_pairs={{0,8},{8,16},{16,24},{24,32},{32,40},{40,48},{48,56},{56,64},{64,7... | collective-permute-start | bytes 98312 | tf_op jit(solution)/shard_map/ppermute | solution.py:87
  5.2 5.4 %collective-permute-start.1 = (bf16[1,2,8192]{2,1,0:T(2,128)(2,1)S(1)}, bf16[1,2,8192]{2,1,0:T(2,128)(2,1)S(1)}, u32[]{:S(2)}, u32[]{:S(2)}) collective-permute-start(bf16[1,2,8192]{2,1,0:T(2,128)(2,1)S(1)} %get-tuple-element.101), channel_id=1, source_target_pairs={{8,0},{16,8},{24,16},{32,24},{40,32},{48,40},{56,48},{64,56},{72,6... | collective-permute-start | bytes 98312 | tf_op jit(solution)/shard_map/ppermute | solution.py:89
  10.9 8.3 %collective-permute-start.2 = (bf16[4,1,8192]{2,1,0:T(2,128)(2,1)S(1)}, bf16[4,1,8192]{2,1,0:T(2,128)(2,1)S(1)}, u32[]{:S(2)}, u32[]{:S(2)}) collective-permute-start(bf16[4,1,8192]{2,1,0:T(2,128)(2,1)S(1)} %get-tuple-element.99), channel_id=1, source_target_pairs={{0,1},{1,2},{2,3},{3,4},{4,5},{5,6},{6,7},{8,9},{9,10},{10,11},{11... | collective-permute-start | bytes 196616 | tf_op jit(solution)/shard_map/ppermute | solution.py:87
  14.5 6.2 %collective-permute-start.3 = (bf16[4,1,8192]{2,1,0:T(2,128)(2,1)S(1)}, bf16[4,1,8192]{2,1,0:T(2,128)(2,1)S(1)}, u32[]{:S(2)}, u32[]{:S(2)}) collective-permute-start(bf16[4,1,8192]{2,1,0:T(2,128)(2,1)S(1)} %get-tuple-element.100), channel_id=1, source_target_pairs={{1,0},{2,1},{3,2},{4,3},{5,4},{6,5},{7,6},{9,8},{10,9},{11,10},{12... | collective-permute-start | bytes 196616 | tf_op jit(solution)/shard_map/ppermute | solution.py:89
  24.6 42.0 %collective-permute-start.6 = (bf16[2,2,128,3072]{3,2,1,0:T(8,128)(2,1)}, bf16[2,2,128,3072]{3,2,1,0:T(8,128)(2,1)}, u32[]{:S(2)}, u32[]{:S(2)}) collective-permute-start(bf16[2,2,128,3072]{3,2,1,0:T(8,128)(2,1)} %param.17), channel_id=1, source_target_pairs={{0,8},{16,24},{32,40},{48,56},{64,72},{80,88},{96,104},{112,120},{... | collective-permute-start | bytes 9437192 | tf_op jit(solution)/shard_map/ppermute | solution.py:31
  28.8 71.3 %collective-permute-start.4 = (bf16[2,2,128,3072]{3,2,1,0:T(8,128)(2,1)}, bf16[2,2,128,3072]{3,2,1,0:T(8,128)(2,1)}, u32[]{:S(2)}, u32[]{:S(2)}) collective-permute-start(bf16[2,2,128,3072]{3,2,1,0:T(8,128)(2,1)} %param.17), channel_id=1, source_target_pairs={{0,16},{8,24},{16,32},{24,40},{32,48},{40,56},{48,0},{56,8},{64,80... | collective-permute-start | bytes 9437192 | tf_op jit(solution)/shard_map/ppermute | solution.py:27
  28.8 71.3 %collective-permute-start.5 = (bf16[2,2,128,3072]{3,2,1,0:T(8,128)(2,1)}, bf16[2,2,128,3072]{3,2,1,0:T(8,128)(2,1)}, u32[]{:S(2)}, u32[]{:S(2)}) collective-permute-start(bf16[2,2,128,3072]{3,2,1,0:T(8,128)(2,1)} %param.17), channel_id=1, source_target_pairs={{0,48},{8,56},{16,0},{24,8},{32,16},{40,24},{48,32},{56,40},{64,11... | collective-permute-start | bytes 9437192 | tf_op jit(solution)/shard_map/ppermute | solution.py:28
  31.5 80.2 %collective-permute-start.9 = (bf16[2,2,128,3072]{3,2,1,0:T(8,128)(2,1)}, bf16[2,2,128,3072]{3,2,1,0:T(8,128)(2,1)}, u32[]{:S(2)}, u32[]{:S(2)}) collective-permute-start(bf16[2,2,128,3072]{3,2,1,0:T(8,128)(2,1)} %param.17), channel_id=1, source_target_pairs={{0,1},{1,2},{2,3},{3,4},{4,5},{5,6},{6,7},{8,9},{9,10},{10,11},{11... | collective-permute-start | bytes 9437192 | tf_op jit(solution)/shard_map/ppermute | solution.py:99
  35.0 82.2 %collective-permute-start.10 = (bf16[2,2,128,3072]{3,2,1,0:T(8,128)(2,1)}, bf16[2,2,128,3072]{3,2,1,0:T(8,128)(2,1)}, u32[]{:S(2)}, u32[]{:S(2)}) collective-permute-start(bf16[2,2,128,3072]{3,2,1,0:T(8,128)(2,1)} %param.17), channel_id=1, source_target_pairs={{1,0},{2,1},{3,2},{4,3},{5,4},{6,5},{7,6},{9,8},{10,9},{11,10},{12... | collective-permute-start | bytes 9437192 | tf_op jit(solution)/shard_map/ppermute | solution.py:99
  44.0 7.8 %copy-start.5 = (f32[1536]{0:T(1024)S(1)}, f32[1536]{0:T(1024)}, u32[]{:S(2)}) copy-start(f32[1536]{0:T(1024)} %param.14) | copy-start | bytes 18436
  49.3 2.8 %copy-start.4 = (f32[1536]{0:T(1024)S(1)}, f32[1536]{0:T(1024)}, u32[]{:S(2)}) copy-start(f32[1536]{0:T(1024)} %param.15) | copy-start | bytes 18436
  104.0 14.6 %collective-permute-start.11 = (bf16[2,2,128,3072]{3,2,1,0:T(8,128)(2,1)}, bf16[2,2,128,3072]{3,2,1,0:T(8,128)(2,1)}, u32[]{:S(2)}, u32[]{:S(2)}) collective-permute-start(bf16[2,2,128,3072]{3,2,1,0:T(8,128)(2,1)} %broadcast_select_fusion), channel_id=1, source_target_pairs={{0,8},{16,24},{32,40},{48,56},{64,72},{80,88},{96,104},{112,120},{... | collective-permute-start | bytes 9437192 | tf_op jit(solution)/shard_map/ppermute | solution.py:52
  104.8 89.1 %slice-start = ((s8[4718592]{0:T(1024)(128)(4,1)}), s8[4194304]{0:T(1024)(128)(4,1)S(1)}, s32[]{:S(2)}) async-start(s8[4718592]{0:T(1024)(128)(4,1)} %bitcast.31), calls=%async_computation | async-start | bytes 8388608
  110.1 39.7 %collective-permute-start.8 = (bf16[2,2,128,1536]{3,2,1,0:T(8,128)(2,1)}, bf16[2,2,128,1536]{3,2,1,0:T(8,128)(2,1)}, u32[]{:S(2)}, u32[]{:S(2)}) collective-permute-start(bf16[2,2,128,1536]{3,2,1,0:T(8,128)(2,1)} %get-tuple-element.43), channel_id=1, source_target_pairs={{0,64},{8,72},{16,80},{24,88},{96,32},{104,40},{112,48},{120,56},{... | collective-permute-start | bytes 4718600 | tf_op jit(solution)/shard_map/ppermute | solution.py:50
  111.4 44.6 %collective-permute-start.14 = (bf16[2,2,128,1536]{3,2,1,0:T(8,128)(2,1)}, bf16[2,2,128,1536]{3,2,1,0:T(8,128)(2,1)}, u32[]{:S(2)}, u32[]{:S(2)}) collective-permute-start(bf16[2,2,128,1536]{3,2,1,0:T(8,128)(2,1)} %get-tuple-element.51), channel_id=1, source_target_pairs={{0,16},{8,24},{16,32},{24,40},{32,48},{40,56},{48,0},{56,8},{64,80... | collective-permute-start | bytes 4718600 | tf_op jit(solution)/shard_map/ppermute | solution.py:48
  111.7 44.3 %collective-permute-start.15 = (bf16[2,2,128,1536]{3,2,1,0:T(8,128)(2,1)}, bf16[2,2,128,1536]{3,2,1,0:T(8,128)(2,1)}, u32[]{:S(2)}, u32[]{:S(2)}) collective-permute-start(bf16[2,2,128,1536]{3,2,1,0:T(8,128)(2,1)} %get-tuple-element.52), channel_id=1, source_target_pairs={{0,48},{8,56},{16,0},{24,8},{32,16},{40,24},{48,32},{56,40},{64,11... | collective-permute-start | bytes 4718600 | tf_op jit(solution)/shard_map/ppermute | solution.py:49
  117.3 66.3 %collective-permute-start.7 = (bf16[2,2,128,1536]{3,2,1,0:T(8,128)(2,1)S(1)}, bf16[2,2,128,1536]{3,2,1,0:T(8,128)(2,1)}, u32[]{:S(2)}, u32[]{:S(2)}) collective-permute-start(bf16[2,2,128,1536]{3,2,1,0:T(8,128)(2,1)S(1)} %get-tuple-element.42), channel_id=1, source_target_pairs={{0,64},{8,72},{16,80},{24,88},{96,32},{104,40},{112,48},{120,56},{... | collective-permute-start | bytes 4718600 | tf_op jit(solution)/shard_map/ppermute | solution.py:51
  118.6 75.3 %slice-start.1 = ((s8[4718592]{0:T(1024)(128)(4,1)}), s8[524288]{0:T(1024)(128)(4,1)S(1)}, s32[]{:S(2)}) async-start(s8[4718592]{0:T(1024)(128)(4,1)} %bitcast.31), calls=%async_computation.1 | async-start | bytes 1048576
  149.8 36.9 %collective-permute-start.12 = (bf16[2,2,128,1536]{3,2,1,0:T(8,128)(2,1)}, bf16[2,2,128,1536]{3,2,1,0:T(8,128)(2,1)}, u32[]{:S(2)}, u32[]{:S(2)}) collective-permute-start(bf16[2,2,128,1536]{3,2,1,0:T(8,128)(2,1)} %collective-permute-done.8), channel_id=1, source_target_pairs={{64,80},{72,88},{80,64},{88,72},{32,48},{40,56},{48,32},{56,40},{6... | collective-permute-start | bytes 4718600 | tf_op jit(solution)/shard_map/ppermute | solution.py:58
  151.7 35.0 %collective-permute-start.13 = (bf16[2,2,128,1536]{3,2,1,0:T(8,128)(2,1)}, bf16[2,2,128,1536]{3,2,1,0:T(8,128)(2,1)}, u32[]{:S(2)}, u32[]{:S(2)}) collective-permute-start(bf16[2,2,128,1536]{3,2,1,0:T(8,128)(2,1)} %collective-permute-done.8), channel_id=1, source_target_pairs={{72,64},{48,56},{73,65},{49,57},{74,66},{50,58},{75,67},{51,59},{7... | collective-permute-start | bytes 4718600 | tf_op jit(solution)/shard_map/ppermute | solution.py:58
  186.7 9.2 %collective-permute-start.17 = (bf16[2,2,128,1536]{3,2,1,0:T(8,128)(2,1)}, bf16[2,2,128,1536]{3,2,1,0:T(8,128)(2,1)}, u32[]{:S(2)}, u32[]{:S(2)}) collective-permute-start(bf16[2,2,128,1536]{3,2,1,0:T(8,128)(2,1)} %collective-permute-done.7), channel_id=1, source_target_pairs={{72,64},{48,56},{73,65},{49,57},{74,66},{50,58},{75,67},{51,59},{7... | collective-permute-start | bytes 4718600 | tf_op jit(solution)/shard_map/ppermute | solution.py:58
  191.9 36.9 %collective-permute-start.16 = (bf16[2,2,128,1536]{3,2,1,0:T(8,128)(2,1)}, bf16[2,2,128,1536]{3,2,1,0:T(8,128)(2,1)S(1)}, u32[]{:S(2)}, u32[]{:S(2)}) collective-permute-start(bf16[2,2,128,1536]{3,2,1,0:T(8,128)(2,1)} %collective-permute-done.7), channel_id=1, source_target_pairs={{64,80},{72,88},{80,64},{88,72},{32,48},{40,56},{48,32},{56,40},{6... | collective-permute-start | bytes 4718600 | tf_op jit(solution)/shard_map/ppermute | solution.py:58
  230.0 9.0 %copy-start.1 = (bf16[1728,256]{1,0:T(8,128)(2,1)S(1)}, bf16[1728,256]{1,0:T(8,128)(2,1)}, u32[]{:S(2)}) copy-start(bf16[1728,256]{1,0:T(8,128)(2,1)} %param.12) | copy-start | bytes 2654212
  (2 other events, 4.1 us)

commit v2 on v1

--- a/solution.py
+++ b/solution.py
@@ -22,14 +22,18 @@
     return [(i, i ^ 1) for i in range(2 * RING) if i % 2 == parity]
 
 
-def nearest(kv):
+def ring_sides(kv):
     everyone = range(2 * RING)
     below = lax.ppermute(kv, "tm", [(i, around(i, 2)) for i in everyone])
     above = lax.ppermute(kv, "tm", [(i, around(i, -2)) for i in everyone])
+    return below, above
+
+
+def nearest(kv):
     rows_before = from_behind(kv, "height", 1)
     rows_after = from_behind(kv, "height", -1)
     mate = lax.ppermute(kv, "tm", swap(0) + swap(1))
-    return below, above, rows_before, rows_after, mate
+    return rows_before, rows_after, mate
 
 
 def second(below, above, frame_idx):
@@ -43,7 +47,8 @@
         jnp.where(from_below, below[..., :half], above[..., :half]),
         jnp.where(from_below, below[..., half:], above[..., half:]),
     )
-    below_keys, above_values, edge_keys, edge_values = lax.optimization_barrier(parts)
+    parts, below, above = lax.optimization_barrier((parts, below, above))
+    below_keys, above_values, edge_keys, edge_values = parts
     over = [(0, 8), (1, 9), (2, 10), (3, 11), (12, 4), (13, 5), (14, 6), (15, 7)]
     far_keys = lax.ppermute(below_keys, "tm", [(i, around(i, 2)) for i in everyone])
     far_values = lax.ppermute(above_values, "tm", [(i, around(i, -2)) for i in everyone])
@@ -262,8 +267,12 @@
     cin = conv_weight.shape[0] // 27
     attn_width = HEADS * HD
     planes = frames * rows
-    rim = with_halo(control, (("tm", 0), ("height", 1)), 1)
+    rim = with_halo(control, (("tm", 0),), 1)
     rim, kv_stale = lax.optimization_barrier((rim, kv_stale))
+    below, above = ring_sides(kv_stale)
+    rim = with_halo(rim, (("height", 1),), 1)
+    rim, kv_late = lax.optimization_barrier((rim, kv_stale))
+    rows_before, rows_after, mate = nearest(kv_late)
     grid = rim.reshape(frames + 2, rows + 2, width, cin)
     grid = jnp.pad(grid, ((0, 0), (0, 0), (1, 1), (0, 0)))
     taps = [
@@ -303,7 +312,6 @@
         ]
         return attend(code, qkv, flat, state, last, cost)
 
-    below, above, rows_before, rows_after, mate = nearest(kv_stale)
     state = add(None, 20, (0, kv_stale), (3, mate))
     below, above, state = lax.optimization_barrier((below, above, state))
     far_keys, far_values, cross_keys, cross_values, beside = second(below, above, frame_idx)

time: 242 us -> 233 us (0.963)
  waiting for transfers between devices: 72.8 us -> 62.9 us
    ppermute x2, waiting for transfers between devices: 21.1 us -> 8.3 us  [the longest x1 7.51 us: ring_sides(): below = lax.ppermute(kv, 'tm', [(i, around(i, 2)) for i in everyone])]
    ppermute x1, starting transfers between devices: 5.6 us -> 1.89 us  [second(): lax.ppermute(above_values, 'tm', [(i, around(i, -2)) for i in everyone])]
    ppermute x2, starting transfers between devices: 9.38 us -> 13 us  [third(): lax.ppermute(cross, 'tm', [(9, 8), (6, 7)])]
  transfers between devices with their start and end apart: 18 -> 18, of which waited for: 7 -> 8; matrix products, arithmetic and copies ran while one was open for 17% -> 18% of each run, Pallas kernels for 24% -> 25%
where the time goes in v2:
time: 233 us; the launch traced here: 232 us
  Pallas kernels  68.3 us (29%)
  waiting for transfers between devices  62.9 us (27%)
  starting transfers between devices  51.7 us (22%)
  matrix products  19.7 us (8%)
  local copies, waits for them, and re-layouts  15.3 us (7%)
  other arithmetic  12.8 us (5%)
    pallas_call x5, Pallas kernels, attend(): pl.pallas_call(functools.partial(attend_kernel, ids, first, last), grid=(...  68.3 us
    ppermute x2, waiting for transfers between devices, third(): lax.ppermute(cross, 'tm', trade)  25.2 us
    ppermute x1, waiting for transfers between devices, second(): cross_values = lax.ppermute(edge_values, 'tm', over)  18.8 us
    dot_general x1, matrix products, body(): jnp.dot(normed, w_qkv, preferred_element_type=jnp.float32)  14.4 us
    ppermute x2, starting transfers between devices, third(): lax.ppermute(cross, 'tm', [(9, 8), (6, 7)])  13 us
    ppermute x1, waiting for transfers between devices, ring_sides(): below = lax.ppermute(kv, 'tm', [(i, around(i, 2)) for i in everyone])  7.51 us
    ppermute x2, starting transfers between devices, from_behind(): return lax.ppermute(block, axis, route)  7.39 us
    ppermute x2, starting transfers between devices, with_halo(): lax.ppermute(tail, axis, [(i, (i + 1) % count) for i in range(ends)])  7.23 us
  transfers between devices with their start and end apart: 18, of which 8 were waited for; matrix products, arithmetic and copies ran while one was open for 18% of the time, Pallas kernels for 25%

profile of v2, /device:TPU:25, one launch (start us, length us, event | category | flops | bytes accessed | tf_op | source)
XLA Modules:
  0.0 231.6 jit_solution(14511470974966207937)
XLA Ops:
  1.6 3.7 %collective-permute-start = (bf16[1,2,8192]{2,1,0:T(2,128)(2,1)S(1)}, bf16[1,2,8192]{2,1,0:T(2,128)(2,1)S(1)}, u32[]{:S(2)}, u32[]{:S(2)}) collective-permute-start(bf16[1,2,8192]{2,1,0:T(2,128)(2,1)S(1)} %get-tuple-element.109), channel_id=1, source_target_pairs={{0,8},{8,16},{16,24},{24,32},{32,40},{40,48},{48,56},{56,64},{64,7... | collective-permute-start | bytes 98312 | tf_op jit(solution)/shard_map/ppermute | solution.py:92
  11.9 3.5 %collective-permute-start.2 = (bf16[4,1,8192]{2,1,0:T(2,128)(2,1)S(1)}, bf16[4,1,8192]{2,1,0:T(2,128)(2,1)S(1)}, u32[]{:S(2)}, u32[]{:S(2)}) collective-permute-start(bf16[4,1,8192]{2,1,0:T(2,128)(2,1)S(1)} %get-tuple-element.107), channel_id=1, source_target_pairs={{0,1},{1,2},{2,3},{3,4},{4,5},{5,6},{6,7},{8,9},{9,10},{10,11},{11... | collective-permute-start | bytes 196616 | tf_op jit(solution)/shard_map/ppermute | solution.py:92
  15.5 4.2 %collective-permute-start.3 = (bf16[4,1,8192]{2,1,0:T(2,128)(2,1)S(1)}, bf16[4,1,8192]{2,1,0:T(2,128)(2,1)S(1)}, u32[]{:S(2)}, u32[]{:S(2)}) collective-permute-start(bf16[4,1,8192]{2,1,0:T(2,128)(2,1)S(1)} %get-tuple-element.108), channel_id=1, source_target_pairs={{1,0},{2,1},{3,2},{4,3},{5,4},{6,5},{7,6},{9,8},{10,9},{11,10},{12... | collective-permute-start | bytes 196616 | tf_op jit(solution)/shard_map/ppermute | solution.py:94
  26.9 3.2 %collective-permute-start.6 = (bf16[2,2,128,3072]{3,2,1,0:T(8,128)(2,1)}, bf16[2,2,128,3072]{3,2,1,0:T(8,128)(2,1)}, u32[]{:S(2)}, u32[]{:S(2)}) collective-permute-start(bf16[2,2,128,3072]{3,2,1,0:T(8,128)(2,1)} %param.17), channel_id=1, source_target_pairs={{0,8},{16,24},{32,40},{48,56},{64,72},{80,88},{96,104},{112,120},{... | collective-permute-start | bytes 9437192 | tf_op jit(solution)/shard_map/ppermute | solution.py:35
  30.1 2.4 %collective-permute-start.9 = (bf16[2,2,128,3072]{3,2,1,0:T(8,128)(2,1)}, bf16[2,2,128,3072]{3,2,1,0:T(8,128)(2,1)}, u32[]{:S(2)}, u32[]{:S(2)}) collective-permute-start(bf16[2,2,128,3072]{3,2,1,0:T(8,128)(2,1)} %param.17), channel_id=1, source_target_pairs={{0,1},{1,2},{2,3},{3,4},{4,5},{5,6},{6,7},{8,9},{9,10},{10,11},{11... | collective-permute-start | bytes 9437192 | tf_op jit(solution)/shard_map/ppermute | solution.py:104
  32.5 5.0 %collective-permute-start.10 = (bf16[2,2,128,3072]{3,2,1,0:T(8,128)(2,1)}, bf16[2,2,128,3072]{3,2,1,0:T(8,128)(2,1)}, u32[]{:S(2)}, u32[]{:S(2)}) collective-permute-start(bf16[2,2,128,3072]{3,2,1,0:T(8,128)(2,1)} %param.17), channel_id=1, source_target_pairs={{1,0},{2,1},{3,2},{4,3},{5,4},{6,5},{7,6},{9,8},{10,9},{11,10},{12... | collective-permute-start | bytes 9437192 | tf_op jit(solution)/shard_map/ppermute | solution.py:104
  37.5 4.5 %concatenate.11 = bf16[2,2,128,1728]{3,2,1,0:T(8,128)(2,1)S(1)} concatenate(bf16[2,2,128,64]{3,2,1,0:T(8,128)(2,1)} %get-tuple-element.106, bf16[2,2,128,64]{3,2,1,0:T(8,128)(2,1)} %get-tuple-element.105, bf16[2,2,128,64]{3,2,1,0:T(8,128)(2,1)} %get-tuple-element.81, bf16[2,2,128,64]{3,2,1,0:T(8,128)(2,1)} %get-tuple-element.82, bf16[2,2,128,64]{3,2,1,0:T(8,128)(2,1)} %get-tuple-element.104, ...), dimensions={3} | concatenate | bytes 3538944 | tf_op jit(solution)/shard_map/concatenate | solution.py:284
  42.1 5.2 %fusion.14 = (f32[512]{0:T(512)S(1)}, f32[512,1536]{1,0:T(8,128)}) fusion(bf16[256,1536]{1,0:T(8,128)(2,1)} %param.13, bf16[512,1536]{1,0:T(8,128)(2,1)} %bitcast.36, bf16[512,1728]{1,0:T(8,128)(2,1)S(1)} %bitcast.34, bf16[1728,256]{1,0:T(8,128)(2,1)S(1)} %copy-done), kind=kOutput, calls=%fused_computation.64 | convolution fusion | flops 858652160 | bytes 8161280 | tf_op jit(solution)/shard_map/dot_general | solution.py:287
  47.3 2.5 %multiply_reduce_fusion = f32[512]{0:T(512)S(1)} fusion(f32[512,1536]{1,0:T(8,128)} %get-tuple-element.112, f32[512]{0:T(512)S(1)} %broadcast_multiply_fusion), kind=kLoop, calls=%fused_computation.3 | loop fusion | flops 2358784 | bytes 3149824 | tf_op jit(solution)/shard_map/reduce_sum | solution.py:291
  50.1 14.4 %convolution_convert_fusion = bf16[512,4608]{1,0:T(8,128)(2,1)} fusion(bf16[1536,4608]{1,0:T(8,128)(2,1)} %param.16, f32[512,1536]{1,0:T(8,128)S(1)} %copy-done.2, f32[1536]{0:T(1024)S(1)} %copy-done.5, f32[1536]{0:T(1024)S(1)} %copy-done.6, f32[512]{0:T(512)S(1)} %add_rsqrt_fusion, f32[512]{0:T(512)S(1)} %broadcast_multiply_fusion), kind=kOutput, calls=%fused_computation | convolution fusion | flops 7254048768 | bytes 22036480 | tf_op jit(solution)/shard_map/dot_general | solution.py:293
  64.6 16.7 %shard_map.113 = (f32[4,12,128,128]{3,2,1,0:T(8,128)}, f32[4,12,128]{2,1,0:T(8,128)}, f32[4,12,128]{2,1,0:T(8,128)}) custom-call(s32[32]{0:T(128)} %fusion.6.refs_0_, bf16[4,128,4608]{2,1,0:T(8,128)(2,1)} %bitcast.26, bf16[4,128,3072]{2,1,0:T(8,128)(2,1)} %bitcast.4.refs_2_, bf16[4,128,3072]{2,1,0:T(8,128)(2,1)} %bitcast.5.refs_3_), custom_call_target="tpu_custom_call" | custom-call | flops 20000000000 | bytes 60000000 | tf_op jit(solution)/shard_map/pallas_call | solution.py:239
  81.3 7.5 %collective-permute-done.4 = bf16[2,2,128,3072]{3,2,1,0:T(8,128)(2,1)} collective-permute-done((bf16[2,2,128,3072]{3,2,1,0:T(8,128)(2,1)}, bf16[2,2,128,3072]{3,2,1,0:T(8,128)(2,1)}, u32[]{:S(2)}, u32[]{:S(2)}) %collective-permute-start.4) | collective-permute-done | bytes 3145760 | tf_op jit(solution)/shard_map/ppermute | solution.py:27
  89.6 5.2 %slice_select_fusion = (bf16[2,2,128,1536]{3,2,1,0:T(8,128)(2,1)S(1)}, bf16[2,2,128,1536]{3,2,1,0:T(8,128)(2,1)}, bf16[2,2,128,1536]{3,2,1,0:T(8,128)(2,1)}, bf16[2,2,128,1536]{3,2,1,0:T(8,128)(2,1)}) fusion(bf16[2,2,128,3072]{3,2,1,0:T(8,128)(2,1)} %collective-permute-done.4, pred[]{:T(512)S(6)} %or.7, bf16[2,2,128,3072]{3,2,1,0:T(8,128)(2,1)} %collective-permute-done.5), kind=kLoop, calls=%fused_computation.5 | loop fusion | flops 1572864 | bytes 12582913 | tf_op jit(solution)/shard_map/jit(_where)/select_n | solution.py:48
  94.8 2.4 %broadcast_select_fusion = bf16[2,2,128,3072]{3,2,1,0:T(8,128)(2,1)S(1)} fusion(bf16[2,2,128,3072]{3,2,1,0:T(8,128)(2,1)} %collective-permute-done.4, bf16[2,2,128,3072]{3,2,1,0:T(8,128)(2,1)} %collective-permute-done.5, pred[]{:T(512)S(6)} %eq.79), kind=kLoop, calls=%fused_computation.4 | loop fusion | flops 1572864 | bytes 9437185 | tf_op jit(solution)/shard_map/jit(_where)/select_n | solution.py:57
  97.1 2.8 %collective-permute-start.11 = (bf16[2,2,128,3072]{3,2,1,0:T(8,128)(2,1)S(1)}, bf16[2,2,128,3072]{3,2,1,0:T(8,128)(2,1)S(1)}, u32[]{:S(2)}, u32[]{:S(2)}) collective-permute-start(bf16[2,2,128,3072]{3,2,1,0:T(8,128)(2,1)S(1)} %broadcast_select_fusion), channel_id=1, source_target_pairs={{0,8},{16,24},{32,40},{48,56},{64,72},{80,88},{96,104},{112,120},{... | collective-permute-start | bytes 9437192 | tf_op jit(solution)/shard_map/ppermute | solution.py:57
  109.0 25.6 %shard_map.114 = (f32[4,12,128,128]{3,2,1,0:T(8,128)}, f32[4,12,128]{2,1,0:T(8,128)}, f32[4,12,128]{2,1,0:T(8,128)}) custom-call(s32[32]{0:T(128)} %fusion.6.refs_0_, bf16[4,128,4608]{2,1,0:T(8,128)(2,1)} %bitcast.27, bf16[4,128,3072]{2,1,0:T(8,128)(2,1)} %bitcast.6.refs_2_, bf16[4,128,3072]{2,1,0:T(8,128)(2,1)} %bitcast.7.refs_3_, ...), custom_call_target="tpu_custom_call" | custom-call | flops 30000001024 | bytes 90000000 | tf_op jit(solution)/shard_map/pallas_call | solution.py:239
  134.6 6.7 %collective-permute-done.8 = bf16[2,2,128,1536]{3,2,1,0:T(8,128)(2,1)} collective-permute-done((bf16[2,2,128,1536]{3,2,1,0:T(8,128)(2,1)}, bf16[2,2,128,1536]{3,2,1,0:T(8,128)(2,1)}, u32[]{:S(2)}, u32[]{:S(2)}) %collective-permute-start.8) | collective-permute-done | bytes 1572896 | tf_op jit(solution)/shard_map/ppermute | solution.py:55
  143.2 6.0 %collective-permute-start.13 = (bf16[2,2,128,1536]{3,2,1,0:T(8,128)(2,1)}, bf16[2,2,128,1536]{3,2,1,0:T(8,128)(2,1)}, u32[]{:S(2)}, u32[]{:S(2)}) collective-permute-start(bf16[2,2,128,1536]{3,2,1,0:T(8,128)(2,1)} %collective-permute-done.8), channel_id=1, source_target_pairs={{72,64},{48,56},{73,65},{49,57},{74,66},{50,58},{75,67},{51,59},{7... | collective-permute-start | bytes 4718600 | tf_op jit(solution)/shard_map/ppermute | solution.py:63
  149.3 6.9 %shard_map.115 = (f32[4,12,128,128]{3,2,1,0:T(8,128)}, f32[4,12,128]{2,1,0:T(8,128)}, f32[4,12,128]{2,1,0:T(8,128)}) custom-call(s32[32]{0:T(128)} %fusion.6.refs_0_, bf16[4,128,4608]{2,1,0:T(8,128)(2,1)} %bitcast.28, bf16[4,128,1536]{2,1,0:T(8,128)(2,1)} %bitcast.11.refs_2_, bf16[4,128,1536]{2,1,0:T(8,128)(2,1)} %bitcast.12.refs_3_, ...), custom_call_target="tpu_custom_call" | custom-call | flops 15000000512 | bytes 45000000 | tf_op jit(solution)/shard_map/pallas_call | solution.py:239
  156.2 18.8 %collective-permute-done.7 = bf16[2,2,128,1536]{3,2,1,0:T(8,128)(2,1)} collective-permute-done((bf16[2,2,128,1536]{3,2,1,0:T(8,128)(2,1)S(1)}, bf16[2,2,128,1536]{3,2,1,0:T(8,128)(2,1)}, u32[]{:S(2)}, u32[]{:S(2)}) %collective-permute-start.7) | collective-permute-done | bytes 1572896 | tf_op jit(solution)/shard_map/ppermute | solution.py:56
  176.4 7.0 %collective-permute-start.17 = (bf16[2,2,128,1536]{3,2,1,0:T(8,128)(2,1)}, bf16[2,2,128,1536]{3,2,1,0:T(8,128)(2,1)}, u32[]{:S(2)}, u32[]{:S(2)}) collective-permute-start(bf16[2,2,128,1536]{3,2,1,0:T(8,128)(2,1)} %collective-permute-done.7), channel_id=1, source_target_pairs={{72,64},{48,56},{73,65},{49,57},{74,66},{50,58},{75,67},{51,59},{7... | collective-permute-start | bytes 4718600 | tf_op jit(solution)/shard_map/ppermute | solution.py:63
  187.5 9.1 %shard_map.116 = (f32[4,12,128,128]{3,2,1,0:T(8,128)}, f32[4,12,128]{2,1,0:T(8,128)}, f32[4,12,128]{2,1,0:T(8,128)}) custom-call(s32[32]{0:T(128)} %fusion.6.refs_0_, bf16[4,128,4608]{2,1,0:T(8,128)(2,1)} %bitcast.29, bf16[4,128,1536]{2,1,0:T(8,128)(2,1)} %bitcast.15.refs_2_, bf16[4,128,1536]{2,1,0:T(8,128)(2,1)} %bitcast.16.refs_3_, ...), custom_call_target="tpu_custom_call" | custom-call | flops 12000000000 | bytes 36000000 | tf_op jit(solution)/shard_map/pallas_call | solution.py:239
  196.5 23.7 %collective-permute-done.16 = bf16[2,2,128,1536]{3,2,1,0:T(8,128)(2,1)S(1)} collective-permute-done((bf16[2,2,128,1536]{3,2,1,0:T(8,128)(2,1)}, bf16[2,2,128,1536]{3,2,1,0:T(8,128)(2,1)S(1)}, u32[]{:S(2)}, u32[]{:S(2)}) %collective-permute-start.16) | collective-permute-done | bytes 1572896 | tf_op jit(solution)/shard_map/ppermute | solution.py:63
  221.5 10.1 %shard_map.117 = bf16[4,128,1536]{2,1,0:T(8,128)(2,1)} custom-call(s32[32]{0:T(128)} %fusion.6.refs_0_, bf16[4,128,4608]{2,1,0:T(8,128)(2,1)} %bitcast.30, bf16[4,128,1536]{2,1,0:T(8,128)(2,1)} %bitcast.13.refs_2_, bf16[4,128,1536]{2,1,0:T(8,128)(2,1)} %bitcast.37, f32[4,12,128,128]{3,2,1,0:T(8,128)} %get-tuple-element.73.refs_4_, ...), custom_call_target="tpu_custom_call" | custom-call | flops 8000000000 | bytes 24000000 | tf_op jit(solution)/shard_map/pallas_call | solution.py:239
  (57 shorter events, 33.5 us)
Async XLA Ops:
  0.6 41.4 %copy-start = (bf16[1728,256]{1,0:T(8,128)(2,1)S(1)}, bf16[1728,256]{1,0:T(8,128)(2,1)}, u32[]{:S(2)}) copy-start(bf16[1728,256]{1,0:T(8,128)(2,1)} %param.12) | copy-start | bytes 2654212
  1.6 7.2 %collective-permute-start = (bf16[1,2,8192]{2,1,0:T(2,128)(2,1)S(1)}, bf16[1,2,8192]{2,1,0:T(2,128)(2,1)S(1)}, u32[]{:S(2)}, u32[]{:S(2)}) collective-permute-start(bf16[1,2,8192]{2,1,0:T(2,128)(2,1)S(1)} %get-tuple-element.109), channel_id=1, source_target_pairs={{0,8},{8,16},{16,24},{24,32},{32,40},{40,48},{48,56},{56,64},{64,7... | collective-permute-start | bytes 98312 | tf_op jit(solution)/shard_map/ppermute | solution.py:92
  5.2 5.4 %collective-permute-start.1 = (bf16[1,2,8192]{2,1,0:T(2,128)(2,1)S(1)}, bf16[1,2,8192]{2,1,0:T(2,128)(2,1)S(1)}, u32[]{:S(2)}, u32[]{:S(2)}) collective-permute-start(bf16[1,2,8192]{2,1,0:T(2,128)(2,1)S(1)} %get-tuple-element.110), channel_id=1, source_target_pairs={{8,0},{16,8},{24,16},{32,24},{40,32},{48,40},{56,48},{64,56},{72,6... | collective-permute-start | bytes 98312 | tf_op jit(solution)/shard_map/ppermute | solution.py:94
  11.9 11.0 %collective-permute-start.2 = (bf16[4,1,8192]{2,1,0:T(2,128)(2,1)S(1)}, bf16[4,1,8192]{2,1,0:T(2,128)(2,1)S(1)}, u32[]{:S(2)}, u32[]{:S(2)}) collective-permute-start(bf16[4,1,8192]{2,1,0:T(2,128)(2,1)S(1)} %get-tuple-element.107), channel_id=1, source_target_pairs={{0,1},{1,2},{2,3},{3,4},{4,5},{5,6},{6,7},{8,9},{9,10},{10,11},{11... | collective-permute-start | bytes 196616 | tf_op jit(solution)/shard_map/ppermute | solution.py:92
  15.5 7.5 %collective-permute-start.3 = (bf16[4,1,8192]{2,1,0:T(2,128)(2,1)S(1)}, bf16[4,1,8192]{2,1,0:T(2,128)(2,1)S(1)}, u32[]{:S(2)}, u32[]{:S(2)}) collective-permute-start(bf16[4,1,8192]{2,1,0:T(2,128)(2,1)S(1)} %get-tuple-element.108), channel_id=1, source_target_pairs={{1,0},{2,1},{3,2},{4,3},{5,4},{6,5},{7,6},{9,8},{10,9},{11,10},{12... | collective-permute-start | bytes 196616 | tf_op jit(solution)/shard_map/ppermute | solution.py:94
  20.3 68.5 %collective-permute-start.4 = (bf16[2,2,128,3072]{3,2,1,0:T(8,128)(2,1)}, bf16[2,2,128,3072]{3,2,1,0:T(8,128)(2,1)}, u32[]{:S(2)}, u32[]{:S(2)}) collective-permute-start(bf16[2,2,128,3072]{3,2,1,0:T(8,128)(2,1)} %param.17), channel_id=1, source_target_pairs={{0,16},{8,24},{16,32},{24,40},{32,48},{40,56},{48,0},{56,8},{64,80... | collective-permute-start | bytes 9437192 | tf_op jit(solution)/shard_map/ppermute | solution.py:27
  21.3 68.3 %collective-permute-start.5 = (bf16[2,2,128,3072]{3,2,1,0:T(8,128)(2,1)}, bf16[2,2,128,3072]{3,2,1,0:T(8,128)(2,1)}, u32[]{:S(2)}, u32[]{:S(2)}) collective-permute-start(bf16[2,2,128,3072]{3,2,1,0:T(8,128)(2,1)} %param.17), channel_id=1, source_target_pairs={{0,48},{8,56},{16,0},{24,8},{32,16},{40,24},{48,32},{56,40},{64,11... | collective-permute-start | bytes 9437192 | tf_op jit(solution)/shard_map/ppermute | solution.py:28
  26.9 37.6 %collective-permute-start.6 = (bf16[2,2,128,3072]{3,2,1,0:T(8,128)(2,1)}, bf16[2,2,128,3072]{3,2,1,0:T(8,128)(2,1)}, u32[]{:S(2)}, u32[]{:S(2)}) collective-permute-start(bf16[2,2,128,3072]{3,2,1,0:T(8,128)(2,1)} %param.17), channel_id=1, source_target_pairs={{0,8},{16,24},{32,40},{48,56},{64,72},{80,88},{96,104},{112,120},{... | collective-permute-start | bytes 9437192 | tf_op jit(solution)/shard_map/ppermute | solution.py:35
  30.1 74.0 %collective-permute-start.9 = (bf16[2,2,128,3072]{3,2,1,0:T(8,128)(2,1)}, bf16[2,2,128,3072]{3,2,1,0:T(8,128)(2,1)}, u32[]{:S(2)}, u32[]{:S(2)}) collective-permute-start(bf16[2,2,128,3072]{3,2,1,0:T(8,128)(2,1)} %param.17), channel_id=1, source_target_pairs={{0,1},{1,2},{2,3},{3,4},{4,5},{5,6},{6,7},{8,9},{9,10},{10,11},{11... | collective-permute-start | bytes 9437192 | tf_op jit(solution)/shard_map/ppermute | solution.py:104
  32.5 73.6 %collective-permute-start.10 = (bf16[2,2,128,3072]{3,2,1,0:T(8,128)(2,1)}, bf16[2,2,128,3072]{3,2,1,0:T(8,128)(2,1)}, u32[]{:S(2)}, u32[]{:S(2)}) collective-permute-start(bf16[2,2,128,3072]{3,2,1,0:T(8,128)(2,1)} %param.17), channel_id=1, source_target_pairs={{1,0},{2,1},{3,2},{4,3},{5,4},{6,5},{7,6},{9,8},{10,9},{11,10},{12... | collective-permute-start | bytes 9437192 | tf_op jit(solution)/shard_map/ppermute | solution.py:104
  42.1 7.8 %copy-start.6 = (f32[1536]{0:T(1024)S(1)}, f32[1536]{0:T(1024)}, u32[]{:S(2)}) copy-start(f32[1536]{0:T(1024)} %param.14) | copy-start | bytes 18436
  47.3 2.8 %copy-start.5 = (f32[1536]{0:T(1024)S(1)}, f32[1536]{0:T(1024)}, u32[]{:S(2)}) copy-start(f32[1536]{0:T(1024)} %param.15) | copy-start | bytes 18436
  94.8 90.6 %slice-start = ((s8[4718592]{0:T(1024)(128)(4,1)}), s8[4194304]{0:T(1024)(128)(4,1)S(1)}, s32[]{:S(2)}) async-start(s8[4718592]{0:T(1024)(128)(4,1)} %bitcast.31), calls=%async_computation | async-start | bytes 8388608
  97.1 10.2 %collective-permute-start.11 = (bf16[2,2,128,3072]{3,2,1,0:T(8,128)(2,1)S(1)}, bf16[2,2,128,3072]{3,2,1,0:T(8,128)(2,1)S(1)}, u32[]{:S(2)}, u32[]{:S(2)}) collective-permute-start(bf16[2,2,128,3072]{3,2,1,0:T(8,128)(2,1)S(1)} %broadcast_select_fusion), channel_id=1, source_target_pairs={{0,8},{16,24},{32,40},{48,56},{64,72},{80,88},{96,104},{112,120},{... | collective-permute-start | bytes 9437192 | tf_op jit(solution)/shard_map/ppermute | solution.py:57
  100.0 41.3 %collective-permute-start.8 = (bf16[2,2,128,1536]{3,2,1,0:T(8,128)(2,1)}, bf16[2,2,128,1536]{3,2,1,0:T(8,128)(2,1)}, u32[]{:S(2)}, u32[]{:S(2)}) collective-permute-start(bf16[2,2,128,1536]{3,2,1,0:T(8,128)(2,1)} %get-tuple-element.49), channel_id=1, source_target_pairs={{0,64},{8,72},{16,80},{24,88},{96,32},{104,40},{112,48},{120,56},{... | collective-permute-start | bytes 4718600 | tf_op jit(solution)/shard_map/ppermute | solution.py:55
  101.4 47.8 %collective-permute-start.14 = (bf16[2,2,128,1536]{3,2,1,0:T(8,128)(2,1)}, bf16[2,2,128,1536]{3,2,1,0:T(8,128)(2,1)}, u32[]{:S(2)}, u32[]{:S(2)}) collective-permute-start(bf16[2,2,128,1536]{3,2,1,0:T(8,128)(2,1)} %get-tuple-element.59), channel_id=1, source_target_pairs={{0,16},{8,24},{16,32},{24,40},{32,48},{40,56},{48,0},{56,8},{64,80... | collective-permute-start | bytes 4718600 | tf_op jit(solution)/shard_map/ppermute | solution.py:53
  104.1 45.1 %collective-permute-start.15 = (bf16[2,2,128,1536]{3,2,1,0:T(8,128)(2,1)}, bf16[2,2,128,1536]{3,2,1,0:T(8,128)(2,1)}, u32[]{:S(2)}, u32[]{:S(2)}) collective-permute-start(bf16[2,2,128,1536]{3,2,1,0:T(8,128)(2,1)} %get-tuple-element.60), channel_id=1, source_target_pairs={{0,48},{8,56},{16,0},{24,8},{32,16},{40,24},{48,32},{56,40},{64,11... | collective-permute-start | bytes 4718600 | tf_op jit(solution)/shard_map/ppermute | solution.py:54
  106.0 69.0 %collective-permute-start.7 = (bf16[2,2,128,1536]{3,2,1,0:T(8,128)(2,1)S(1)}, bf16[2,2,128,1536]{3,2,1,0:T(8,128)(2,1)}, u32[]{:S(2)}, u32[]{:S(2)}) collective-permute-start(bf16[2,2,128,1536]{3,2,1,0:T(8,128)(2,1)S(1)} %get-tuple-element.48), channel_id=1, source_target_pairs={{0,64},{8,72},{16,80},{24,88},{96,32},{104,40},{112,48},{120,56},{... | collective-permute-start | bytes 4718600 | tf_op jit(solution)/shard_map/ppermute | solution.py:56
  109.0 76.3 %slice-start.1 = ((s8[4718592]{0:T(1024)(128)(4,1)}), s8[524288]{0:T(1024)(128)(4,1)S(1)}, s32[]{:S(2)}) async-start(s8[4718592]{0:T(1024)(128)(4,1)} %bitcast.31), calls=%async_computation.1 | async-start | bytes 1048576
  141.3 35.1 %collective-permute-start.12 = (bf16[2,2,128,1536]{3,2,1,0:T(8,128)(2,1)}, bf16[2,2,128,1536]{3,2,1,0:T(8,128)(2,1)}, u32[]{:S(2)}, u32[]{:S(2)}) collective-permute-start(bf16[2,2,128,1536]{3,2,1,0:T(8,128)(2,1)} %collective-permute-done.8), channel_id=1, source_target_pairs={{64,80},{72,88},{80,64},{88,72},{32,48},{40,56},{48,32},{56,40},{6... | collective-permute-start | bytes 4718600 | tf_op jit(solution)/shard_map/ppermute | solution.py:63
  143.2 33.2 %collective-permute-start.13 = (bf16[2,2,128,1536]{3,2,1,0:T(8,128)(2,1)}, bf16[2,2,128,1536]{3,2,1,0:T(8,128)(2,1)}, u32[]{:S(2)}, u32[]{:S(2)}) collective-permute-start(bf16[2,2,128,1536]{3,2,1,0:T(8,128)(2,1)} %collective-permute-done.8), channel_id=1, source_target_pairs={{72,64},{48,56},{73,65},{49,57},{74,66},{50,58},{75,67},{51,59},{7... | collective-permute-start | bytes 4718600 | tf_op jit(solution)/shard_map/ppermute | solution.py:63
  176.4 11.0 %collective-permute-start.17 = (bf16[2,2,128,1536]{3,2,1,0:T(8,128)(2,1)}, bf16[2,2,128,1536]{3,2,1,0:T(8,128)(2,1)}, u32[]{:S(2)}, u32[]{:S(2)}) collective-permute-start(bf16[2,2,128,1536]{3,2,1,0:T(8,128)(2,1)} %collective-permute-done.7), channel_id=1, source_target_pairs={{72,64},{48,56},{73,65},{49,57},{74,66},{50,58},{75,67},{51,59},{7... | collective-permute-start | bytes 4718600 | tf_op jit(solution)/shard_map/ppermute | solution.py:63
  183.4 36.9 %collective-permute-start.16 = (bf16[2,2,128,1536]{3,2,1,0:T(8,128)(2,1)}, bf16[2,2,128,1536]{3,2,1,0:T(8,128)(2,1)S(1)}, u32[]{:S(2)}, u32[]{:S(2)}) collective-permute-start(bf16[2,2,128,1536]{3,2,1,0:T(8,128)(2,1)} %collective-permute-done.7), channel_id=1, source_target_pairs={{64,80},{72,88},{80,64},{88,72},{32,48},{40,56},{48,32},{56,40},{6... | collective-permute-start | bytes 4718600 | tf_op jit(solution)/shard_map/ppermute | solution.py:63
  221.5 10.1 %copy-start.1 = (bf16[1728,256]{1,0:T(8,128)(2,1)S(1)}, bf16[1728,256]{1,0:T(8,128)(2,1)}, u32[]{:S(2)}) copy-start(bf16[1728,256]{1,0:T(8,128)(2,1)} %param.12) | copy-start | bytes 2654212
  (3 other events, 5.7 us)

commit v3 on v2

--- a/solution.py
+++ b/solution.py
@@ -41,19 +41,17 @@
     half = below.shape[-1] // 2
     from_below = (frame_idx < 2) | (frame_idx == 12) | (frame_idx == 13)
     odd = frame_idx % 2 == 1
-    parts = (
-        below[..., :half],
-        above[..., half:],
-        jnp.where(from_below, below[..., :half], above[..., :half]),
-        jnp.where(from_below, below[..., half:], above[..., half:]),
-    )
+    edge_keys = jnp.where(from_below, below[..., :half], above[..., :half])
+    edge_keys, below, above = lax.optimization_barrier((edge_keys, below, above))
+    edge_values = jnp.where(from_below, below[..., half:], above[..., half:])
+    parts = (edge_values, below[..., :half], above[..., half:])
     parts, below, above = lax.optimization_barrier((parts, below, above))
-    below_keys, above_values, edge_keys, edge_values = parts
+    edge_values, below_keys, above_values = parts
     over = [(0, 8), (1, 9), (2, 10), (3, 11), (12, 4), (13, 5), (14, 6), (15, 7)]
+    cross_keys = lax.ppermute(edge_keys, "tm", over)
+    cross_values = lax.ppermute(edge_values, "tm", over)
     far_keys = lax.ppermute(below_keys, "tm", [(i, around(i, 2)) for i in everyone])
     far_values = lax.ppermute(above_values, "tm", [(i, around(i, -2)) for i in everyone])
-    cross_keys = lax.ppermute(edge_keys, "tm", over)
-    cross_values = lax.ppermute(edge_values, "tm", over)
     beside = lax.ppermute(jnp.where(odd, below, above), "tm", swap(0) + swap(1))
     return far_keys, far_values, cross_keys, cross_values, beside
 

time: 233 us -> 266 us (1.14)
  waiting for transfers between devices: 62.9 us -> 92.3 us
    ppermute x1, waiting for transfers between devices: 6.68 us -> 37.8 us  [second(): cross_keys = lax.ppermute(edge_keys, 'tm', over)]
    ppermute x2, waiting for transfers between devices: 25.2 us -> 44 us  [third(): lax.ppermute(cross, 'tm', trade)]
    ppermute x1, waiting for transfers between devices: 18.8 us -> 0.01 us  [second(): cross_values = lax.ppermute(edge_values, 'tm', over)]
    ppermute x1, waiting for transfers between devices: 7.51 us -> 0.01 us  [ring_sides(): below = lax.ppermute(kv, 'tm', [(i, around(i, 2)) for i in everyone])]
    ppermute x2, waiting for transfers between devices: 1.94 us -> 6.97 us  [from_behind(): return lax.ppermute(block, axis, route)]
    ppermute x1, starting transfers between devices: 3.17 us -> 7.63 us  [nearest(): mate = lax.ppermute(kv, 'tm', swap(0) + swap(1))]
    slice x0 -> x1, other arithmetic: none -> 4.41 us  [second(): edge_values = jnp.where(from_below, below[..., half:], above[..., half:])]
    ppermute x2, starting transfers between devices: 13 us -> 8.78 us  [third(): lax.ppermute(cross, 'tm', [(9, 8), (6, 7)])]
  transfers between devices with their start and end apart: 18 -> 18, of which waited for: 8 -> 7; matrix products, arithmetic and copies ran while one was open for 18% -> 17% of each run, Pallas kernels for 25% -> 22%
where the time goes in v3:
time: 266 us; the launch traced here: 263 us
  waiting for transfers between devices  92.3 us (35%)
  Pallas kernels  67.1 us (25%)
  starting transfers between devices  52.6 us (20%)
  matrix products  19.7 us (7%)
  local copies, waits for them, and re-layouts  15.3 us (6%)
  other arithmetic  15.3 us (6%)
    pallas_call x5, Pallas kernels, attend(): pl.pallas_call(functools.partial(attend_kernel, ids, first, last), grid=(...  67.1 us
    ppermute x2, waiting for transfers between devices, third(): lax.ppermute(cross, 'tm', trade)  44 us
    ppermute x1, waiting for transfers between devices, second(): cross_keys = lax.ppermute(edge_keys, 'tm', over)  37.8 us
    dot_general x1, matrix products, body(): jnp.dot(normed, w_qkv, preferred_element_type=jnp.float32)  14.4 us
    ppermute x2, starting transfers between devices, third(): lax.ppermute(cross, 'tm', [(9, 8), (6, 7)])  8.78 us
    ppermute x1, starting transfers between devices, nearest(): mate = lax.ppermute(kv, 'tm', swap(0) + swap(1))  7.63 us
    ppermute x2, starting transfers between devices, with_halo(): lax.ppermute(head, axis, [((i + 1) % count, i) for i in range(ends)])  7.57 us
    ppermute x2, starting transfers between devices, from_behind(): return lax.ppermute(block, axis, route)  7.39 us
  transfers between devices with their start and end apart: 18, of which 7 were waited for; matrix products, arithmetic and copies ran while one was open for 17% of the time, Pallas kernels for 22%

profile of v3, /device:TPU:25, one launch (start us, length us, event | category | flops | bytes accessed | tf_op | source)
XLA Modules:
  0.0 263.0 jit_solution(14290699193640105986)
XLA Ops:
  1.6 2.6 collective-permute-start.1
  4.1 3.0 %collective-permute-start = (bf16[1,2,8192]{2,1,0:T(2,128)(2,1)S(1)}, bf16[1,2,8192]{2,1,0:T(2,128)(2,1)S(1)}, u32[]{:S(2)}, u32[]{:S(2)}) collective-permute-start(bf16[1,2,8192]{2,1,0:T(2,128)(2,1)S(1)} %get-tuple-element.112), channel_id=1, source_target_pairs={{0,8},{8,16},{16,24},{24,32},{32,40},{40,48},{48,56},{56,64},{64,7... | collective-permute-start | bytes 98312 | tf_op jit(solution)/shard_map/ppermute | solution.py:90
  10.8 5.0 %collective-permute-start.3 = (bf16[4,1,8192]{2,1,0:T(2,128)(2,1)S(1)}, bf16[4,1,8192]{2,1,0:T(2,128)(2,1)S(1)}, u32[]{:S(2)}, u32[]{:S(2)}) collective-permute-start(bf16[4,1,8192]{2,1,0:T(2,128)(2,1)S(1)} %get-tuple-element.111), channel_id=1, source_target_pairs={{1,0},{2,1},{3,2},{4,3},{5,4},{6,5},{7,6},{9,8},{10,9},{11,10},{12... | collective-permute-start | bytes 196616 | tf_op jit(solution)/shard_map/ppermute | solution.py:92
  21.0 2.6 %collective-permute-done.2 = bf16[4,1,8192]{2,1,0:T(2,128)(2,1)S(1)} collective-permute-done((bf16[4,1,8192]{2,1,0:T(2,128)(2,1)S(1)}, bf16[4,1,8192]{2,1,0:T(2,128)(2,1)S(1)}, u32[]{:S(2)}, u32[]{:S(2)}) %collective-permute-start.2) | collective-permute-done | bytes 65568 | tf_op jit(solution)/shard_map/ppermute | solution.py:90
  27.6 7.6 %collective-permute-start.6 = (bf16[2,2,128,3072]{3,2,1,0:T(8,128)(2,1)}, bf16[2,2,128,3072]{3,2,1,0:T(8,128)(2,1)}, u32[]{:S(2)}, u32[]{:S(2)}) collective-permute-start(bf16[2,2,128,3072]{3,2,1,0:T(8,128)(2,1)} %param.17), channel_id=1, source_target_pairs={{0,8},{16,24},{32,40},{48,56},{64,72},{80,88},{96,104},{112,120},{... | collective-permute-start | bytes 9437192 | tf_op jit(solution)/shard_map/ppermute | solution.py:35
  37.2 5.5 %collective-permute-start.10 = (bf16[2,2,128,3072]{3,2,1,0:T(8,128)(2,1)}, bf16[2,2,128,3072]{3,2,1,0:T(8,128)(2,1)}, u32[]{:S(2)}, u32[]{:S(2)}) collective-permute-start(bf16[2,2,128,3072]{3,2,1,0:T(8,128)(2,1)} %param.17), channel_id=1, source_target_pairs={{1,0},{2,1},{3,2},{4,3},{5,4},{6,5},{7,6},{9,8},{10,9},{11,10},{12... | collective-permute-start | bytes 9437192 | tf_op jit(solution)/shard_map/ppermute | solution.py:102
  42.7 4.5 %concatenate.11 = bf16[2,2,128,1728]{3,2,1,0:T(8,128)(2,1)S(1)} concatenate(bf16[2,2,128,64]{3,2,1,0:T(8,128)(2,1)} %get-tuple-element.109, bf16[2,2,128,64]{3,2,1,0:T(8,128)(2,1)} %get-tuple-element.108, bf16[2,2,128,64]{3,2,1,0:T(8,128)(2,1)} %get-tuple-element.84, bf16[2,2,128,64]{3,2,1,0:T(8,128)(2,1)} %get-tuple-element.85, bf16[2,2,128,64]{3,2,1,0:T(8,128)(2,1)} %get-tuple-element.107, ...), dimensions={3} | concatenate | bytes 3538944 | tf_op jit(solution)/shard_map/concatenate | solution.py:282
  47.2 5.2 %fusion.15 = (f32[512]{0:T(512)S(1)}, f32[512,1536]{1,0:T(8,128)}) fusion(bf16[256,1536]{1,0:T(8,128)(2,1)} %param.13, bf16[512,1536]{1,0:T(8,128)(2,1)} %bitcast.36, bf16[512,1728]{1,0:T(8,128)(2,1)S(1)} %bitcast.34, bf16[1728,256]{1,0:T(8,128)(2,1)S(1)} %copy-done), kind=kOutput, calls=%fused_computation.65 | convolution fusion | flops 858652160 | bytes 8161280 | tf_op jit(solution)/shard_map/dot_general | solution.py:285
  55.3 14.4 %convolution_convert_fusion = bf16[512,4608]{1,0:T(8,128)(2,1)} fusion(bf16[1536,4608]{1,0:T(8,128)(2,1)} %param.16, f32[512,1536]{1,0:T(8,128)S(1)} %copy-done.2, f32[1536]{0:T(1024)S(1)} %copy-done.5, f32[1536]{0:T(1024)S(1)} %copy-done.6, f32[512]{0:T(512)S(1)} %add_rsqrt_fusion, f32[512]{0:T(512)S(1)} %broadcast_multiply_fusion), kind=kOutput, calls=%fused_computation | convolution fusion | flops 7254048768 | bytes 22036480 | tf_op jit(solution)/shard_map/dot_general | solution.py:291
  69.7 16.7 %shard_map.113 = (f32[4,12,128,128]{3,2,1,0:T(8,128)}, f32[4,12,128]{2,1,0:T(8,128)}, f32[4,12,128]{2,1,0:T(8,128)}) custom-call(s32[32]{0:T(128)} %fusion.6.refs_0_, bf16[4,128,4608]{2,1,0:T(8,128)(2,1)} %bitcast.26, bf16[4,128,3072]{2,1,0:T(8,128)(2,1)} %bitcast.4.refs_2_, bf16[4,128,3072]{2,1,0:T(8,128)(2,1)} %bitcast.5.refs_3_), custom_call_target="tpu_custom_call" | custom-call | flops 20000000000 | bytes 60000000 | tf_op jit(solution)/shard_map/pallas_call | solution.py:237
  86.4 3.2 %slice_select_fusion.1 = bf16[2,2,128,1536]{3,2,1,0:T(8,128)(2,1)} fusion(bf16[2,2,128,3072]{3,2,1,0:T(8,128)(2,1)} %collective-permute-done.5, bf16[2,2,128,3072]{3,2,1,0:T(8,128)(2,1)} %collective-permute-done.4, pred[]{:T(512)S(6)} %or.7), kind=kLoop, calls=%fused_computation.6 | loop fusion | flops 786432 | bytes 4718593 | tf_op jit(solution)/shard_map/jit(_where)/select_n | solution.py:44
  89.6 4.4 %fusion.11 = (bf16[2,2,128,1536]{3,2,1,0:T(8,128)(2,1)}, bf16[2,2,128,1536]{3,2,1,0:T(8,128)(2,1)S(1)}, bf16[2,2,128,1536]{3,2,1,0:T(8,128)(2,1)}) fusion(bf16[2,2,128,3072]{3,2,1,0:T(8,128)(2,1)} %collective-permute-done.5, bf16[2,2,128,3072]{3,2,1,0:T(8,128)(2,1)} %collective-permute-done.4, pred[]{:T(512)S(6)} %or.7), kind=kLoop, calls=%fused_computation.61 | loop fusion | flops 786432 | bytes 9437185 | tf_op jit(solution)/shard_map/slice | solution.py:46
  96.4 4.0 %collective-permute-start.11 = (bf16[2,2,128,3072]{3,2,1,0:T(8,128)(2,1)S(1)}, bf16[2,2,128,3072]{3,2,1,0:T(8,128)(2,1)S(1)}, u32[]{:S(2)}, u32[]{:S(2)}) collective-permute-start(bf16[2,2,128,3072]{3,2,1,0:T(8,128)(2,1)S(1)} %broadcast_select_fusion), channel_id=1, source_target_pairs={{0,8},{16,24},{32,40},{48,56},{64,72},{80,88},{96,104},{112,120},{... | collective-permute-start | bytes 9437192 | tf_op jit(solution)/shard_map/ppermute | solution.py:55
  103.2 6.1 %collective-permute-done.9 = bf16[2,2,128,3072]{3,2,1,0:T(8,128)(2,1)} collective-permute-done((bf16[2,2,128,3072]{3,2,1,0:T(8,128)(2,1)}, bf16[2,2,128,3072]{3,2,1,0:T(8,128)(2,1)}, u32[]{:S(2)}, u32[]{:S(2)}) %collective-permute-start.9) | collective-permute-done | bytes 3145760 | tf_op jit(solution)/shard_map/ppermute | solution.py:102
  113.7 22.4 %shard_map.114 = (f32[4,12,128,128]{3,2,1,0:T(8,128)}, f32[4,12,128]{2,1,0:T(8,128)}, f32[4,12,128]{2,1,0:T(8,128)}) custom-call(s32[32]{0:T(128)} %fusion.6.refs_0_, bf16[4,128,4608]{2,1,0:T(8,128)(2,1)} %bitcast.27, bf16[4,128,3072]{2,1,0:T(8,128)(2,1)} %bitcast.6.refs_2_, bf16[4,128,3072]{2,1,0:T(8,128)(2,1)} %bitcast.7.refs_3_, ...), custom_call_target="tpu_custom_call" | custom-call | flops 30000001024 | bytes 90000000 | tf_op jit(solution)/shard_map/pallas_call | solution.py:237
  136.1 37.8 %collective-permute-done.8 = bf16[2,2,128,1536]{3,2,1,0:T(8,128)(2,1)} collective-permute-done((bf16[2,2,128,1536]{3,2,1,0:T(8,128)(2,1)}, bf16[2,2,128,1536]{3,2,1,0:T(8,128)(2,1)}, u32[]{:S(2)}, u32[]{:S(2)}) %collective-permute-start.8) | collective-permute-done | bytes 1572896 | tf_op jit(solution)/shard_map/ppermute | solution.py:51
  173.9 3.1 %collective-permute-start.12 = (bf16[2,2,128,1536]{3,2,1,0:T(8,128)(2,1)}, bf16[2,2,128,1536]{3,2,1,0:T(8,128)(2,1)}, u32[]{:S(2)}, u32[]{:S(2)}) collective-permute-start(bf16[2,2,128,1536]{3,2,1,0:T(8,128)(2,1)} %collective-permute-done.8), channel_id=1, source_target_pairs={{64,80},{72,88},{80,64},{88,72},{32,48},{40,56},{48,32},{56,40},{6... | collective-permute-start | bytes 4718600 | tf_op jit(solution)/shard_map/ppermute | solution.py:61
  176.9 4.1 %collective-permute-start.13 = (bf16[2,2,128,1536]{3,2,1,0:T(8,128)(2,1)}, bf16[2,2,128,1536]{3,2,1,0:T(8,128)(2,1)}, u32[]{:S(2)}, u32[]{:S(2)}) collective-permute-start(bf16[2,2,128,1536]{3,2,1,0:T(8,128)(2,1)} %collective-permute-done.8), channel_id=1, source_target_pairs={{72,64},{48,56},{73,65},{49,57},{74,66},{50,58},{75,67},{51,59},{7... | collective-permute-start | bytes 4718600 | tf_op jit(solution)/shard_map/ppermute | solution.py:61
  181.1 8.0 %shard_map.115 = (f32[4,12,128,128]{3,2,1,0:T(8,128)}, f32[4,12,128]{2,1,0:T(8,128)}, f32[4,12,128]{2,1,0:T(8,128)}) custom-call(s32[32]{0:T(128)} %fusion.6.refs_0_, bf16[4,128,4608]{2,1,0:T(8,128)(2,1)} %bitcast.28, bf16[4,128,1536]{2,1,0:T(8,128)(2,1)} %bitcast.11.refs_2_, bf16[4,128,1536]{2,1,0:T(8,128)(2,1)} %bitcast.12.refs_3_, ...), custom_call_target="tpu_custom_call" | custom-call | flops 15000000512 | bytes 45000000 | tf_op jit(solution)/shard_map/pallas_call | solution.py:237
  189.0 22.3 %collective-permute-done.12 = bf16[2,2,128,1536]{3,2,1,0:T(8,128)(2,1)} collective-permute-done((bf16[2,2,128,1536]{3,2,1,0:T(8,128)(2,1)}, bf16[2,2,128,1536]{3,2,1,0:T(8,128)(2,1)}, u32[]{:S(2)}, u32[]{:S(2)}) %collective-permute-start.12) | collective-permute-done | bytes 1572896 | tf_op jit(solution)/shard_map/ppermute | solution.py:61
  211.3 4.7 %collective-permute-start.17 = (bf16[2,2,128,1536]{3,2,1,0:T(8,128)(2,1)}, bf16[2,2,128,1536]{3,2,1,0:T(8,128)(2,1)}, u32[]{:S(2)}, u32[]{:S(2)}) collective-permute-start(bf16[2,2,128,1536]{3,2,1,0:T(8,128)(2,1)} %collective-permute-done.7), channel_id=1, source_target_pairs={{72,64},{48,56},{73,65},{49,57},{74,66},{50,58},{75,67},{51,59},{7... | collective-permute-start | bytes 4718600 | tf_op jit(solution)/shard_map/ppermute | solution.py:61
  220.0 11.1 %shard_map.116 = (f32[4,12,128,128]{3,2,1,0:T(8,128)}, f32[4,12,128]{2,1,0:T(8,128)}, f32[4,12,128]{2,1,0:T(8,128)}) custom-call(s32[32]{0:T(128)} %fusion.6.refs_0_, bf16[4,128,4608]{2,1,0:T(8,128)(2,1)} %bitcast.29, bf16[4,128,1536]{2,1,0:T(8,128)(2,1)} %bitcast.15.refs_2_, bf16[4,128,1536]{2,1,0:T(8,128)(2,1)} %bitcast.16.refs_3_, ...), custom_call_target="tpu_custom_call" | custom-call | flops 12000000000 | bytes 36000000 | tf_op jit(solution)/shard_map/pallas_call | solution.py:237
  231.1 21.7 %collective-permute-done.16 = bf16[2,2,128,1536]{3,2,1,0:T(8,128)(2,1)S(1)} collective-permute-done((bf16[2,2,128,1536]{3,2,1,0:T(8,128)(2,1)}, bf16[2,2,128,1536]{3,2,1,0:T(8,128)(2,1)S(1)}, u32[]{:S(2)}, u32[]{:S(2)}) %collective-permute-start.16) | collective-permute-done | bytes 1572896 | tf_op jit(solution)/shard_map/ppermute | solution.py:61
  254.1 8.9 %shard_map.117 = bf16[4,128,1536]{2,1,0:T(8,128)(2,1)} custom-call(s32[32]{0:T(128)} %fusion.6.refs_0_, bf16[4,128,4608]{2,1,0:T(8,128)(2,1)} %bitcast.30, bf16[4,128,1536]{2,1,0:T(8,128)(2,1)} %bitcast.13.refs_2_, bf16[4,128,1536]{2,1,0:T(8,128)(2,1)} %bitcast.37, f32[4,12,128,128]{3,2,1,0:T(8,128)} %get-tuple-element.77.refs_4_, ...), custom_call_target="tpu_custom_call" | custom-call | flops 8000000000 | bytes 24000000 | tf_op jit(solution)/shard_map/pallas_call | solution.py:237
  (58 shorter events, 33.2 us)
Async XLA Ops:
  0.6 46.6 %copy-start = (bf16[1728,256]{1,0:T(8,128)(2,1)S(1)}, bf16[1728,256]{1,0:T(8,128)(2,1)}, u32[]{:S(2)}) copy-start(bf16[1728,256]{1,0:T(8,128)(2,1)} %param.12) | copy-start | bytes 2654212
  1.6 7.2 %collective-permute-start.1 = (bf16[1,2,8192]{2,1,0:T(2,128)(2,1)S(1)}, bf16[1,2,8192]{2,1,0:T(2,128)(2,1)S(1)}, u32[]{:S(2)}, u32[]{:S(2)}) collective-permute-start(bf16[1,2,8192]{2,1,0:T(2,128)(2,1)S(1)} %get-tuple-element.113), channel_id=1, source_target_pairs={{8,0},{16,8},{24,16},{32,24},{40,32},{48,40},{56,48},{64,56},{72,6... | collective-permute-start | bytes 98312 | tf_op jit(solution)/shard_map/ppermute | solution.py:92
  4.1 5.5 %collective-permute-start = (bf16[1,2,8192]{2,1,0:T(2,128)(2,1)S(1)}, bf16[1,2,8192]{2,1,0:T(2,128)(2,1)S(1)}, u32[]{:S(2)}, u32[]{:S(2)}) collective-permute-start(bf16[1,2,8192]{2,1,0:T(2,128)(2,1)S(1)} %get-tuple-element.112), channel_id=1, source_target_pairs={{0,8},{8,16},{16,24},{24,32},{32,40},{40,48},{48,56},{56,64},{64,7... | collective-permute-start | bytes 98312 | tf_op jit(solution)/shard_map/ppermute | solution.py:90
  10.8 10.2 %collective-permute-start.3 = (bf16[4,1,8192]{2,1,0:T(2,128)(2,1)S(1)}, bf16[4,1,8192]{2,1,0:T(2,128)(2,1)S(1)}, u32[]{:S(2)}, u32[]{:S(2)}) collective-permute-start(bf16[4,1,8192]{2,1,0:T(2,128)(2,1)S(1)} %get-tuple-element.111), channel_id=1, source_target_pairs={{1,0},{2,1},{3,2},{4,3},{5,4},{6,5},{7,6},{9,8},{10,9},{11,10},{12... | collective-permute-start | bytes 196616 | tf_op jit(solution)/shard_map/ppermute | solution.py:92
  15.8 7.8 %collective-permute-start.2 = (bf16[4,1,8192]{2,1,0:T(2,128)(2,1)S(1)}, bf16[4,1,8192]{2,1,0:T(2,128)(2,1)S(1)}, u32[]{:S(2)}, u32[]{:S(2)}) collective-permute-start(bf16[4,1,8192]{2,1,0:T(2,128)(2,1)S(1)} %get-tuple-element.110), channel_id=1, source_target_pairs={{0,1},{1,2},{2,3},{3,4},{4,5},{5,6},{6,7},{8,9},{9,10},{10,11},{11... | collective-permute-start | bytes 196616 | tf_op jit(solution)/shard_map/ppermute | solution.py:90
  18.3 68.1 %collective-permute-start.4 = (bf16[2,2,128,3072]{3,2,1,0:T(8,128)(2,1)}, bf16[2,2,128,3072]{3,2,1,0:T(8,128)(2,1)}, u32[]{:S(2)}, u32[]{:S(2)}) collective-permute-start(bf16[2,2,128,3072]{3,2,1,0:T(8,128)(2,1)} %param.17), channel_id=1, source_target_pairs={{0,16},{8,24},{16,32},{24,40},{32,48},{40,56},{48,0},{56,8},{64,80... | collective-permute-start | bytes 9437192 | tf_op jit(solution)/shard_map/ppermute | solution.py:27
  19.6 66.9 %collective-permute-start.5 = (bf16[2,2,128,3072]{3,2,1,0:T(8,128)(2,1)}, bf16[2,2,128,3072]{3,2,1,0:T(8,128)(2,1)}, u32[]{:S(2)}, u32[]{:S(2)}) collective-permute-start(bf16[2,2,128,3072]{3,2,1,0:T(8,128)(2,1)} %param.17), channel_id=1, source_target_pairs={{0,48},{8,56},{16,0},{24,8},{32,16},{40,24},{48,32},{56,40},{64,11... | collective-permute-start | bytes 9437192 | tf_op jit(solution)/shard_map/ppermute | solution.py:28
  27.6 42.1 %collective-permute-start.6 = (bf16[2,2,128,3072]{3,2,1,0:T(8,128)(2,1)}, bf16[2,2,128,3072]{3,2,1,0:T(8,128)(2,1)}, u32[]{:S(2)}, u32[]{:S(2)}) collective-permute-start(bf16[2,2,128,3072]{3,2,1,0:T(8,128)(2,1)} %param.17), channel_id=1, source_target_pairs={{0,8},{16,24},{32,40},{48,56},{64,72},{80,88},{96,104},{112,120},{... | collective-permute-start | bytes 9437192 | tf_op jit(solution)/shard_map/ppermute | solution.py:35
  35.3 74.0 %collective-permute-start.9 = (bf16[2,2,128,3072]{3,2,1,0:T(8,128)(2,1)}, bf16[2,2,128,3072]{3,2,1,0:T(8,128)(2,1)}, u32[]{:S(2)}, u32[]{:S(2)}) collective-permute-start(bf16[2,2,128,3072]{3,2,1,0:T(8,128)(2,1)} %param.17), channel_id=1, source_target_pairs={{0,1},{1,2},{2,3},{3,4},{4,5},{5,6},{6,7},{8,9},{9,10},{10,11},{11... | collective-permute-start | bytes 9437192 | tf_op jit(solution)/shard_map/ppermute | solution.py:102
  37.2 73.0 %collective-permute-start.10 = (bf16[2,2,128,3072]{3,2,1,0:T(8,128)(2,1)}, bf16[2,2,128,3072]{3,2,1,0:T(8,128)(2,1)}, u32[]{:S(2)}, u32[]{:S(2)}) collective-permute-start(bf16[2,2,128,3072]{3,2,1,0:T(8,128)(2,1)} %param.17), channel_id=1, source_target_pairs={{1,0},{2,1},{3,2},{4,3},{5,4},{6,5},{7,6},{9,8},{10,9},{11,10},{12... | collective-permute-start | bytes 9437192 | tf_op jit(solution)/shard_map/ppermute | solution.py:102
  47.2 7.8 %copy-start.6 = (f32[1536]{0:T(1024)S(1)}, f32[1536]{0:T(1024)}, u32[]{:S(2)}) copy-start(f32[1536]{0:T(1024)} %param.14) | copy-start | bytes 18436
  52.5 2.8 %copy-start.5 = (f32[1536]{0:T(1024)S(1)}, f32[1536]{0:T(1024)}, u32[]{:S(2)}) copy-start(f32[1536]{0:T(1024)} %param.15) | copy-start | bytes 18436
  94.0 123.8 %slice-start = ((s8[4718592]{0:T(1024)(128)(4,1)}), s8[4194304]{0:T(1024)(128)(4,1)S(1)}, s32[]{:S(2)}) async-start(s8[4718592]{0:T(1024)(128)(4,1)} %bitcast.31), calls=%async_computation | async-start | bytes 8388608
  96.4 15.6 %collective-permute-start.11 = (bf16[2,2,128,3072]{3,2,1,0:T(8,128)(2,1)S(1)}, bf16[2,2,128,3072]{3,2,1,0:T(8,128)(2,1)S(1)}, u32[]{:S(2)}, u32[]{:S(2)}) collective-permute-start(bf16[2,2,128,3072]{3,2,1,0:T(8,128)(2,1)S(1)} %broadcast_select_fusion), channel_id=1, source_target_pairs={{0,8},{16,24},{32,40},{48,56},{64,72},{80,88},{96,104},{112,120},{... | collective-permute-start | bytes 9437192 | tf_op jit(solution)/shard_map/ppermute | solution.py:55
  100.4 88.6 %collective-permute-start.7 = (bf16[2,2,128,1536]{3,2,1,0:T(8,128)(2,1)S(1)}, bf16[2,2,128,1536]{3,2,1,0:T(8,128)(2,1)}, u32[]{:S(2)}, u32[]{:S(2)}) collective-permute-start(bf16[2,2,128,1536]{3,2,1,0:T(8,128)(2,1)S(1)} %get-tuple-element.52), channel_id=1, source_target_pairs={{0,64},{8,72},{16,80},{24,88},{96,32},{104,40},{112,48},{120,56},{... | collective-permute-start | bytes 4718600 | tf_op jit(solution)/shard_map/ppermute | solution.py:52
  101.9 71.9 %collective-permute-start.8 = (bf16[2,2,128,1536]{3,2,1,0:T(8,128)(2,1)}, bf16[2,2,128,1536]{3,2,1,0:T(8,128)(2,1)}, u32[]{:S(2)}, u32[]{:S(2)}) collective-permute-start(bf16[2,2,128,1536]{3,2,1,0:T(8,128)(2,1)} %slice_select_fusion.1), channel_id=1, source_target_pairs={{0,64},{8,72},{16,80},{24,88},{96,32},{104,40},{112,48},{120,56},{... | collective-permute-start | bytes 4718600 | tf_op jit(solution)/shard_map/ppermute | solution.py:51
  109.3 71.7 %collective-permute-start.14 = (bf16[2,2,128,1536]{3,2,1,0:T(8,128)(2,1)}, bf16[2,2,128,1536]{3,2,1,0:T(8,128)(2,1)}, u32[]{:S(2)}, u32[]{:S(2)}) collective-permute-start(bf16[2,2,128,1536]{3,2,1,0:T(8,128)(2,1)} %get-tuple-element.63), channel_id=1, source_target_pairs={{0,16},{8,24},{16,32},{24,40},{32,48},{40,56},{48,0},{56,8},{64,80... | collective-permute-start | bytes 4718600 | tf_op jit(solution)/shard_map/ppermute | solution.py:53
  110.2 70.9 %collective-permute-start.15 = (bf16[2,2,128,1536]{3,2,1,0:T(8,128)(2,1)}, bf16[2,2,128,1536]{3,2,1,0:T(8,128)(2,1)}, u32[]{:S(2)}, u32[]{:S(2)}) collective-permute-start(bf16[2,2,128,1536]{3,2,1,0:T(8,128)(2,1)} %get-tuple-element.64), channel_id=1, source_target_pairs={{0,48},{8,56},{16,0},{24,8},{32,16},{40,24},{48,32},{56,40},{64,11... | collective-permute-start | bytes 4718600 | tf_op jit(solution)/shard_map/ppermute | solution.py:54
  113.7 104.2 %slice-start.1 = ((s8[4718592]{0:T(1024)(128)(4,1)}), s8[524288]{0:T(1024)(128)(4,1)S(1)}, s32[]{:S(2)}) async-start(s8[4718592]{0:T(1024)(128)(4,1)} %bitcast.31), calls=%async_computation.1 | async-start | bytes 1048576
  173.9 37.4 %collective-permute-start.12 = (bf16[2,2,128,1536]{3,2,1,0:T(8,128)(2,1)}, bf16[2,2,128,1536]{3,2,1,0:T(8,128)(2,1)}, u32[]{:S(2)}, u32[]{:S(2)}) collective-permute-start(bf16[2,2,128,1536]{3,2,1,0:T(8,128)(2,1)} %collective-permute-done.8), channel_id=1, source_target_pairs={{64,80},{72,88},{80,64},{88,72},{32,48},{40,56},{48,32},{56,40},{6... | collective-permute-start | bytes 4718600 | tf_op jit(solution)/shard_map/ppermute | solution.py:61
  176.9 34.3 %collective-permute-start.13 = (bf16[2,2,128,1536]{3,2,1,0:T(8,128)(2,1)}, bf16[2,2,128,1536]{3,2,1,0:T(8,128)(2,1)}, u32[]{:S(2)}, u32[]{:S(2)}) collective-permute-start(bf16[2,2,128,1536]{3,2,1,0:T(8,128)(2,1)} %collective-permute-done.8), channel_id=1, source_target_pairs={{72,64},{48,56},{73,65},{49,57},{74,66},{50,58},{75,67},{51,59},{7... | collective-permute-start | bytes 4718600 | tf_op jit(solution)/shard_map/ppermute | solution.py:61
  211.3 8.7 %collective-permute-start.17 = (bf16[2,2,128,1536]{3,2,1,0:T(8,128)(2,1)}, bf16[2,2,128,1536]{3,2,1,0:T(8,128)(2,1)}, u32[]{:S(2)}, u32[]{:S(2)}) collective-permute-start(bf16[2,2,128,1536]{3,2,1,0:T(8,128)(2,1)} %collective-permute-done.7), channel_id=1, source_target_pairs={{72,64},{48,56},{73,65},{49,57},{74,66},{50,58},{75,67},{51,59},{7... | collective-permute-start | bytes 4718600 | tf_op jit(solution)/shard_map/ppermute | solution.py:61
  216.0 36.9 %collective-permute-start.16 = (bf16[2,2,128,1536]{3,2,1,0:T(8,128)(2,1)}, bf16[2,2,128,1536]{3,2,1,0:T(8,128)(2,1)S(1)}, u32[]{:S(2)}, u32[]{:S(2)}) collective-permute-start(bf16[2,2,128,1536]{3,2,1,0:T(8,128)(2,1)} %collective-permute-done.7), channel_id=1, source_target_pairs={{64,80},{72,88},{80,64},{88,72},{32,48},{40,56},{48,32},{56,40},{6... | collective-permute-start | bytes 4718600 | tf_op jit(solution)/shard_map/ppermute | solution.py:61
  254.1 8.9 %copy-start.1 = (bf16[1728,256]{1,0:T(8,128)(2,1)S(1)}, bf16[1728,256]{1,0:T(8,128)(2,1)}, u32[]{:S(2)}) copy-start(bf16[1728,256]{1,0:T(8,128)(2,1)} %param.12) | copy-start | bytes 2654212
  (3 other events, 5.7 us)

commit v4 on v2

--- a/solution.py
+++ b/solution.py
@@ -36,26 +36,30 @@
     return rows_before, rows_after, mate
 
 
-def second(below, above, frame_idx):
+def second(below, above, rows_before, rows_after, frame_idx):
     everyone = range(2 * RING)
     half = below.shape[-1] // 2
     from_below = (frame_idx < 2) | (frame_idx == 12) | (frame_idx == 13)
     odd = frame_idx % 2 == 1
     parts = (
+        jnp.where(from_below, below[..., :half], above[..., :half]),
         below[..., :half],
         above[..., half:],
-        jnp.where(from_below, below[..., :half], above[..., :half]),
-        jnp.where(from_below, below[..., half:], above[..., half:]),
     )
     parts, below, above = lax.optimization_barrier((parts, below, above))
-    below_keys, above_values, edge_keys, edge_values = parts
+    edge_keys, below_keys, above_values = parts
     over = [(0, 8), (1, 9), (2, 10), (3, 11), (12, 4), (13, 5), (14, 6), (15, 7)]
+    cross_keys = lax.ppermute(edge_keys, "tm", over)
     far_keys = lax.ppermute(below_keys, "tm", [(i, around(i, 2)) for i in everyone])
     far_values = lax.ppermute(above_values, "tm", [(i, around(i, -2)) for i in everyone])
-    cross_keys = lax.ppermute(edge_keys, "tm", over)
+    below, above, rows_before, rows_after = lax.optimization_barrier(
+        (below, above, rows_before, rows_after)
+    )
+    edge_values = jnp.where(from_below, below[..., half:], above[..., half:])
     cross_values = lax.ppermute(edge_values, "tm", over)
     beside = lax.ppermute(jnp.where(odd, below, above), "tm", swap(0) + swap(1))
-    return far_keys, far_values, cross_keys, cross_values, beside
+    rows = (rows_before, rows_after)
+    return far_keys, far_values, cross_keys, cross_values, beside, rows
 
 
 def third(cross):
@@ -314,12 +318,13 @@
 
     state = add(None, 20, (0, kv_stale), (3, mate))
     below, above, state = lax.optimization_barrier((below, above, state))
-    far_keys, far_values, cross_keys, cross_values, beside = second(below, above, frame_idx)
-    near = [(1, rows_before), (2, rows_after), (4, below), (5, above)]
-    state = add(state, 30, *near, (6, beside))
+    far_keys, far_values, cross_keys, cross_values, beside, level = second(
+        below, above, rows_before, rows_after, frame_idx
+    )
+    state = add(state, 25, (1, level[0]), (2, level[1]), (4, below), (5, above))
     cross_keys, state = lax.optimization_barrier((cross_keys, state))
     trade_keys, mate_keys = third(cross_keys)
-    state = add(state, 15, (7, far_keys, far_values))
+    state = add(state, 20, (6, beside), (7, far_keys, far_values))
     cross_values, trade_keys, mate_keys, state = lax.optimization_barrier(
         (cross_values, trade_keys, mate_keys, state)
     )

time: 233 us -> 281 us (1.21)
  waiting for transfers between devices: 62.9 us -> 112 us
  starting transfers between devices: 51.7 us -> 48.3 us
    ppermute x1, waiting for transfers between devices: 6.68 us -> 49.6 us  [second(): cross_keys = lax.ppermute(edge_keys, 'tm', over)]
    ppermute x1, waiting for transfers between devices: 18.8 us -> 0.01 us  [second(): cross_values = lax.ppermute(edge_values, 'tm', over)]
    ppermute x2, waiting for transfers between devices: 1.94 us -> 20.5 us  [from_behind(): return lax.ppermute(block, axis, route)]
    ppermute x2, waiting for transfers between devices: 25.2 us -> 38.5 us  [third(): lax.ppermute(cross, 'tm', trade)]
    ppermute x1, waiting for transfers between devices: 7.51 us -> 0.01 us  [ring_sides(): below = lax.ppermute(kv, 'tm', [(i, around(i, 2)) for i in everyone])]
    ppermute x2, starting transfers between devices: 13 us -> 7.55 us  [third(): lax.ppermute(cross, 'tm', [(9, 8), (6, 7)])]
    ppermute x1, starting transfers between devices: 3.17 us -> 7.63 us  [nearest(): mate = lax.ppermute(kv, 'tm', swap(0) + swap(1))]
    slice x0 -> x1, other arithmetic: none -> 4.33 us  [second(): above[..., half:]]
  transfers between devices with their start and end apart: 18 -> 18, of which waited for: 8 -> 7; matrix products, arithmetic and copies ran while one was open for 18% -> 15% of each run, Pallas kernels for 25% -> 21%
where the time goes in v4:
time: 281 us; the launch traced here: 279 us
  waiting for transfers between devices  112 us (40%)
  Pallas kernels  68 us (24%)
  starting transfers between devices  48.3 us (17%)
  matrix products  19.7 us (7%)
  local copies, waits for them, and re-layouts  16.4 us (6%)
  other arithmetic  13.9 us (5%)
    pallas_call x5, Pallas kernels, attend(): pl.pallas_call(functools.partial(attend_kernel, ids, first, last), grid=(...  68 us
    ppermute x1, waiting for transfers between devices, second(): cross_keys = lax.ppermute(edge_keys, 'tm', over)  49.6 us
    ppermute x2, waiting for transfers between devices, third(): lax.ppermute(cross, 'tm', trade)  38.5 us
    ppermute x2, waiting for transfers between devices, from_behind(): return lax.ppermute(block, axis, route)  20.5 us
    dot_general x1, matrix products, body(): jnp.dot(normed, w_qkv, preferred_element_type=jnp.float32)  14.4 us
    ppermute x1, starting transfers between devices, nearest(): mate = lax.ppermute(kv, 'tm', swap(0) + swap(1))  7.63 us
    ppermute x2, starting transfers between devices, with_halo(): lax.ppermute(head, axis, [((i + 1) % count, i) for i in range(ends)])  7.57 us
    ppermute x2, starting transfers between devices, third(): lax.ppermute(cross, 'tm', [(9, 8), (6, 7)])  7.55 us
  transfers between devices with their start and end apart: 18, of which 7 were waited for; matrix products, arithmetic and copies ran while one was open for 15% of the time, Pallas kernels for 21%

profile of v4, /device:TPU:25, one launch (start us, length us, event | category | flops | bytes accessed | tf_op | source)
XLA Modules:
  0.0 279.1 jit_solution(8235082657692398885)
XLA Ops:
  1.6 2.6 collective-permute-start.1
  4.1 3.0 %collective-permute-start = (bf16[1,2,8192]{2,1,0:T(2,128)(2,1)S(1)}, bf16[1,2,8192]{2,1,0:T(2,128)(2,1)S(1)}, u32[]{:S(2)}, u32[]{:S(2)}) collective-permute-start(bf16[1,2,8192]{2,1,0:T(2,128)(2,1)S(1)} %get-tuple-element.114), channel_id=1, source_target_pairs={{0,8},{8,16},{16,24},{24,32},{32,40},{40,48},{48,56},{56,64},{64,7... | collective-permute-start | bytes 98312 | tf_op jit(solution)/shard_map/ppermute | solution.py:96
  10.8 5.0 %collective-permute-start.3 = (bf16[4,1,8192]{2,1,0:T(2,128)(2,1)S(1)}, bf16[4,1,8192]{2,1,0:T(2,128)(2,1)S(1)}, u32[]{:S(2)}, u32[]{:S(2)}) collective-permute-start(bf16[4,1,8192]{2,1,0:T(2,128)(2,1)S(1)} %get-tuple-element.113), channel_id=1, source_target_pairs={{1,0},{2,1},{3,2},{4,3},{5,4},{6,5},{7,6},{9,8},{10,9},{11,10},{12... | collective-permute-start | bytes 196616 | tf_op jit(solution)/shard_map/ppermute | solution.py:98
  21.0 2.7 collective-permute-done.2
  27.6 7.6 %collective-permute-start.6 = (bf16[2,2,128,3072]{3,2,1,0:T(8,128)(2,1)}, bf16[2,2,128,3072]{3,2,1,0:T(8,128)(2,1)}, u32[]{:S(2)}, u32[]{:S(2)}) collective-permute-start(bf16[2,2,128,3072]{3,2,1,0:T(8,128)(2,1)} %param.17), channel_id=1, source_target_pairs={{0,8},{16,24},{32,40},{48,56},{64,72},{80,88},{96,104},{112,120},{... | collective-permute-start | bytes 9437192 | tf_op jit(solution)/shard_map/ppermute | solution.py:35
  37.1 5.5 %collective-permute-start.8 = (bf16[2,2,128,3072]{3,2,1,0:T(8,128)(2,1)}, bf16[2,2,128,3072]{3,2,1,0:T(8,128)(2,1)}, u32[]{:S(2)}, u32[]{:S(2)}) collective-permute-start(bf16[2,2,128,3072]{3,2,1,0:T(8,128)(2,1)} %param.17), channel_id=1, source_target_pairs={{1,0},{2,1},{3,2},{4,3},{5,4},{6,5},{7,6},{9,8},{10,9},{11,10},{12... | collective-permute-start | bytes 9437192 | tf_op jit(solution)/shard_map/ppermute | solution.py:108
  42.6 4.5 %concatenate.11 = bf16[2,2,128,1728]{3,2,1,0:T(8,128)(2,1)S(1)} concatenate(bf16[2,2,128,64]{3,2,1,0:T(8,128)(2,1)} %get-tuple-element.111, bf16[2,2,128,64]{3,2,1,0:T(8,128)(2,1)} %get-tuple-element.110, bf16[2,2,128,64]{3,2,1,0:T(8,128)(2,1)} %get-tuple-element.86, bf16[2,2,128,64]{3,2,1,0:T(8,128)(2,1)} %get-tuple-element.87, bf16[2,2,128,64]{3,2,1,0:T(8,128)(2,1)} %get-tuple-element.109, ...), dimensions={3} | concatenate | bytes 3538944 | tf_op jit(solution)/shard_map/concatenate | solution.py:288
  47.2 5.2 %fusion.15 = (f32[512]{0:T(512)S(1)}, f32[512,1536]{1,0:T(8,128)}) fusion(bf16[256,1536]{1,0:T(8,128)(2,1)} %param.13, bf16[512,1536]{1,0:T(8,128)(2,1)} %bitcast.33, bf16[512,1728]{1,0:T(8,128)(2,1)S(1)} %bitcast.32, bf16[1728,256]{1,0:T(8,128)(2,1)S(1)} %copy-done), kind=kOutput, calls=%fused_computation.65 | convolution fusion | flops 858652160 | bytes 8161280 | tf_op jit(solution)/shard_map/dot_general | solution.py:291
  52.4 2.5 multiply_reduce_fusion
  55.3 14.4 %convolution_convert_fusion = bf16[512,4608]{1,0:T(8,128)(2,1)} fusion(bf16[1536,4608]{1,0:T(8,128)(2,1)} %param.16, f32[512,1536]{1,0:T(8,128)S(1)} %copy-done.2, f32[1536]{0:T(1024)S(1)} %copy-done.5, f32[1536]{0:T(1024)S(1)} %copy-done.6, f32[512]{0:T(512)S(1)} %add_rsqrt_fusion, f32[512]{0:T(512)S(1)} %broadcast_multiply_fusion), kind=kOutput, calls=%fused_computation | convolution fusion | flops 7254048768 | bytes 22036480 | tf_op jit(solution)/shard_map/dot_general | solution.py:297
  69.7 15.6 %shard_map.113 = (f32[4,12,128,128]{3,2,1,0:T(8,128)}, f32[4,12,128]{2,1,0:T(8,128)}, f32[4,12,128]{2,1,0:T(8,128)}) custom-call(s32[32]{0:T(128)} %fusion.6.refs_0_, bf16[4,128,4608]{2,1,0:T(8,128)(2,1)} %bitcast.26, bf16[4,128,3072]{2,1,0:T(8,128)(2,1)} %bitcast.4.refs_2_, bf16[4,128,3072]{2,1,0:T(8,128)(2,1)} %bitcast.5.refs_3_), custom_call_target="tpu_custom_call" | custom-call | flops 20000000000 | bytes 60000000 | tf_op jit(solution)/shard_map/pallas_call | solution.py:243
  85.3 4.3 %fusion.11 = (bf16[2,2,128,1536]{3,2,1,0:T(8,128)(2,1)S(1)}, bf16[2,2,128,1536]{3,2,1,0:T(8,128)(2,1)}, bf16[2,2,128,1536]{3,2,1,0:T(8,128)(2,1)}) fusion(bf16[2,2,128,3072]{3,2,1,0:T(8,128)(2,1)} %collective-permute-done.5, bf16[2,2,128,3072]{3,2,1,0:T(8,128)(2,1)} %collective-permute-done.4, pred[]{:T(512)S(6)} %or.7), kind=kLoop, calls=%fused_computation.61 | loop fusion | flops 786432 | bytes 9437185 | tf_op jit(solution)/shard_map/slice | solution.py:47
  89.6 19.6 %collective-permute-done.7 = bf16[2,2,128,3072]{3,2,1,0:T(8,128)(2,1)} collective-permute-done((bf16[2,2,128,3072]{3,2,1,0:T(8,128)(2,1)}, bf16[2,2,128,3072]{3,2,1,0:T(8,128)(2,1)}, u32[]{:S(2)}, u32[]{:S(2)}) %collective-permute-start.7) | collective-permute-done | bytes 3145760 | tf_op jit(solution)/shard_map/ppermute | solution.py:108
  118.4 2.7 collective-permute-start.15
  121.1 18.1 %shard_map.114 = (f32[4,12,128,128]{3,2,1,0:T(8,128)}, f32[4,12,128]{2,1,0:T(8,128)}, f32[4,12,128]{2,1,0:T(8,128)}) custom-call(s32[32]{0:T(128)} %fusion.6.refs_0_, bf16[4,128,4608]{2,1,0:T(8,128)(2,1)} %bitcast.27, bf16[4,128,3072]{2,1,0:T(8,128)(2,1)} %bitcast.6.refs_2_, bf16[4,128,3072]{2,1,0:T(8,128)(2,1)} %bitcast.7.refs_3_, ...), custom_call_target="tpu_custom_call" | custom-call | flops 24999999488 | bytes 75000000 | tf_op jit(solution)/shard_map/pallas_call | solution.py:243
  139.2 49.6 %collective-permute-done.10 = bf16[2,2,128,1536]{3,2,1,0:T(8,128)(2,1)} collective-permute-done((bf16[2,2,128,1536]{3,2,1,0:T(8,128)(2,1)}, bf16[2,2,128,1536]{3,2,1,0:T(8,128)(2,1)}, u32[]{:S(2)}, u32[]{:S(2)}) %collective-permute-start.10) | collective-permute-done | bytes 1572896 | tf_op jit(solution)/shard_map/ppermute | solution.py:52
  190.7 3.9 %collective-permute-start.12 = (bf16[2,2,128,1536]{3,2,1,0:T(8,128)(2,1)}, bf16[2,2,128,1536]{3,2,1,0:T(8,128)(2,1)}, u32[]{:S(2)}, u32[]{:S(2)}) collective-permute-start(bf16[2,2,128,1536]{3,2,1,0:T(8,128)(2,1)} %collective-permute-done.10), channel_id=1, source_target_pairs={{72,64},{48,56},{73,65},{49,57},{74,66},{50,58},{75,67},{51,59},{7... | collective-permute-start | bytes 4718600 | tf_op jit(solution)/shard_map/ppermute | solution.py:67
  194.6 13.1 %shard_map.115 = (f32[4,12,128,128]{3,2,1,0:T(8,128)}, f32[4,12,128]{2,1,0:T(8,128)}, f32[4,12,128]{2,1,0:T(8,128)}) custom-call(s32[32]{0:T(128)} %fusion.6.refs_0_, bf16[4,128,4608]{2,1,0:T(8,128)(2,1)} %bitcast.28, bf16[4,128,3072]{2,1,0:T(8,128)(2,1)} %bitcast.10.refs_2_, bf16[4,128,1536]{2,1,0:T(8,128)(2,1)} %bitcast.11.refs_3_, ...), custom_call_target="tpu_custom_call" | custom-call | flops 20000000000 | bytes 60000000 | tf_op jit(solution)/shard_map/pallas_call | solution.py:243
  207.8 18.4 %collective-permute-done.11 = bf16[2,2,128,1536]{3,2,1,0:T(8,128)(2,1)} collective-permute-done((bf16[2,2,128,1536]{3,2,1,0:T(8,128)(2,1)}, bf16[2,2,128,1536]{3,2,1,0:T(8,128)(2,1)}, u32[]{:S(2)}, u32[]{:S(2)}) %collective-permute-start.11) | collective-permute-done | bytes 1572896 | tf_op jit(solution)/shard_map/ppermute | solution.py:67
  226.1 3.7 %collective-permute-start.17 = (bf16[2,2,128,1536]{3,2,1,0:T(8,128)(2,1)}, bf16[2,2,128,1536]{3,2,1,0:T(8,128)(2,1)S(1)}, u32[]{:S(2)}, u32[]{:S(2)}) collective-permute-start(bf16[2,2,128,1536]{3,2,1,0:T(8,128)(2,1)} %collective-permute-done.9), channel_id=1, source_target_pairs={{72,64},{48,56},{73,65},{49,57},{74,66},{50,58},{75,67},{51,59},{7... | collective-permute-start | bytes 4718600 | tf_op jit(solution)/shard_map/ppermute | solution.py:67
  231.7 3.8 %slice.167 = bf16[2,2,128,3072]{3,2,1,0:T(8,128)(2,1)} slice(bf16[2,2,128,4608]{3,2,1,0:T(8,128)(2,1)} %bitcast.29), slice={[0:2], [0:2], [0:128], [1536:4608]} | slice | bytes 6291456 | tf_op jit(solution)/shard_map/slice | solution.py:299
  236.6 11.0 %shard_map.116 = (f32[4,12,128,128]{3,2,1,0:T(8,128)}, f32[4,12,128]{2,1,0:T(8,128)}, f32[4,12,128]{2,1,0:T(8,128)}) custom-call(s32[32]{0:T(128)} %fusion.6.refs_0_, bf16[4,128,4608]{2,1,0:T(8,128)(2,1)} %bitcast.30, bf16[4,128,1536]{2,1,0:T(8,128)(2,1)} %bitcast.15.refs_2_, bf16[4,128,1536]{2,1,0:T(8,128)(2,1)} %bitcast.16.refs_3_, ...), custom_call_target="tpu_custom_call" | custom-call | flops 12000000000 | bytes 36000000 | tf_op jit(solution)/shard_map/pallas_call | solution.py:243
  247.7 20.2 %collective-permute-done.16 = bf16[2,2,128,1536]{3,2,1,0:T(8,128)(2,1)S(1)} collective-permute-done((bf16[2,2,128,1536]{3,2,1,0:T(8,128)(2,1)}, bf16[2,2,128,1536]{3,2,1,0:T(8,128)(2,1)S(1)}, u32[]{:S(2)}, u32[]{:S(2)}) %collective-permute-start.16) | collective-permute-done | bytes 1572896 | tf_op jit(solution)/shard_map/ppermute | solution.py:67
  269.0 10.1 %shard_map.117 = bf16[4,128,1536]{2,1,0:T(8,128)(2,1)} custom-call(s32[32]{0:T(128)} %fusion.6.refs_0_, bf16[4,128,4608]{2,1,0:T(8,128)(2,1)} %bitcast.31, bf16[4,128,1536]{2,1,0:T(8,128)(2,1)} %bitcast.13.refs_2_, bf16[4,128,1536]{2,1,0:T(8,128)(2,1)} %bitcast.34, f32[4,12,128,128]{3,2,1,0:T(8,128)} %get-tuple-element.79.refs_4_, ...), custom_call_target="tpu_custom_call" | custom-call | flops 8000000000 | bytes 24000000 | tf_op jit(solution)/shard_map/pallas_call | solution.py:243
  (53 shorter events, 31.2 us)
Async XLA Ops:
  0.6 46.5 %copy-start = (bf16[1728,256]{1,0:T(8,128)(2,1)S(1)}, bf16[1728,256]{1,0:T(8,128)(2,1)}, u32[]{:S(2)}) copy-start(bf16[1728,256]{1,0:T(8,128)(2,1)} %param.12) | copy-start | bytes 2654212
  1.6 7.2 %collective-permute-start.1 = (bf16[1,2,8192]{2,1,0:T(2,128)(2,1)S(1)}, bf16[1,2,8192]{2,1,0:T(2,128)(2,1)S(1)}, u32[]{:S(2)}, u32[]{:S(2)}) collective-permute-start(bf16[1,2,8192]{2,1,0:T(2,128)(2,1)S(1)} %get-tuple-element.115), channel_id=1, source_target_pairs={{8,0},{16,8},{24,16},{32,24},{40,32},{48,40},{56,48},{64,56},{72,6... | collective-permute-start | bytes 98312 | tf_op jit(solution)/shard_map/ppermute | solution.py:98
  4.1 5.5 %collective-permute-start = (bf16[1,2,8192]{2,1,0:T(2,128)(2,1)S(1)}, bf16[1,2,8192]{2,1,0:T(2,128)(2,1)S(1)}, u32[]{:S(2)}, u32[]{:S(2)}) collective-permute-start(bf16[1,2,8192]{2,1,0:T(2,128)(2,1)S(1)} %get-tuple-element.114), channel_id=1, source_target_pairs={{0,8},{8,16},{16,24},{24,32},{32,40},{40,48},{48,56},{56,64},{64,7... | collective-permute-start | bytes 98312 | tf_op jit(solution)/shard_map/ppermute | solution.py:96
  10.8 10.2 %collective-permute-start.3 = (bf16[4,1,8192]{2,1,0:T(2,128)(2,1)S(1)}, bf16[4,1,8192]{2,1,0:T(2,128)(2,1)S(1)}, u32[]{:S(2)}, u32[]{:S(2)}) collective-permute-start(bf16[4,1,8192]{2,1,0:T(2,128)(2,1)S(1)} %get-tuple-element.113), channel_id=1, source_target_pairs={{1,0},{2,1},{3,2},{4,3},{5,4},{6,5},{7,6},{9,8},{10,9},{11,10},{12... | collective-permute-start | bytes 196616 | tf_op jit(solution)/shard_map/ppermute | solution.py:98
  15.8 7.8 %collective-permute-start.2 = (bf16[4,1,8192]{2,1,0:T(2,128)(2,1)S(1)}, bf16[4,1,8192]{2,1,0:T(2,128)(2,1)S(1)}, u32[]{:S(2)}, u32[]{:S(2)}) collective-permute-start(bf16[4,1,8192]{2,1,0:T(2,128)(2,1)S(1)} %get-tuple-element.112), channel_id=1, source_target_pairs={{0,1},{1,2},{2,3},{3,4},{4,5},{5,6},{6,7},{8,9},{9,10},{10,11},{11... | collective-permute-start | bytes 196616 | tf_op jit(solution)/shard_map/ppermute | solution.py:96
  18.3 67.0 %collective-permute-start.4 = (bf16[2,2,128,3072]{3,2,1,0:T(8,128)(2,1)}, bf16[2,2,128,3072]{3,2,1,0:T(8,128)(2,1)}, u32[]{:S(2)}, u32[]{:S(2)}) collective-permute-start(bf16[2,2,128,3072]{3,2,1,0:T(8,128)(2,1)} %param.17), channel_id=1, source_target_pairs={{0,16},{8,24},{16,32},{24,40},{32,48},{40,56},{48,0},{56,8},{64,80... | collective-permute-start | bytes 9437192 | tf_op jit(solution)/shard_map/ppermute | solution.py:27
  19.5 65.7 %collective-permute-start.5 = (bf16[2,2,128,3072]{3,2,1,0:T(8,128)(2,1)}, bf16[2,2,128,3072]{3,2,1,0:T(8,128)(2,1)}, u32[]{:S(2)}, u32[]{:S(2)}) collective-permute-start(bf16[2,2,128,3072]{3,2,1,0:T(8,128)(2,1)} %param.17), channel_id=1, source_target_pairs={{0,48},{8,56},{16,0},{24,8},{32,16},{40,24},{48,32},{56,40},{64,11... | collective-permute-start | bytes 9437192 | tf_op jit(solution)/shard_map/ppermute | solution.py:28
  27.6 42.1 %collective-permute-start.6 = (bf16[2,2,128,3072]{3,2,1,0:T(8,128)(2,1)}, bf16[2,2,128,3072]{3,2,1,0:T(8,128)(2,1)}, u32[]{:S(2)}, u32[]{:S(2)}) collective-permute-start(bf16[2,2,128,3072]{3,2,1,0:T(8,128)(2,1)} %param.17), channel_id=1, source_target_pairs={{0,8},{16,24},{32,40},{48,56},{64,72},{80,88},{96,104},{112,120},{... | collective-permute-start | bytes 9437192 | tf_op jit(solution)/shard_map/ppermute | solution.py:35
  35.2 74.0 %collective-permute-start.7 = (bf16[2,2,128,3072]{3,2,1,0:T(8,128)(2,1)}, bf16[2,2,128,3072]{3,2,1,0:T(8,128)(2,1)}, u32[]{:S(2)}, u32[]{:S(2)}) collective-permute-start(bf16[2,2,128,3072]{3,2,1,0:T(8,128)(2,1)} %param.17), channel_id=1, source_target_pairs={{0,1},{1,2},{2,3},{3,4},{4,5},{5,6},{6,7},{8,9},{9,10},{10,11},{11... | collective-permute-start | bytes 9437192 | tf_op jit(solution)/shard_map/ppermute | solution.py:108
  37.1 73.0 %collective-permute-start.8 = (bf16[2,2,128,3072]{3,2,1,0:T(8,128)(2,1)}, bf16[2,2,128,3072]{3,2,1,0:T(8,128)(2,1)}, u32[]{:S(2)}, u32[]{:S(2)}) collective-permute-start(bf16[2,2,128,3072]{3,2,1,0:T(8,128)(2,1)} %param.17), channel_id=1, source_target_pairs={{1,0},{2,1},{3,2},{4,3},{5,4},{6,5},{7,6},{9,8},{10,9},{11,10},{12... | collective-permute-start | bytes 9437192 | tf_op jit(solution)/shard_map/ppermute | solution.py:108
  47.2 7.8 %copy-start.6 = (f32[1536]{0:T(1024)S(1)}, f32[1536]{0:T(1024)}, u32[]{:S(2)}) copy-start(f32[1536]{0:T(1024)} %param.14) | copy-start | bytes 18436
  52.4 2.8 %copy-start.2 = (f32[512,1536]{1,0:T(8,128)S(1)}, f32[512,1536]{1,0:T(8,128)}, u32[]{:S(2)}) copy-start(f32[512,1536]{1,0:T(8,128)} %get-tuple-element.117) | copy-start | bytes 9437188
  52.4 2.8 %copy-start.5 = (f32[1536]{0:T(1024)S(1)}, f32[1536]{0:T(1024)}, u32[]{:S(2)}) copy-start(f32[1536]{0:T(1024)} %param.15) | copy-start | bytes 18436
  112.3 82.3 %collective-permute-start.13 = (bf16[2,2,128,3072]{3,2,1,0:T(8,128)(2,1)S(1)}, bf16[2,2,128,3072]{3,2,1,0:T(8,128)(2,1)}, u32[]{:S(2)}, u32[]{:S(2)}) collective-permute-start(bf16[2,2,128,3072]{3,2,1,0:T(8,128)(2,1)S(1)} %broadcast_select_fusion), channel_id=1, source_target_pairs={{0,8},{16,24},{32,40},{48,56},{64,72},{80,88},{96,104},{112,120},{... | collective-permute-start | bytes 9437192 | tf_op jit(solution)/shard_map/ppermute | solution.py:60
  115.6 92.2 %collective-permute-start.9 = (bf16[2,2,128,1536]{3,2,1,0:T(8,128)(2,1)S(1)}, bf16[2,2,128,1536]{3,2,1,0:T(8,128)(2,1)}, u32[]{:S(2)}, u32[]{:S(2)}) collective-permute-start(bf16[2,2,128,1536]{3,2,1,0:T(8,128)(2,1)S(1)} %slice_select_fusion), channel_id=1, source_target_pairs={{0,64},{8,72},{16,80},{24,88},{96,32},{104,40},{112,48},{120,56},{... | collective-permute-start | bytes 4718600 | tf_op jit(solution)/shard_map/ppermute | solution.py:59
  117.1 71.7 %collective-permute-start.10 = (bf16[2,2,128,1536]{3,2,1,0:T(8,128)(2,1)}, bf16[2,2,128,1536]{3,2,1,0:T(8,128)(2,1)}, u32[]{:S(2)}, u32[]{:S(2)}) collective-permute-start(bf16[2,2,128,1536]{3,2,1,0:T(8,128)(2,1)} %get-tuple-element.55), channel_id=1, source_target_pairs={{0,64},{8,72},{16,80},{24,88},{96,32},{104,40},{112,48},{120,56},{... | collective-permute-start | bytes 4718600 | tf_op jit(solution)/shard_map/ppermute | solution.py:52
  118.4 72.4 %collective-permute-start.14 = (bf16[2,2,128,1536]{3,2,1,0:T(8,128)(2,1)}, bf16[2,2,128,1536]{3,2,1,0:T(8,128)(2,1)}, u32[]{:S(2)}, u32[]{:S(2)}) collective-permute-start(bf16[2,2,128,1536]{3,2,1,0:T(8,128)(2,1)} %get-tuple-element.65), channel_id=1, source_target_pairs={{0,16},{8,24},{16,32},{24,40},{32,48},{40,56},{48,0},{56,8},{64,80... | collective-permute-start | bytes 4718600 | tf_op jit(solution)/shard_map/ppermute | solution.py:53
  118.4 76.2 %collective-permute-start.15 = (bf16[2,2,128,1536]{3,2,1,0:T(8,128)(2,1)S(1)}, bf16[2,2,128,1536]{3,2,1,0:T(8,128)(2,1)}, u32[]{:S(2)}, u32[]{:S(2)}) collective-permute-start(bf16[2,2,128,1536]{3,2,1,0:T(8,128)(2,1)S(1)} %get-tuple-element.66), channel_id=1, source_target_pairs={{0,48},{8,56},{16,0},{24,8},{32,16},{40,24},{48,32},{56,40},{64,11... | collective-permute-start | bytes 4718600 | tf_op jit(solution)/shard_map/ppermute | solution.py:54
  188.8 37.3 %collective-permute-start.11 = (bf16[2,2,128,1536]{3,2,1,0:T(8,128)(2,1)}, bf16[2,2,128,1536]{3,2,1,0:T(8,128)(2,1)}, u32[]{:S(2)}, u32[]{:S(2)}) collective-permute-start(bf16[2,2,128,1536]{3,2,1,0:T(8,128)(2,1)} %collective-permute-done.10), channel_id=1, source_target_pairs={{64,80},{72,88},{80,64},{88,72},{32,48},{40,56},{48,32},{56,40},{6... | collective-permute-start | bytes 4718600 | tf_op jit(solution)/shard_map/ppermute | solution.py:67
  190.7 35.4 %collective-permute-start.12 = (bf16[2,2,128,1536]{3,2,1,0:T(8,128)(2,1)}, bf16[2,2,128,1536]{3,2,1,0:T(8,128)(2,1)}, u32[]{:S(2)}, u32[]{:S(2)}) collective-permute-start(bf16[2,2,128,1536]{3,2,1,0:T(8,128)(2,1)} %collective-permute-done.10), channel_id=1, source_target_pairs={{72,64},{48,56},{73,65},{49,57},{74,66},{50,58},{75,67},{51,59},{7... | collective-permute-start | bytes 4718600 | tf_op jit(solution)/shard_map/ppermute | solution.py:67
  226.1 9.4 %collective-permute-start.17 = (bf16[2,2,128,1536]{3,2,1,0:T(8,128)(2,1)}, bf16[2,2,128,1536]{3,2,1,0:T(8,128)(2,1)S(1)}, u32[]{:S(2)}, u32[]{:S(2)}) collective-permute-start(bf16[2,2,128,1536]{3,2,1,0:T(8,128)(2,1)} %collective-permute-done.9), channel_id=1, source_target_pairs={{72,64},{48,56},{73,65},{49,57},{74,66},{50,58},{75,67},{51,59},{7... | collective-permute-start | bytes 4718600 | tf_op jit(solution)/shard_map/ppermute | solution.py:67
  229.8 38.0 %collective-permute-start.16 = (bf16[2,2,128,1536]{3,2,1,0:T(8,128)(2,1)}, bf16[2,2,128,1536]{3,2,1,0:T(8,128)(2,1)S(1)}, u32[]{:S(2)}, u32[]{:S(2)}) collective-permute-start(bf16[2,2,128,1536]{3,2,1,0:T(8,128)(2,1)} %collective-permute-done.9), channel_id=1, source_target_pairs={{64,80},{72,88},{80,64},{88,72},{32,48},{40,56},{48,32},{56,40},{6... | collective-permute-start | bytes 4718600 | tf_op jit(solution)/shard_map/ppermute | solution.py:67
  267.8 1.2 copy-start.3
  269.0 10.1 %copy-start.1 = (bf16[1728,256]{1,0:T(8,128)(2,1)S(1)}, bf16[1728,256]{1,0:T(8,128)(2,1)}, u32[]{:S(2)}) copy-start(bf16[1728,256]{1,0:T(8,128)(2,1)} %param.12) | copy-start | bytes 2654212
  (1 other events, 1.1 us)

commit v5 on v2

--- a/solution.py
+++ b/solution.py
@@ -10,7 +10,7 @@
 HEADS = 12
 HD = 128
 LOG2E = 1.4426950408889634
-AHEAD = 2
+AHEAD = 3
 RING = 8
 
 

time: 233 us -> 232 us (level)
  Pallas kernels: 68.3 us -> 59.6 us
  waiting for transfers between devices: 62.9 us -> 69.9 us
    pallas_call x5, Pallas kernels: 68.3 us -> 59.6 us  [attend(): pl.pallas_call(functools.partial(attend_kernel, ids, first, last), grid=(...]
    ppermute x1, waiting for transfers between devices: 7.51 us -> 12.6 us  [ring_sides(): below = lax.ppermute(kv, 'tm', [(i, around(i, 2)) for i in everyone])]
    ppermute x1, waiting for transfers between devices: 6.68 us -> 9.76 us  [second(): cross_keys = lax.ppermute(edge_keys, 'tm', over)]
  transfers between devices with their start and end apart: 18 -> 18, of which waited for: 8 -> 8; matrix products, arithmetic and copies ran while one was open for 18% -> 18% of each run, Pallas kernels for 25% -> 22%
where the time goes in v5:
time: 232 us; the launch traced here: 230 us
  waiting for transfers between devices  69.9 us (30%)
  Pallas kernels  59.6 us (26%)
  starting transfers between devices  51.5 us (22%)
  matrix products  19.7 us (8%)
  local copies, waits for them, and re-layouts  15.3 us (7%)
  other arithmetic  12.8 us (6%)
    pallas_call x5, Pallas kernels, attend(): pl.pallas_call(functools.partial(attend_kernel, ids, first, last), grid=(...  59.6 us
    ppermute x2, waiting for transfers between devices, third(): lax.ppermute(cross, 'tm', trade)  26 us
    ppermute x1, waiting for transfers between devices, second(): cross_values = lax.ppermute(edge_values, 'tm', over)  16.9 us
    dot_general x1, matrix products, body(): jnp.dot(normed, w_qkv, preferred_element_type=jnp.float32)  14.4 us
    ppermute x2, starting transfers between devices, third(): lax.ppermute(cross, 'tm', [(9, 8), (6, 7)])  13 us
    ppermute x1, waiting for transfers between devices, ring_sides(): below = lax.ppermute(kv, 'tm', [(i, around(i, 2)) for i in everyone])  12.6 us
    ppermute x1, waiting for transfers between devices, second(): cross_keys = lax.ppermute(edge_keys, 'tm', over)  9.76 us
    ppermute x2, starting transfers between devices, from_behind(): return lax.ppermute(block, axis, route)  7.39 us
  transfers between devices with their start and end apart: 18, of which 8 were waited for; matrix products, arithmetic and copies ran while one was open for 18% of the time, Pallas kernels for 22%

profile of v5, /device:TPU:25, one launch (start us, length us, event | category | flops | bytes accessed | tf_op | source)
XLA Modules:
  0.0 229.7 jit_solution(10769523497866505989)
XLA Ops:
  1.6 3.7 %collective-permute-start = (bf16[1,2,8192]{2,1,0:T(2,128)(2,1)S(1)}, bf16[1,2,8192]{2,1,0:T(2,128)(2,1)S(1)}, u32[]{:S(2)}, u32[]{:S(2)}) collective-permute-start(bf16[1,2,8192]{2,1,0:T(2,128)(2,1)S(1)} %get-tuple-element.109), channel_id=1, source_target_pairs={{0,8},{8,16},{16,24},{24,32},{32,40},{40,48},{48,56},{56,64},{64,7... | collective-permute-start | bytes 98312 | tf_op jit(solution)/shard_map/ppermute | solution.py:92
  11.9 3.5 %collective-permute-start.2 = (bf16[4,1,8192]{2,1,0:T(2,128)(2,1)S(1)}, bf16[4,1,8192]{2,1,0:T(2,128)(2,1)S(1)}, u32[]{:S(2)}, u32[]{:S(2)}) collective-permute-start(bf16[4,1,8192]{2,1,0:T(2,128)(2,1)S(1)} %get-tuple-element.107), channel_id=1, source_target_pairs={{0,1},{1,2},{2,3},{3,4},{4,5},{5,6},{6,7},{8,9},{9,10},{10,11},{11... | collective-permute-start | bytes 196616 | tf_op jit(solution)/shard_map/ppermute | solution.py:92
  15.5 4.2 %collective-permute-start.3 = (bf16[4,1,8192]{2,1,0:T(2,128)(2,1)S(1)}, bf16[4,1,8192]{2,1,0:T(2,128)(2,1)S(1)}, u32[]{:S(2)}, u32[]{:S(2)}) collective-permute-start(bf16[4,1,8192]{2,1,0:T(2,128)(2,1)S(1)} %get-tuple-element.108), channel_id=1, source_target_pairs={{1,0},{2,1},{3,2},{4,3},{5,4},{6,5},{7,6},{9,8},{10,9},{11,10},{12... | collective-permute-start | bytes 196616 | tf_op jit(solution)/shard_map/ppermute | solution.py:94
  26.9 3.2 %collective-permute-start.6 = (bf16[2,2,128,3072]{3,2,1,0:T(8,128)(2,1)}, bf16[2,2,128,3072]{3,2,1,0:T(8,128)(2,1)}, u32[]{:S(2)}, u32[]{:S(2)}) collective-permute-start(bf16[2,2,128,3072]{3,2,1,0:T(8,128)(2,1)} %param.17), channel_id=1, source_target_pairs={{0,8},{16,24},{32,40},{48,56},{64,72},{80,88},{96,104},{112,120},{... | collective-permute-start | bytes 9437192 | tf_op jit(solution)/shard_map/ppermute | solution.py:35
  30.1 2.4 %collective-permute-start.9 = (bf16[2,2,128,3072]{3,2,1,0:T(8,128)(2,1)}, bf16[2,2,128,3072]{3,2,1,0:T(8,128)(2,1)}, u32[]{:S(2)}, u32[]{:S(2)}) collective-permute-start(bf16[2,2,128,3072]{3,2,1,0:T(8,128)(2,1)} %param.17), channel_id=1, source_target_pairs={{0,1},{1,2},{2,3},{3,4},{4,5},{5,6},{6,7},{8,9},{9,10},{10,11},{11... | collective-permute-start | bytes 9437192 | tf_op jit(solution)/shard_map/ppermute | solution.py:104
  32.5 5.0 %collective-permute-start.10 = (bf16[2,2,128,3072]{3,2,1,0:T(8,128)(2,1)}, bf16[2,2,128,3072]{3,2,1,0:T(8,128)(2,1)}, u32[]{:S(2)}, u32[]{:S(2)}) collective-permute-start(bf16[2,2,128,3072]{3,2,1,0:T(8,128)(2,1)} %param.17), channel_id=1, source_target_pairs={{1,0},{2,1},{3,2},{4,3},{5,4},{6,5},{7,6},{9,8},{10,9},{11,10},{12... | collective-permute-start | bytes 9437192 | tf_op jit(solution)/shard_map/ppermute | solution.py:104
  37.5 4.5 %concatenate.11 = bf16[2,2,128,1728]{3,2,1,0:T(8,128)(2,1)S(1)} concatenate(bf16[2,2,128,64]{3,2,1,0:T(8,128)(2,1)} %get-tuple-element.106, bf16[2,2,128,64]{3,2,1,0:T(8,128)(2,1)} %get-tuple-element.105, bf16[2,2,128,64]{3,2,1,0:T(8,128)(2,1)} %get-tuple-element.81, bf16[2,2,128,64]{3,2,1,0:T(8,128)(2,1)} %get-tuple-element.82, bf16[2,2,128,64]{3,2,1,0:T(8,128)(2,1)} %get-tuple-element.104, ...), dimensions={3} | concatenate | bytes 3538944 | tf_op jit(solution)/shard_map/concatenate | solution.py:284
  42.1 5.2 %fusion.14 = (f32[512]{0:T(512)S(1)}, f32[512,1536]{1,0:T(8,128)}) fusion(bf16[256,1536]{1,0:T(8,128)(2,1)} %param.13, bf16[512,1536]{1,0:T(8,128)(2,1)} %bitcast.36, bf16[512,1728]{1,0:T(8,128)(2,1)S(1)} %bitcast.34, bf16[1728,256]{1,0:T(8,128)(2,1)S(1)} %copy-done), kind=kOutput, calls=%fused_computation.64 | convolution fusion | flops 858652160 | bytes 8161280 | tf_op jit(solution)/shard_map/dot_general | solution.py:287
  47.3 2.5 %multiply_reduce_fusion = f32[512]{0:T(512)S(1)} fusion(f32[512,1536]{1,0:T(8,128)} %get-tuple-element.112, f32[512]{0:T(512)S(1)} %broadcast_multiply_fusion), kind=kLoop, calls=%fused_computation.3 | loop fusion | flops 2358784 | bytes 3149824 | tf_op jit(solution)/shard_map/reduce_sum | solution.py:291
  50.1 14.4 %convolution_convert_fusion = bf16[512,4608]{1,0:T(8,128)(2,1)} fusion(bf16[1536,4608]{1,0:T(8,128)(2,1)} %param.16, f32[512,1536]{1,0:T(8,128)S(1)} %copy-done.2, f32[1536]{0:T(1024)S(1)} %copy-done.5, f32[1536]{0:T(1024)S(1)} %copy-done.6, f32[512]{0:T(512)S(1)} %add_rsqrt_fusion, f32[512]{0:T(512)S(1)} %broadcast_multiply_fusion), kind=kOutput, calls=%fused_computation | convolution fusion | flops 7254048768 | bytes 22036480 | tf_op jit(solution)/shard_map/dot_general | solution.py:293
  64.6 11.6 %shard_map.113 = (f32[4,12,128,128]{3,2,1,0:T(8,128)}, f32[4,12,128]{2,1,0:T(8,128)}, f32[4,12,128]{2,1,0:T(8,128)}) custom-call(s32[32]{0:T(128)} %fusion.6.refs_0_, bf16[4,128,4608]{2,1,0:T(8,128)(2,1)} %bitcast.26, bf16[4,128,3072]{2,1,0:T(8,128)(2,1)} %bitcast.4.refs_2_, bf16[4,128,3072]{2,1,0:T(8,128)(2,1)} %bitcast.5.refs_3_), custom_call_target="tpu_custom_call" | custom-call | flops 20000000000 | bytes 60000000 | tf_op jit(solution)/shard_map/pallas_call | solution.py:239
  76.2 12.6 %collective-permute-done.4 = bf16[2,2,128,3072]{3,2,1,0:T(8,128)(2,1)} collective-permute-done((bf16[2,2,128,3072]{3,2,1,0:T(8,128)(2,1)}, bf16[2,2,128,3072]{3,2,1,0:T(8,128)(2,1)}, u32[]{:S(2)}, u32[]{:S(2)}) %collective-permute-start.4) | collective-permute-done | bytes 3145760 | tf_op jit(solution)/shard_map/ppermute | solution.py:27
  89.6 5.2 %slice_select_fusion = (bf16[2,2,128,1536]{3,2,1,0:T(8,128)(2,1)S(1)}, bf16[2,2,128,1536]{3,2,1,0:T(8,128)(2,1)}, bf16[2,2,128,1536]{3,2,1,0:T(8,128)(2,1)}, bf16[2,2,128,1536]{3,2,1,0:T(8,128)(2,1)}) fusion(bf16[2,2,128,3072]{3,2,1,0:T(8,128)(2,1)} %collective-permute-done.4, pred[]{:T(512)S(6)} %or.7, bf16[2,2,128,3072]{3,2,1,0:T(8,128)(2,1)} %collective-permute-done.5), kind=kLoop, calls=%fused_computation.5 | loop fusion | flops 1572864 | bytes 12582913 | tf_op jit(solution)/shard_map/jit(_where)/select_n | solution.py:48
  94.8 2.4 %broadcast_select_fusion = bf16[2,2,128,3072]{3,2,1,0:T(8,128)(2,1)S(1)} fusion(bf16[2,2,128,3072]{3,2,1,0:T(8,128)(2,1)} %collective-permute-done.4, bf16[2,2,128,3072]{3,2,1,0:T(8,128)(2,1)} %collective-permute-done.5, pred[]{:T(512)S(6)} %eq.79), kind=kLoop, calls=%fused_computation.4 | loop fusion | flops 1572864 | bytes 9437185 | tf_op jit(solution)/shard_map/jit(_where)/select_n | solution.py:57
  97.1 2.8 %collective-permute-start.11 = (bf16[2,2,128,3072]{3,2,1,0:T(8,128)(2,1)S(1)}, bf16[2,2,128,3072]{3,2,1,0:T(8,128)(2,1)S(1)}, u32[]{:S(2)}, u32[]{:S(2)}) collective-permute-start(bf16[2,2,128,3072]{3,2,1,0:T(8,128)(2,1)S(1)} %broadcast_select_fusion), channel_id=1, source_target_pairs={{0,8},{16,24},{32,40},{48,56},{64,72},{80,88},{96,104},{112,120},{... | collective-permute-start | bytes 9437192 | tf_op jit(solution)/shard_map/ppermute | solution.py:57
  108.8 22.7 %shard_map.114 = (f32[4,12,128,128]{3,2,1,0:T(8,128)}, f32[4,12,128]{2,1,0:T(8,128)}, f32[4,12,128]{2,1,0:T(8,128)}) custom-call(s32[32]{0:T(128)} %fusion.6.refs_0_, bf16[4,128,4608]{2,1,0:T(8,128)(2,1)} %bitcast.27, bf16[4,128,3072]{2,1,0:T(8,128)(2,1)} %bitcast.6.refs_2_, bf16[4,128,3072]{2,1,0:T(8,128)(2,1)} %bitcast.7.refs_3_, ...), custom_call_target="tpu_custom_call" | custom-call | flops 30000001024 | bytes 90000000 | tf_op jit(solution)/shard_map/pallas_call | solution.py:239
  131.5 9.8 %collective-permute-done.8 = bf16[2,2,128,1536]{3,2,1,0:T(8,128)(2,1)} collective-permute-done((bf16[2,2,128,1536]{3,2,1,0:T(8,128)(2,1)}, bf16[2,2,128,1536]{3,2,1,0:T(8,128)(2,1)}, u32[]{:S(2)}, u32[]{:S(2)}) %collective-permute-start.8) | collective-permute-done | bytes 1572896 | tf_op jit(solution)/shard_map/ppermute | solution.py:55
  143.2 6.0 %collective-permute-start.13 = (bf16[2,2,128,1536]{3,2,1,0:T(8,128)(2,1)}, bf16[2,2,128,1536]{3,2,1,0:T(8,128)(2,1)}, u32[]{:S(2)}, u32[]{:S(2)}) collective-permute-start(bf16[2,2,128,1536]{3,2,1,0:T(8,128)(2,1)} %collective-permute-done.8), channel_id=1, source_target_pairs={{72,64},{48,56},{73,65},{49,57},{74,66},{50,58},{75,67},{51,59},{7... | collective-permute-start | bytes 4718600 | tf_op jit(solution)/shard_map/ppermute | solution.py:63
  149.3 8.9 %shard_map.115 = (f32[4,12,128,128]{3,2,1,0:T(8,128)}, f32[4,12,128]{2,1,0:T(8,128)}, f32[4,12,128]{2,1,0:T(8,128)}) custom-call(s32[32]{0:T(128)} %fusion.6.refs_0_, bf16[4,128,4608]{2,1,0:T(8,128)(2,1)} %bitcast.28, bf16[4,128,1536]{2,1,0:T(8,128)(2,1)} %bitcast.11.refs_2_, bf16[4,128,1536]{2,1,0:T(8,128)(2,1)} %bitcast.12.refs_3_, ...), custom_call_target="tpu_custom_call" | custom-call | flops 15000000512 | bytes 45000000 | tf_op jit(solution)/shard_map/pallas_call | solution.py:239
  158.1 16.9 %collective-permute-done.7 = bf16[2,2,128,1536]{3,2,1,0:T(8,128)(2,1)} collective-permute-done((bf16[2,2,128,1536]{3,2,1,0:T(8,128)(2,1)S(1)}, bf16[2,2,128,1536]{3,2,1,0:T(8,128)(2,1)}, u32[]{:S(2)}, u32[]{:S(2)}) %collective-permute-start.7) | collective-permute-done | bytes 1572896 | tf_op jit(solution)/shard_map/ppermute | solution.py:56
  176.4 7.0 %collective-permute-start.17 = (bf16[2,2,128,1536]{3,2,1,0:T(8,128)(2,1)}, bf16[2,2,128,1536]{3,2,1,0:T(8,128)(2,1)}, u32[]{:S(2)}, u32[]{:S(2)}) collective-permute-start(bf16[2,2,128,1536]{3,2,1,0:T(8,128)(2,1)} %collective-permute-done.7), channel_id=1, source_target_pairs={{72,64},{48,56},{73,65},{49,57},{74,66},{50,58},{75,67},{51,59},{7... | collective-permute-start | bytes 4718600 | tf_op jit(solution)/shard_map/ppermute | solution.py:63
  187.5 8.2 %shard_map.116 = (f32[4,12,128,128]{3,2,1,0:T(8,128)}, f32[4,12,128]{2,1,0:T(8,128)}, f32[4,12,128]{2,1,0:T(8,128)}) custom-call(s32[32]{0:T(128)} %fusion.6.refs_0_, bf16[4,128,4608]{2,1,0:T(8,128)(2,1)} %bitcast.29, bf16[4,128,1536]{2,1,0:T(8,128)(2,1)} %bitcast.15.refs_2_, bf16[4,128,1536]{2,1,0:T(8,128)(2,1)} %bitcast.16.refs_3_, ...), custom_call_target="tpu_custom_call" | custom-call | flops 12000000000 | bytes 36000000 | tf_op jit(solution)/shard_map/pallas_call | solution.py:239
  195.7 24.6 %collective-permute-done.16 = bf16[2,2,128,1536]{3,2,1,0:T(8,128)(2,1)S(1)} collective-permute-done((bf16[2,2,128,1536]{3,2,1,0:T(8,128)(2,1)}, bf16[2,2,128,1536]{3,2,1,0:T(8,128)(2,1)S(1)}, u32[]{:S(2)}, u32[]{:S(2)}) %collective-permute-start.16) | collective-permute-done | bytes 1572896 | tf_op jit(solution)/shard_map/ppermute | solution.py:63
  221.5 8.2 %shard_map.117 = bf16[4,128,1536]{2,1,0:T(8,128)(2,1)} custom-call(s32[32]{0:T(128)} %fusion.6.refs_0_, bf16[4,128,4608]{2,1,0:T(8,128)(2,1)} %bitcast.30, bf16[4,128,1536]{2,1,0:T(8,128)(2,1)} %bitcast.13.refs_2_, bf16[4,128,1536]{2,1,0:T(8,128)(2,1)} %bitcast.37, f32[4,12,128,128]{3,2,1,0:T(8,128)} %get-tuple-element.73.refs_4_, ...), custom_call_target="tpu_custom_call" | custom-call | flops 8000000000 | bytes 24000000 | tf_op jit(solution)/shard_map/pallas_call | solution.py:239
  (57 shorter events, 33.3 us)
Async XLA Ops:
  0.6 41.4 %copy-start = (bf16[1728,256]{1,0:T(8,128)(2,1)S(1)}, bf16[1728,256]{1,0:T(8,128)(2,1)}, u32[]{:S(2)}) copy-start(bf16[1728,256]{1,0:T(8,128)(2,1)} %param.12) | copy-start | bytes 2654212
  1.6 7.2 %collective-permute-start = (bf16[1,2,8192]{2,1,0:T(2,128)(2,1)S(1)}, bf16[1,2,8192]{2,1,0:T(2,128)(2,1)S(1)}, u32[]{:S(2)}, u32[]{:S(2)}) collective-permute-start(bf16[1,2,8192]{2,1,0:T(2,128)(2,1)S(1)} %get-tuple-element.109), channel_id=1, source_target_pairs={{0,8},{8,16},{16,24},{24,32},{32,40},{40,48},{48,56},{56,64},{64,7... | collective-permute-start | bytes 98312 | tf_op jit(solution)/shard_map/ppermute | solution.py:92
  5.2 5.4 %collective-permute-start.1 = (bf16[1,2,8192]{2,1,0:T(2,128)(2,1)S(1)}, bf16[1,2,8192]{2,1,0:T(2,128)(2,1)S(1)}, u32[]{:S(2)}, u32[]{:S(2)}) collective-permute-start(bf16[1,2,8192]{2,1,0:T(2,128)(2,1)S(1)} %get-tuple-element.110), channel_id=1, source_target_pairs={{8,0},{16,8},{24,16},{32,24},{40,32},{48,40},{56,48},{64,56},{72,6... | collective-permute-start | bytes 98312 | tf_op jit(solution)/shard_map/ppermute | solution.py:94
  11.9 11.0 %collective-permute-start.2 = (bf16[4,1,8192]{2,1,0:T(2,128)(2,1)S(1)}, bf16[4,1,8192]{2,1,0:T(2,128)(2,1)S(1)}, u32[]{:S(2)}, u32[]{:S(2)}) collective-permute-start(bf16[4,1,8192]{2,1,0:T(2,128)(2,1)S(1)} %get-tuple-element.107), channel_id=1, source_target_pairs={{0,1},{1,2},{2,3},{3,4},{4,5},{5,6},{6,7},{8,9},{9,10},{10,11},{11... | collective-permute-start | bytes 196616 | tf_op jit(solution)/shard_map/ppermute | solution.py:92
  15.5 7.5 %collective-permute-start.3 = (bf16[4,1,8192]{2,1,0:T(2,128)(2,1)S(1)}, bf16[4,1,8192]{2,1,0:T(2,128)(2,1)S(1)}, u32[]{:S(2)}, u32[]{:S(2)}) collective-permute-start(bf16[4,1,8192]{2,1,0:T(2,128)(2,1)S(1)} %get-tuple-element.108), channel_id=1, source_target_pairs={{1,0},{2,1},{3,2},{4,3},{5,4},{6,5},{7,6},{9,8},{10,9},{11,10},{12... | collective-permute-start | bytes 196616 | tf_op jit(solution)/shard_map/ppermute | solution.py:94
  20.3 68.5 %collective-permute-start.4 = (bf16[2,2,128,3072]{3,2,1,0:T(8,128)(2,1)}, bf16[2,2,128,3072]{3,2,1,0:T(8,128)(2,1)}, u32[]{:S(2)}, u32[]{:S(2)}) collective-permute-start(bf16[2,2,128,3072]{3,2,1,0:T(8,128)(2,1)} %param.17), channel_id=1, source_target_pairs={{0,16},{8,24},{16,32},{24,40},{32,48},{40,56},{48,0},{56,8},{64,80... | collective-permute-start | bytes 9437192 | tf_op jit(solution)/shard_map/ppermute | solution.py:27
  21.3 68.3 %collective-permute-start.5 = (bf16[2,2,128,3072]{3,2,1,0:T(8,128)(2,1)}, bf16[2,2,128,3072]{3,2,1,0:T(8,128)(2,1)}, u32[]{:S(2)}, u32[]{:S(2)}) collective-permute-start(bf16[2,2,128,3072]{3,2,1,0:T(8,128)(2,1)} %param.17), channel_id=1, source_target_pairs={{0,48},{8,56},{16,0},{24,8},{32,16},{40,24},{48,32},{56,40},{64,11... | collective-permute-start | bytes 9437192 | tf_op jit(solution)/shard_map/ppermute | solution.py:28
  26.9 37.6 %collective-permute-start.6 = (bf16[2,2,128,3072]{3,2,1,0:T(8,128)(2,1)}, bf16[2,2,128,3072]{3,2,1,0:T(8,128)(2,1)}, u32[]{:S(2)}, u32[]{:S(2)}) collective-permute-start(bf16[2,2,128,3072]{3,2,1,0:T(8,128)(2,1)} %param.17), channel_id=1, source_target_pairs={{0,8},{16,24},{32,40},{48,56},{64,72},{80,88},{96,104},{112,120},{... | collective-permute-start | bytes 9437192 | tf_op jit(solution)/shard_map/ppermute | solution.py:35
  30.1 74.0 %collective-permute-start.9 = (bf16[2,2,128,3072]{3,2,1,0:T(8,128)(2,1)}, bf16[2,2,128,3072]{3,2,1,0:T(8,128)(2,1)}, u32[]{:S(2)}, u32[]{:S(2)}) collective-permute-start(bf16[2,2,128,3072]{3,2,1,0:T(8,128)(2,1)} %param.17), channel_id=1, source_target_pairs={{0,1},{1,2},{2,3},{3,4},{4,5},{5,6},{6,7},{8,9},{9,10},{10,11},{11... | collective-permute-start | bytes 9437192 | tf_op jit(solution)/shard_map/ppermute | solution.py:104
  32.5 73.4 %collective-permute-start.10 = (bf16[2,2,128,3072]{3,2,1,0:T(8,128)(2,1)}, bf16[2,2,128,3072]{3,2,1,0:T(8,128)(2,1)}, u32[]{:S(2)}, u32[]{:S(2)}) collective-permute-start(bf16[2,2,128,3072]{3,2,1,0:T(8,128)(2,1)} %param.17), channel_id=1, source_target_pairs={{1,0},{2,1},{3,2},{4,3},{5,4},{6,5},{7,6},{9,8},{10,9},{11,10},{12... | collective-permute-start | bytes 9437192 | tf_op jit(solution)/shard_map/ppermute | solution.py:104
  42.1 7.8 %copy-start.6 = (f32[1536]{0:T(1024)S(1)}, f32[1536]{0:T(1024)}, u32[]{:S(2)}) copy-start(f32[1536]{0:T(1024)} %param.14) | copy-start | bytes 18436
  47.3 2.8 %copy-start.5 = (f32[1536]{0:T(1024)S(1)}, f32[1536]{0:T(1024)}, u32[]{:S(2)}) copy-start(f32[1536]{0:T(1024)} %param.15) | copy-start | bytes 18436
  94.8 90.6 %slice-start = ((s8[4718592]{0:T(1024)(128)(4,1)}), s8[4194304]{0:T(1024)(128)(4,1)S(1)}, s32[]{:S(2)}) async-start(s8[4718592]{0:T(1024)(128)(4,1)} %bitcast.31), calls=%async_computation | async-start | bytes 8388608
  97.1 10.0 %collective-permute-start.11 = (bf16[2,2,128,3072]{3,2,1,0:T(8,128)(2,1)S(1)}, bf16[2,2,128,3072]{3,2,1,0:T(8,128)(2,1)S(1)}, u32[]{:S(2)}, u32[]{:S(2)}) collective-permute-start(bf16[2,2,128,3072]{3,2,1,0:T(8,128)(2,1)S(1)} %broadcast_select_fusion), channel_id=1, source_target_pairs={{0,8},{16,24},{32,40},{48,56},{64,72},{80,88},{96,104},{112,120},{... | collective-permute-start | bytes 9437192 | tf_op jit(solution)/shard_map/ppermute | solution.py:57
  100.0 41.3 %collective-permute-start.8 = (bf16[2,2,128,1536]{3,2,1,0:T(8,128)(2,1)}, bf16[2,2,128,1536]{3,2,1,0:T(8,128)(2,1)}, u32[]{:S(2)}, u32[]{:S(2)}) collective-permute-start(bf16[2,2,128,1536]{3,2,1,0:T(8,128)(2,1)} %get-tuple-element.49), channel_id=1, source_target_pairs={{0,64},{8,72},{16,80},{24,88},{96,32},{104,40},{112,48},{120,56},{... | collective-permute-start | bytes 4718600 | tf_op jit(solution)/shard_map/ppermute | solution.py:55
  101.2 48.0 %collective-permute-start.14 = (bf16[2,2,128,1536]{3,2,1,0:T(8,128)(2,1)}, bf16[2,2,128,1536]{3,2,1,0:T(8,128)(2,1)}, u32[]{:S(2)}, u32[]{:S(2)}) collective-permute-start(bf16[2,2,128,1536]{3,2,1,0:T(8,128)(2,1)} %get-tuple-element.59), channel_id=1, source_target_pairs={{0,16},{8,24},{16,32},{24,40},{32,48},{40,56},{48,0},{56,8},{64,80... | collective-permute-start | bytes 4718600 | tf_op jit(solution)/shard_map/ppermute | solution.py:53
  104.1 45.1 %collective-permute-start.15 = (bf16[2,2,128,1536]{3,2,1,0:T(8,128)(2,1)}, bf16[2,2,128,1536]{3,2,1,0:T(8,128)(2,1)}, u32[]{:S(2)}, u32[]{:S(2)}) collective-permute-start(bf16[2,2,128,1536]{3,2,1,0:T(8,128)(2,1)} %get-tuple-element.60), channel_id=1, source_target_pairs={{0,48},{8,56},{16,0},{24,8},{32,16},{40,24},{48,32},{56,40},{64,11... | collective-permute-start | bytes 4718600 | tf_op jit(solution)/shard_map/ppermute | solution.py:54
  105.9 69.2 %collective-permute-start.7 = (bf16[2,2,128,1536]{3,2,1,0:T(8,128)(2,1)S(1)}, bf16[2,2,128,1536]{3,2,1,0:T(8,128)(2,1)}, u32[]{:S(2)}, u32[]{:S(2)}) collective-permute-start(bf16[2,2,128,1536]{3,2,1,0:T(8,128)(2,1)S(1)} %get-tuple-element.48), channel_id=1, source_target_pairs={{0,64},{8,72},{16,80},{24,88},{96,32},{104,40},{112,48},{120,56},{... | collective-permute-start | bytes 4718600 | tf_op jit(solution)/shard_map/ppermute | solution.py:56
  108.8 76.5 %slice-start.1 = ((s8[4718592]{0:T(1024)(128)(4,1)}), s8[524288]{0:T(1024)(128)(4,1)S(1)}, s32[]{:S(2)}) async-start(s8[4718592]{0:T(1024)(128)(4,1)} %bitcast.31), calls=%async_computation.1 | async-start | bytes 1048576
  141.3 35.1 %collective-permute-start.12 = (bf16[2,2,128,1536]{3,2,1,0:T(8,128)(2,1)}, bf16[2,2,128,1536]{3,2,1,0:T(8,128)(2,1)}, u32[]{:S(2)}, u32[]{:S(2)}) collective-permute-start(bf16[2,2,128,1536]{3,2,1,0:T(8,128)(2,1)} %collective-permute-done.8), channel_id=1, source_target_pairs={{64,80},{72,88},{80,64},{88,72},{32,48},{40,56},{48,32},{56,40},{6... | collective-permute-start | bytes 4718600 | tf_op jit(solution)/shard_map/ppermute | solution.py:63
  143.2 33.2 %collective-permute-start.13 = (bf16[2,2,128,1536]{3,2,1,0:T(8,128)(2,1)}, bf16[2,2,128,1536]{3,2,1,0:T(8,128)(2,1)}, u32[]{:S(2)}, u32[]{:S(2)}) collective-permute-start(bf16[2,2,128,1536]{3,2,1,0:T(8,128)(2,1)} %collective-permute-done.8), channel_id=1, source_target_pairs={{72,64},{48,56},{73,65},{49,57},{74,66},{50,58},{75,67},{51,59},{7... | collective-permute-start | bytes 4718600 | tf_op jit(solution)/shard_map/ppermute | solution.py:63
  176.4 11.0 %collective-permute-start.17 = (bf16[2,2,128,1536]{3,2,1,0:T(8,128)(2,1)}, bf16[2,2,128,1536]{3,2,1,0:T(8,128)(2,1)}, u32[]{:S(2)}, u32[]{:S(2)}) collective-permute-start(bf16[2,2,128,1536]{3,2,1,0:T(8,128)(2,1)} %collective-permute-done.7), channel_id=1, source_target_pairs={{72,64},{48,56},{73,65},{49,57},{74,66},{50,58},{75,67},{51,59},{7... | collective-permute-start | bytes 4718600 | tf_op jit(solution)/shard_map/ppermute | solution.py:63
  183.4 36.9 %collective-permute-start.16 = (bf16[2,2,128,1536]{3,2,1,0:T(8,128)(2,1)}, bf16[2,2,128,1536]{3,2,1,0:T(8,128)(2,1)S(1)}, u32[]{:S(2)}, u32[]{:S(2)}) collective-permute-start(bf16[2,2,128,1536]{3,2,1,0:T(8,128)(2,1)} %collective-permute-done.7), channel_id=1, source_target_pairs={{64,80},{72,88},{80,64},{88,72},{32,48},{40,56},{48,32},{56,40},{6... | collective-permute-start | bytes 4718600 | tf_op jit(solution)/shard_map/ppermute | solution.py:63
  221.5 8.2 %copy-start.1 = (bf16[1728,256]{1,0:T(8,128)(2,1)S(1)}, bf16[1728,256]{1,0:T(8,128)(2,1)}, u32[]{:S(2)}) copy-start(bf16[1728,256]{1,0:T(8,128)(2,1)} %param.12) | copy-start | bytes 2654212
  (3 other events, 5.7 us)
